TPU v7x, 32 devices: a whole 2x2x4 slice. The times are simulated.
32 devices in a mesh: ctx: 4 (over z), fsdp: 8 (over y, x, core).
Axes of the slice: x: 2, y: 2, z: 4, core: 2. Of those that a mesh axis runs over, the one named last changes fastest.
Arguments:
- tokens: bfloat16 [8, 1024, 2048], P('fsdp', 'ctx'), may hold values from -6 to 6
- block_order: int32 [8, 4], P('fsdp'), may hold values from 0 to 3, each once within a row
- ln_gain: bfloat16 [2048], P('fsdp'), may hold values from 0.5 to 1.5
- ln_bias: bfloat16 [2048], P('fsdp'), may hold values from -2 to 2
- w_qkv: bfloat16 [2048, 6144], P('fsdp'), may hold values from -0.125 to 0.125
- w_out: bfloat16 [2048, 2048], P('fsdp'), may hold values from -2 to 2
- w_gate: bfloat16 [2048, 5632], P('fsdp'), may hold values from -0.125 to 0.125
- w_up: bfloat16 [2048, 5632], P('fsdp'), may hold values from -0.125 to 0.125
- w_down: bfloat16 [5632, 2048], P('fsdp'), may hold values from -0.109375 to 0.109375
- cotangent: bfloat16 [8, 1024, 2048], P('fsdp', 'ctx'), may hold values from -6 to 6
Outputs:
- out: bfloat16 [8, 1024, 2048], P('fsdp', 'ctx')
- grad_in: float32 [8, 1024, 2048], P('fsdp', 'ctx')
- d_gain: float32 [2048], P('fsdp')
- d_bias: float32 [2048], P('fsdp')
- d_qkv: float32 [2048, 6144], P('fsdp')
- d_out: float32 [2048, 2048], P('fsdp')
- d_gate: float32 [2048, 5632], P('fsdp')
- d_up: float32 [2048, 5632], P('fsdp')
- d_down: float32 [5632, 2048], P('fsdp')
Inputs may be any that keep to these rules, and one draw needn't show every extreme that they name: Each row of block_order holds every block number from 0 to 3 once.
All inputs are finite; a program needn't handle non-finite values.
Results may differ from a plain program's by a relative error of at most 0.018.
Values may be sent and summed in bfloat16 or wider, within the bound.
A program may use at most 512 MiB of HBM per device.

v0:
```python
import functools

import jax
import jax.numpy as jnp
from jax import lax
from jax.experimental import pallas as pl
from jax.experimental.pallas import tpu as pltpu
from jax.sharding import PartitionSpec as P

H = 32
HD = 64
ROT = 16
EPS = 1e-05
NEG = -1e30
CHUNK = 256

BF = jnp.bfloat16
F32 = jnp.float32


def xor_send(value, mask):
    count = lax.axis_size("fsdp")
    return lax.ppermute(value, "fsdp", [(i, i ^ mask) for i in range(count)])


def ring_send(value, steps):
    count = lax.axis_size("ctx")
    return lax.ppermute(value, "ctx", [(i, (i + steps) % count) for i in range(count)])


def after(value, *done):
    return lax.optimization_barrier((value,) + done)[0]


def dot(a, b, dims, out=F32):
    return lax.dot_general(a, b, (dims, ((), ())), preferred_element_type=F32).astype(out)


def gather_rows(piece):
    count = lax.axis_size("fsdp")
    chips = count // 2
    me = lax.axis_index("fsdp")
    chip, core = me // 2, me % 2
    parts = [piece] + [xor_send(piece, 2 * m) for m in range(1, chips)]
    others = [xor_send(p, 1) for p in parts]
    whole = jnp.zeros((count,) + piece.shape, piece.dtype)
    for m in range(chips):
        at = 2 * (chip ^ m)
        whole = lax.dynamic_update_index_in_dim(whole, parts[m], at + core, 0)
        whole = lax.dynamic_update_index_in_dim(whole, others[m], at + 1 - core, 0)
    return whole.reshape(count * piece.shape[0], piece.shape[1]), parts[-1]


def scatter_rows(grad):
    count = lax.axis_size("fsdp")
    chips = count // 2
    me = lax.axis_index("fsdp")
    chip, core = me // 2, me % 2
    rows = grad.shape[0] // count
    split = grad.reshape(chips, 2, rows, grad.shape[1])
    theirs = xor_send(lax.dynamic_index_in_dim(split, 1 - core, 1, False), 1)
    pair = lax.dynamic_index_in_dim(split, core, 1, False).astype(F32) + theirs.astype(F32)
    pair = pair.astype(BF)
    total = lax.dynamic_index_in_dim(pair, chip, 0, False).astype(F32)
    for m in range(1, chips):
        part = lax.dynamic_index_in_dim(pair, chip ^ m, 0, False)
        total = total + xor_send(part, 2 * m).astype(F32)
    return total.astype(BF)


def gather_ctx(piece):
    count = lax.axis_size("ctx")
    me = lax.axis_index("ctx")
    whole = jnp.zeros((count,) + piece.shape, piece.dtype)
    whole = lax.dynamic_update_index_in_dim(whole, piece, me, 0)
    for k in range(1, count):
        part = ring_send(piece, k)
        whole = lax.dynamic_update_index_in_dim(whole, part, (me - k) % count, 0)
    return whole


def line_scatter(blocks):
    count = lax.axis_size("ctx")
    me = lax.axis_index("ctx")
    down = up = None
    for t in range(1, count):
        to_down = blocks(jnp.clip(t + me - count, 0, count - 1))
        to_up = blocks(jnp.clip(count - 1 - (t + (count - 1 - me) - count), 0, count - 1))
        if down is not None:
            to_down = to_down + down.astype(F32)
            to_up = to_up + up.astype(F32)
        pairs = [(i, i - 1) for i in range(count - t, count)]
        down = lax.ppermute(to_down.astype(BF), "ctx", pairs)
        up = lax.ppermute(to_up.astype(BF), "ctx", [(count - 1 - i, count - 1 - j) for i, j in pairs])
    return blocks(me) + down.astype(F32) + up.astype(F32)


def turn(x, cos, first, second):
    width = x.shape[1]
    half = ROT // 2
    return x * cos + pltpu.roll(x, width - half, 1) * first + pltpu.roll(x, half, 1) * second


def contract(a, b, dims):
    return lax.dot_general(a, b, (dims, ((), ())), preferred_element_type=F32)


def attend_kernel(mq, mk, mv, cos, first, second, q_out, k_out, v_out, att_out, lse_out):
    length = mq.shape[0]
    scale = HD ** (-0.5)
    q_out[...] = (turn(mq[...], cos[...], first[...], second[...]).astype(BF).astype(F32) * scale).astype(BF)
    k_out[...] = turn(mk[...], cos[...], first[...], second[...]).astype(BF)
    v_out[...] = mv[...].astype(BF)
    row = lax.broadcasted_iota(jnp.int32, (CHUNK, CHUNK), 0)
    col = lax.broadcasted_iota(jnp.int32, (CHUNK, CHUNK), 1)
    for c in range(length // CHUNK):
        lo, hi = c * CHUNK, (c + 1) * CHUNK
        for h in range(2):
            lanes = slice(h * HD, (h + 1) * HD)
            q = q_out[lo:hi, lanes]
            s = contract(q, k_out[lo:hi, lanes], ((1,), (1,)))
            s = jnp.where(col <= row, s, NEG)
            if c:
                s = jnp.concatenate([contract(q, k_out[:lo, lanes], ((1,), (1,))), s], axis=1)
            top = jnp.max(s, axis=1, keepdims=True)
            p = jnp.exp(s - top)
            total = jnp.sum(p, axis=1, keepdims=True)
            o = contract(p.astype(BF), v_out[:hi, lanes], ((1,), (0,)))
            att_out[lo:hi, lanes] = o / total
            lse_out[lo:hi, lanes] = jnp.broadcast_to(top + jnp.log(total), (CHUNK, HD))


def attend(mixed, tables, heads):
    length = mixed.shape[0]
    pairs = heads // 2
    block = lambda at: pl.BlockSpec((length, 2 * HD), lambda h, at=at: (0, at + h))
    table = pl.BlockSpec((length, 2 * HD), lambda h: (0, 0))
    width = heads * HD
    return pl.pallas_call(
        attend_kernel,
        grid=(pairs,),
        in_specs=[block(0), block(pairs), block(2 * pairs), table, table, table],
        out_specs=[block(0)] * 5,
        out_shape=[jax.ShapeDtypeStruct((length, width), BF)] * 3
        + [jax.ShapeDtypeStruct((length, width), F32)] * 2,
        compiler_params=pltpu.CompilerParams(vmem_limit_bytes=40 * 2**20),
        cost_estimate=pl.CostEstimate(
            flops=16 * heads * length * length * HD // 2,
            bytes_accessed=26 * length * width,
            transcendentals=heads * length * length // 2,
        ),
        name="attend",
    )(mixed, mixed, mixed, *tables)


def attend_back_kernel(q_in, k_in, v_in, do_in, att, lse, cos, first, second, dq_out, dk_out, dv_out, dk, dv):
    length = q_in.shape[0]
    scale = HD ** (-0.5)
    row = lax.broadcasted_iota(jnp.int32, (CHUNK, CHUNK), 0)
    col = lax.broadcasted_iota(jnp.int32, (CHUNK, CHUNK), 1)
    dk[...] = jnp.zeros_like(dk)
    dv[...] = jnp.zeros_like(dv)
    for c in range(length // CHUNK):
        lo, hi = c * CHUNK, (c + 1) * CHUNK
        dqs = []
        for h in range(2):
            lanes = slice(h * HD, (h + 1) * HD)
            q, do = q_in[lo:hi, lanes], do_in[lo:hi, lanes]
            delta = jnp.sum(do.astype(F32) * att[lo:hi, lanes], axis=1, keepdims=True)
            s = contract(q, k_in[lo:hi, lanes], ((1,), (1,)))
            s = jnp.where(col <= row, s, NEG)
            if c:
                s = jnp.concatenate([contract(q, k_in[:lo, lanes], ((1,), (1,))), s], axis=1)
            p = jnp.exp(s - lse[lo:hi, h * HD : h * HD + 1])
            dp = contract(do, v_in[:hi, lanes], ((1,), (1,)))
            ds = (p * (dp - delta)).astype(BF)
            dqs.append(contract(ds, k_in[:hi, lanes], ((1,), (0,))) * scale)
            dk[:hi, lanes] += contract(ds, q, ((0,), (0,)))
            dv[:hi, lanes] += contract(p.astype(BF), do, ((0,), (0,)))
        dq = jnp.concatenate(dqs, axis=1)
        dq_out[lo:hi, :] = turn(dq, cos[lo:hi, :], -first[lo:hi, :], -second[lo:hi, :]).astype(BF)
    dk_out[...] = turn(dk[...], cos[...], -first[...], -second[...]).astype(BF)
    dv_out[...] = dv[...].astype(BF)


def attend_back(q, k, v, d_attended, attended, lse, tables, heads):
    length, width = q.shape
    block = pl.BlockSpec((length, 2 * HD), lambda h: (0, h))
    table = pl.BlockSpec((length, 2 * HD), lambda h: (0, 0))
    return pl.pallas_call(
        attend_back_kernel,
        grid=(heads // 2,),
        in_specs=[block] * 6 + [table] * 3,
        out_specs=[block] * 3,
        out_shape=[jax.ShapeDtypeStruct((length, width), BF)] * 3,
        scratch_shapes=[pltpu.VMEM((length, 2 * HD), F32)] * 2,
        compiler_params=pltpu.CompilerParams(vmem_limit_bytes=40 * 2**20),
        cost_estimate=pl.CostEstimate(
            flops=40 * heads * length * length * HD // 2,
            bytes_accessed=22 * length * width,
            transcendentals=heads * length * length // 2,
        ),
        name="attend_back",
    )(q, k, v, d_attended, attended, lse, *tables)


MESH = pl.DeviceIdType.MESH
TILE = 256
HALF = 128
DEEP = 4
LAG = 2


def vmem_whole():
    return pl.BlockSpec(memory_space=pltpu.VMEM)


def hbm_whole():
    return pl.BlockSpec(memory_space=pl.ANY)


def chip_away(chip, m):
    return 2 * ((chip // 2 + m // 2) % 2) + (chip + m) % 2


def inner_runs(shards, count, part):
    runs = []
    for block in range(shards * part // HALF):
        first = 0
        while first < HALF:
            shard, unit = divmod(block * HALF + first, part)
            last = min(HALF, first + part - unit)
            runs.append((block, first, last, shard * count * part + unit - first))
            first = last
    return runs


class Line:
    def __init__(self, own, whole, send, recv):
        self.own, self.whole, self.send, self.recv = own, whole, send, recv
        self.count = whole.shape[0]
        self.place, self.me = lax.axis_index("ctx"), lax.axis_index("fsdp")

    def copy(self, way, hop):
        ahead = 1 - 2 * way
        origin = self.place - (hop - 1) * ahead
        return pltpu.make_async_remote_copy(
            src_ref=self.own if hop == 1 else self.whole.at[origin],
            dst_ref=self.whole.at[origin],
            send_sem=self.send.at[way, hop - 1],
            recv_sem=self.recv.at[way, hop - 1],
            device_id=(self.place + ahead, self.me),
            device_id_type=MESH,
        )

    def sends(self, way, hop):
        if way == 0:
            return (self.place >= hop - 1) & (self.place <= self.count - 2)
        return (self.place <= self.count - hop) & (self.place >= 1)

    def lands(self, way, hop):
        return self.place >= hop if way == 0 else self.place <= self.count - 1 - hop

    def pass_on(self, hop):
        for way in range(2):
            if hop > 1:
                @pl.when(self.lands(way, hop - 1))
                def _(way=way):
                    self.copy(way, hop - 1).wait_recv()

            if hop < self.count:
                @pl.when(self.sends(way, hop))
                def _(way=way):
                    self.copy(way, hop).start()

    def finish(self):
        for way in range(2):
            for hop in range(1, self.count):
                @pl.when(self.sends(way, hop))
                def _(way=way, hop=hop):
                    self.copy(way, hop).wait_send()


class Plane:
    def __init__(self, mine, wholes, send, recv):
        self.mine, self.wholes, self.send, self.recv = mine, wholes, send, recv
        self.place, self.me = lax.axis_index("ctx"), lax.axis_index("fsdp")
        chip, core = self.me // 2, self.me % 2
        self.sibling = 2 * chip + 1 - core
        self.near = (2 * chip_away(chip, 1) + core, 2 * chip_away(chip, 2) + core)
        self.far = 2 * chip_away(chip, 3) + core

    def copy(self, which, kind, source, target, to):
        return pltpu.make_async_remote_copy(
            src_ref=source,
            dst_ref=target,
            send_sem=self.send.at[which, kind],
            recv_sem=self.recv.at[which, kind],
            device_id=(self.place, to),
            device_id_type=MESH,
        )

    def direct(self, which, a):
        return self.copy(which, a, self.mine[which], self.wholes[which].at[self.me], self.near[a])

    def across(self, which, a):
        half = self.wholes[which].shape[2] // 2
        piece = self.wholes[which].at[self.near[1 - a], :, a * half : (a + 1) * half]
        return self.copy(which, 2 + a, piece, piece, self.near[a])

    def beside(self, which, kind):
        source = (self.me, self.near[0], self.near[1], self.far)[kind]
        piece = self.wholes[which].at[source]
        return self.copy(which, 4 + kind, self.mine[which] if kind == 0 else piece, piece, self.sibling)

    def begin(self, which):
        for a in range(2):
            self.direct(which, a).start()
        self.beside(which, 0).start()

    def relay(self, which):
        for a in range(2):
            self.direct(which, a).wait_recv()
        for a in range(2):
            self.across(which, a).start()
            self.beside(which, 1 + a).start()

    def last(self, which):
        for a in range(2):
            self.across(which, a).wait_recv()
        self.beside(which, 3).start()

    def finish(self, which):
        for kind in range(4):
            self.beside(which, kind).wait()
        for a in range(2):
            self.direct(which, a).wait_send()
            self.across(which, a).wait_send()


def greet(peers):
    barrier = pltpu.get_barrier_semaphore()
    for peer in peers:
        pl.semaphore_signal(barrier, inc=1, device_id=peer, device_id_type=MESH)
    pl.semaphore_wait(barrier, len(peers))


def start_kernel(
    tokens, vectors, w_gate, w_up, w_qkv, x_all, vectors_all, inner, heads,
    raw_gate, raw_up, raw_qkv, my_inner, my_heads,
    load_sem, line_send, line_recv, part_send, part_recv, vector_send, vector_recv, own_sem,
):
    count, shards = x_all.shape[0], inner.shape[0]
    place, me = lax.axis_index("ctx"), lax.axis_index("fsdp")
    loads = [
        pltpu.make_async_copy(w_gate, raw_gate, load_sem.at[0]),
        pltpu.make_async_copy(w_up, raw_up, load_sem.at[1]),
        pltpu.make_async_copy(w_qkv, raw_qkv, load_sem.at[2]),
    ]
    for load in loads:
        load.start()
    peers = [(place, (me + s) % shards) for s in range(1, shards)]
    greet(peers + [((place + 1) % count, me), ((place + count - 1) % count, me)])
    line = Line(tokens, x_all, line_send, line_recv)
    plane = Plane((my_inner, my_heads), (inner, heads), part_send, part_recv)
    line.pass_on(1)
    own_copies = [
        pltpu.make_async_copy(my_inner, inner.at[me], own_sem.at[0]),
        pltpu.make_async_copy(my_heads, heads.at[me], own_sem.at[1]),
        pltpu.make_async_copy(vectors, vectors_all.at[me], own_sem.at[2]),
        pltpu.make_async_copy(tokens, x_all.at[place], own_sem.at[3]),
    ]
    own_copies[2].start()
    own_copies[3].start()
    vector_copies = [
        pltpu.make_async_remote_copy(
            src_ref=vectors,
            dst_ref=vectors_all.at[me],
            send_sem=vector_send.at[s - 1],
            recv_sem=vector_recv.at[s - 1],
            device_id=(place, (me + s) % shards),
            device_id_type=MESH,
        )
        for s in range(1, shards)
    ]
    for c in vector_copies:
        c.start()

    row = lax.broadcasted_iota(jnp.int32, (TILE, HALF), 0)
    col = lax.broadcasted_iota(jnp.int32, (TILE, HALF), 1)

    def picked(raws, first, last, start):
        width = raws[0].shape[1]
        base = jnp.minimum((start + first) // HALF, width // HALF - TILE // HALF) * HALF
        choose = (row + base == col + start) & (col >= first) & (col < last)
        choose = choose.astype(F32).astype(BF)
        at = pl.ds(pl.multiple_of(base, HALF), TILE)
        return [contract(raw[:, at], choose, ((1,), (0,))) for raw in raws]

    part = raw_gate.shape[1] // shards // count
    loads[0].wait()
    loads[1].wait()
    held = None
    for block, first, last, start in inner_runs(shards, count, part):
        values = picked((raw_gate, raw_up), first, last, start + place * part)
        held = values if first == 0 else [a + b for a, b in zip(held, values)]
        if last == HALF:
            for k in range(2):
                at = block * TILE + k * HALF
                my_inner[:, at : at + HALF] = held[k].astype(BF)
    plane.begin(0)
    own_copies[0].start()
    loads[2].wait()
    width = raw_qkv.shape[1] // 3
    for pair in range(shards // 2):
        for kind in range(3):
            value = 0.0
            for h in range(2):
                head = count * (2 * pair + h) + place
                start = kind * width + head * HD - h * HD
                value = value + picked((raw_qkv,), h * HD, (h + 1) * HD, start)[0]
            at = (pair * 3 + kind) * HALF
            my_heads[:, at : at + HALF] = value.astype(BF)
    plane.begin(1)
    own_copies[1].start()
    line.pass_on(2)
    plane.relay(0)
    line.pass_on(3)
    plane.relay(1)
    for hop in range(4, count + 1):
        line.pass_on(hop)
    for which in range(2):
        plane.last(which)
    for which in range(2):
        plane.finish(which)
    for c in vector_copies + own_copies:
        c.wait()
    line.finish()


def start(tokens, vectors, w_gate, w_up, w_qkv, count, shards):
    rows, width = tokens.shape
    shard_rows, ff = w_gate.shape
    inner, heads = 2 * ff // count, 3 * width // count
    dma = pltpu.SemaphoreType.DMA
    return pl.pallas_call(
        start_kernel,
        out_shape=[
            jax.ShapeDtypeStruct((count, rows, width), BF),
            jax.ShapeDtypeStruct((shards,) + vectors.shape, F32),
            jax.ShapeDtypeStruct((shards, shard_rows, inner), BF),
            jax.ShapeDtypeStruct((shards, shard_rows, heads), BF),
        ],
        in_specs=[hbm_whole()] * 5,
        out_specs=[hbm_whole()] * 4,
        scratch_shapes=[
            pltpu.VMEM(w_gate.shape, BF),
            pltpu.VMEM(w_up.shape, BF),
            pltpu.VMEM(w_qkv.shape, BF),
            pltpu.VMEM((shard_rows, inner), BF),
            pltpu.VMEM((shard_rows, heads), BF),
            dma((3,)),
            dma((2, count - 1)),
            dma((2, count - 1)),
            dma((2, 8)),
            dma((2, 8)),
            dma((shards - 1,)),
            dma((shards - 1,)),
            dma((4,)),
        ],
        compiler_params=pltpu.CompilerParams(
            collective_id=2, has_side_effects=True, vmem_limit_bytes=30 * 2**20
        ),
        name="start",
    )(tokens, vectors, w_gate, w_up, w_qkv)


def forward_kernel(
    order, slots, x_all, gain, bias, cos, first, second, cot, w_down, w_out, w_inner, w_heads,
    cot_all, down, attn, normed_t, hat, both, hidden_t, q_out, k_out, v_out, att_out, low_t, lse_out, branch,
    inner, heads, normed, hidden, low, hat_stage, turned_stage, both_stage, hidden_stage,
    q_buf, k_buf, v_buf, att_buf, low_stage, lse_buf, down_tile, attn_tile, term, branch_stage,
    load_sem, line_send, line_recv, part_send, part_recv, own_sem, norm_sem, feed_sem, head_sem, tile_sem, branch_sem,
):
    count, rows = cot_all.shape[0], cot_all.shape[1]
    shards = down.shape[0]
    place, me = lax.axis_index("ctx"), lax.axis_index("fsdp")
    chip, core = me // 2, me % 2
    loads = [
        pltpu.make_async_copy(w_inner, inner, load_sem.at[0]),
        pltpu.make_async_copy(w_heads, heads, load_sem.at[1]),
    ]
    for load in loads:
        load.start()
    peers = [(place, 2 * chip + 1 - core)] + [(place, 2 * chip_away(chip, m) + core) for m in range(1, 3)]
    greet(peers + [((place + 1) % count, me), ((place + count - 1) % count, me)])
    my_down = w_down.at[pl.ds(pl.multiple_of(place * down.shape[1], 16), down.shape[1])]
    my_attn = w_out.at[pl.ds(pl.multiple_of(place * attn.shape[1], 16), attn.shape[1])]
    line = Line(cot, cot_all, line_send, line_recv)
    plane = Plane((my_down, my_attn), (down, attn), part_send, part_recv)
    line.pass_on(1)
    for which in range(2):
        plane.begin(which)
    own_copies = [
        pltpu.make_async_copy(my_down, down.at[me], own_sem.at[0]),
        pltpu.make_async_copy(my_attn, attn.at[me], own_sem.at[1]),
        pltpu.make_async_copy(cot, cot_all.at[place], own_sem.at[2]),
    ]
    for c in own_copies:
        c.start()

    def norm_copies(p):
        at = pl.ds(pl.multiple_of(p * rows, rows), rows)
        return (
            pltpu.make_async_copy(hat_stage.at[p % 2], hat.at[at], norm_sem.at[0, p % 2]),
            pltpu.make_async_copy(turned_stage.at[p % 2], normed_t.at[:, at], norm_sem.at[1, p % 2]),
        )

    def norm_step(p, carry):
        @pl.when(p >= 2)
        def _():
            for c in norm_copies(p - 2):
                c.wait()

        xf = x_all[slots[p]].astype(F32)
        mean = jnp.mean(xf, axis=1, keepdims=True)
        centered = xf - mean
        variance = jnp.mean(centered * centered, axis=1, keepdims=True)
        x_hat = centered * lax.rsqrt(variance + EPS)
        hat_stage[p % 2] = x_hat.astype(BF)
        value = x_hat * gain[...] + bias[...]
        normed[pl.ds(pl.multiple_of(p * rows, rows), rows), :] = value.astype(BF)
        turned_stage[p % 2] = value.T.astype(BF)
        for c in norm_copies(p):
            c.start()
        return carry

    lax.fori_loop(0, count, norm_step, 0)
    loads[0].wait()

    def feed_copies(i):
        wide = pl.ds(pl.multiple_of(i * TILE, TILE), TILE)
        slim = pl.ds(pl.multiple_of(i * HALF, HALF), HALF)
        return (
            pltpu.make_async_copy(both_stage.at[i % 2], both.at[:, wide], feed_sem.at[0, i % 2]),
            pltpu.make_async_copy(hidden_stage.at[i % 2], hidden_t.at[slim], feed_sem.at[1, i % 2]),
        )

    def feed_step(i, carry):
        @pl.when(i >= 2)
        def _():
            for c in feed_copies(i - 2):
                c.wait()

        value = contract(normed[...], inner[:, pl.ds(pl.multiple_of(i * TILE, TILE), TILE)], ((1,), (0,)))
        both_stage[i % 2] = value.astype(BF)
        gate, up = value[:, :HALF], value[:, HALF:]
        value = gate * jax.nn.sigmoid(gate) * up
        hidden[:, pl.ds(pl.multiple_of(i * HALF, HALF), HALF)] = value.astype(BF)
        hidden_stage[i % 2] = value.T.astype(BF)
        for c in feed_copies(i):
            c.start()
        return carry

    tiles = inner.shape[1] // TILE
    lax.fori_loop(0, tiles, feed_step, 0)
    line.pass_on(2)
    for which in range(2):
        plane.relay(which)
    loads[1].wait()
    row = lax.broadcasted_iota(jnp.int32, (CHUNK, CHUNK), 0)
    col = lax.broadcasted_iota(jnp.int32, (CHUNK, CHUNK), 1)
    pairs = heads.shape[1] // (3 * HALF)

    def head_copies(h):
        at = pl.ds(pl.multiple_of(h * HALF, HALF), HALF)
        moves = ((q_buf, q_out), (k_buf, k_out), (v_buf, v_out), (att_buf, att_out), (lse_buf, lse_out))
        copies = [
            pltpu.make_async_copy(a.at[h % 2], b.at[:, at], head_sem.at[n, h % 2]) for n, (a, b) in enumerate(moves)
        ]
        return copies + [pltpu.make_async_copy(low_stage.at[h % 2], low_t.at[at], head_sem.at[5, h % 2])]

    def head_step(h, carry):
        @pl.when(h >= 2)
        def _():
            for c in head_copies(h - 2):
                c.wait()

        slot = h % 2
        mixed = contract(
            normed[...], heads[:, pl.ds(pl.multiple_of(h * 3 * HALF, HALF), 3 * HALF)], ((1,), (0,))
        )
        q = turn(mixed[:, :HALF], cos[...], first[...], second[...]).astype(BF).astype(F32)
        q_buf[slot] = (q * HD ** (-0.5)).astype(BF)
        k_buf[slot] = turn(mixed[:, HALF : 2 * HALF], cos[...], first[...], second[...]).astype(BF)
        v_buf[slot] = mixed[:, 2 * HALF :].astype(BF)
        for c in range(normed.shape[0] // CHUNK):
            lo, hi = c * CHUNK, (c + 1) * CHUNK
            for side in range(2):
                lanes = slice(side * HD, (side + 1) * HD)
                q = q_buf[slot, lo:hi, lanes]
                s = contract(q, k_buf[slot, lo:hi, lanes], ((1,), (1,)))
                s = jnp.where(col <= row, s, NEG)
                if c:
                    s = jnp.concatenate([contract(q, k_buf[slot, :lo, lanes], ((1,), (1,))), s], axis=1)
                top = jnp.max(s, axis=1, keepdims=True)
                p = jnp.exp(s - top)
                total = jnp.sum(p, axis=1, keepdims=True)
                o = contract(p.astype(BF), v_buf[slot, :hi, lanes], ((1,), (0,)))
                att_buf[slot, lo:hi, lanes] = o / total
                lse_buf[slot, lo:hi, lanes] = jnp.broadcast_to(top + jnp.log(total), (CHUNK, HD))
        att = att_buf[slot]
        low[:, pl.ds(pl.multiple_of(h * HALF, HALF), HALF)] = att.astype(BF)
        low_stage[slot] = att.T.astype(BF)
        for c in head_copies(h):
            c.start()
        return carry

    lax.fori_loop(0, pairs // 2, head_step, 0)
    for which in range(2):
        plane.last(which)
    line.pass_on(3)
    lax.fori_loop(pairs // 2, pairs, head_step, 0)
    for which in range(2):
        plane.finish(which)
    for c in own_copies:
        c.wait()

    def tile_copies(i):
        at = pl.ds(pl.multiple_of(i * TILE, TILE), TILE)
        return (
            pltpu.make_async_copy(down.at[:, :, at], down_tile.at[i % 2], tile_sem.at[0, i % 2]),
            pltpu.make_async_copy(attn.at[:, :, at], attn_tile.at[i % 2], tile_sem.at[1, i % 2]),
        )

    def branch_copy(i):
        at = pl.ds(pl.multiple_of(i * TILE, TILE), TILE)
        return pltpu.make_async_copy(branch_stage.at[i % 2], branch.at[:, :, at], branch_sem.at[i % 2])

    steps = branch.shape[2] // TILE
    for c in tile_copies(0):
        c.start()

    def branch_step(i, carry):
        @pl.when(i + 1 < steps)
        def _():
            for c in tile_copies(i + 1):
                c.start()

        for c in tile_copies(i):
            c.wait()

        @pl.when(i >= 2)
        def _():
            branch_copy(i - 2).wait()

        value = contract(hidden[...], down_tile[i % 2].reshape(hidden.shape[1], TILE), ((1,), (0,)))
        value = value + contract(low[...], attn_tile[i % 2].reshape(low.shape[1], TILE), ((1,), (0,)))
        term[...] = value.reshape(term.shape)
        for j in range(count):
            branch_stage[i % 2, j] = term[order[j]].astype(BF)
        branch_copy(i).start()
        return carry

    lax.fori_loop(0, steps, branch_step, 0)
    for hop in range(4, count + 1):
        line.pass_on(hop)
    line.finish()
    for back in range(2):
        for c in norm_copies(count - 1 - back) + feed_copies(tiles - 1 - back):
            c.wait()
        for c in head_copies(pairs - 1 - back):
            c.wait()
        branch_copy(steps - 1 - back).wait()


def forward(order, slots, x_all, gain, bias, tables, cot, w_down, w_out, w_inner, w_heads, shards):
    count, rows, width = x_all.shape
    length = count * rows
    ff_part, attn_part = w_down.shape[0] // count, w_out.shape[0] // count
    ff, cols = shards * ff_part, shards * attn_part
    dma = pltpu.SemaphoreType.DMA
    smem = pl.BlockSpec(memory_space=pltpu.SMEM)
    bf = lambda *shape: jax.ShapeDtypeStruct(shape, BF)
    f32 = lambda *shape: jax.ShapeDtypeStruct(shape, F32)
    out_shape = [
        bf(count, rows, width),
        bf(shards, ff_part, width),
        bf(shards, attn_part, width),
        bf(width, length),
        bf(length, width),
        bf(length, 2 * ff),
        bf(ff, length),
        bf(length, cols),
        bf(length, cols),
        bf(length, cols),
        f32(length, cols),
        bf(cols, length),
        f32(length, cols),
        bf(count, rows, width),
    ]
    return pl.pallas_call(
        forward_kernel,
        out_shape=out_shape,
        in_specs=[smem] * 2 + [vmem_whole()] * 6 + [hbm_whole()] * 5,
        out_specs=[hbm_whole()] * len(out_shape),
        scratch_shapes=[
            pltpu.VMEM(w_inner.shape, BF),
            pltpu.VMEM(w_heads.shape, BF),
            pltpu.VMEM((length, width), BF),
            pltpu.VMEM((length, ff), BF),
            pltpu.VMEM((length, cols), BF),
            pltpu.VMEM((2, rows, width), BF),
            pltpu.VMEM((2, width, rows), BF),
            pltpu.VMEM((2, length, TILE), BF),
            pltpu.VMEM((2, HALF, length), BF),
            pltpu.VMEM((2, length, HALF), BF),
            pltpu.VMEM((2, length, HALF), BF),
            pltpu.VMEM((2, length, HALF), BF),
            pltpu.VMEM((2, length, HALF), F32),
            pltpu.VMEM((2, HALF, length), BF),
            pltpu.VMEM((2, length, HALF), F32),
            pltpu.VMEM((2, shards, ff_part, TILE), BF),
            pltpu.VMEM((2, shards, attn_part, TILE), BF),
            pltpu.VMEM((count, rows, TILE), F32),
            pltpu.VMEM((2, count, rows, TILE), BF),
            dma((2,)),
            dma((2, count - 1)),
            dma((2, count - 1)),
            dma((2, 8)),
            dma((2, 8)),
            dma((3,)),
            dma((2, 2)),
            dma((2, 2)),
            dma((6, 2)),
            dma((2, 2)),
            dma((2,)),
        ],
        compiler_params=pltpu.CompilerParams(
            collective_id=3, has_side_effects=True, vmem_limit_bytes=58 * 2**20
        ),
        name="forward",
    )(order, slots, x_all, gain, bias, *tables, cot, w_down, w_out, w_inner, w_heads)


def feed_back_kernel(cot, down, attn, both, inner, d_att):
    d_att[...] = contract(cot[...], attn[...], ((1,), (1,))).astype(BF)
    d_hidden = contract(cot[...], down[...], ((1,), (1,)))
    for b in range(down.shape[0] // HALF):
        d = d_hidden[:, b * HALF : (b + 1) * HALF]
        gate = both[:, b * TILE : b * TILE + HALF].astype(F32)
        up = both[:, b * TILE + HALF : (b + 1) * TILE].astype(F32)
        sig = jax.nn.sigmoid(gate)
        inner[:, b * TILE : b * TILE + HALF] = (d * up * sig * (1.0 + gate * (1.0 - sig))).astype(BF)
        inner[:, b * TILE + HALF : (b + 1) * TILE] = (d * gate * sig).astype(BF)


def feed_back(cot, down, attn, both):
    length, width = cot.shape
    rows = length // 4
    whole = lambda a: pl.BlockSpec(a.shape, lambda i: (0, 0))
    by_rows = lambda columns: pl.BlockSpec((rows, columns), lambda i: (i, 0))
    return pl.pallas_call(
        feed_back_kernel,
        grid=(length // rows,),
        in_specs=[by_rows(width), whole(down), whole(attn), by_rows(both.shape[1])],
        out_specs=[by_rows(both.shape[1]), by_rows(attn.shape[0])],
        out_shape=[
            jax.ShapeDtypeStruct(both.shape, BF),
            jax.ShapeDtypeStruct((length, attn.shape[0]), BF),
        ],
        compiler_params=pltpu.CompilerParams(vmem_limit_bytes=50 * 2**20),
        cost_estimate=pl.CostEstimate(
            flops=2 * length * width * (down.shape[0] + attn.shape[0]), bytes_accessed=2**25, transcendentals=2**20
        ),
        name="feed_back",
    )(cot, down, attn, both)


def heads_back_kernel(q_in, k_in, v_in, do_in, att, lse, cos, first, second, out, dk, dv):
    length = q_in.shape[0]
    scale = HD ** (-0.5)
    row = lax.broadcasted_iota(jnp.int32, (CHUNK, CHUNK), 0)
    col = lax.broadcasted_iota(jnp.int32, (CHUNK, CHUNK), 1)
    dk[...] = jnp.zeros_like(dk)
    dv[...] = jnp.zeros_like(dv)
    for c in range(length // CHUNK):
        lo, hi = c * CHUNK, (c + 1) * CHUNK
        dqs = []
        for h in range(2):
            lanes = slice(h * HD, (h + 1) * HD)
            q, do = q_in[lo:hi, lanes], do_in[lo:hi, lanes]
            delta = jnp.sum(do.astype(F32) * att[lo:hi, lanes], axis=1, keepdims=True)
            s = contract(q, k_in[lo:hi, lanes], ((1,), (1,)))
            s = jnp.where(col <= row, s, NEG)
            if c:
                s = jnp.concatenate([contract(q, k_in[:lo, lanes], ((1,), (1,))), s], axis=1)
            p = jnp.exp(s - lse[lo:hi, h * HD : h * HD + 1])
            dp = contract(do, v_in[:hi, lanes], ((1,), (1,)))
            ds = (p * (dp - delta)).astype(BF)
            dqs.append(contract(ds, k_in[:hi, lanes], ((1,), (0,))) * scale)
            dk[:hi, lanes] += contract(ds, q, ((0,), (0,)))
            dv[:hi, lanes] += contract(p.astype(BF), do, ((0,), (0,)))
        dq = jnp.concatenate(dqs, axis=1)
        out[lo:hi, :HALF] = turn(dq, cos[lo:hi, :], -first[lo:hi, :], -second[lo:hi, :]).astype(BF)
    out[:, HALF : 2 * HALF] = turn(dk[...], cos[...], -first[...], -second[...]).astype(BF)
    out[:, 2 * HALF :] = dv[...].astype(BF)


def heads_back(q, k, v, d_attended, attended, lse, tables):
    length, width = q.shape
    heads = width // HD
    block = pl.BlockSpec((length, HALF), lambda h: (0, h))
    table = pl.BlockSpec((length, HALF), lambda h: (0, 0))
    return pl.pallas_call(
        heads_back_kernel,
        grid=(heads // 2,),
        in_specs=[block] * 6 + [table] * 3,
        out_specs=pl.BlockSpec((length, 3 * HALF), lambda h: (0, h)),
        out_shape=jax.ShapeDtypeStruct((length, 3 * width), BF),
        scratch_shapes=[pltpu.VMEM((length, HALF), F32)] * 2,
        compiler_params=pltpu.CompilerParams(vmem_limit_bytes=40 * 2**20),
        cost_estimate=pl.CostEstimate(
            flops=40 * heads * length * length * HD // 2,
            bytes_accessed=22 * length * width,
            transcendentals=heads * length * length // 2,
        ),
        name="heads_back",
    )(q, k, v, d_attended, attended, lse, *tables)


def norm_back_kernel(slots, d_inner, inner, d_mixed, heads, hat, out, small):
    value = contract(d_inner[...], inner[...], ((1,), (1,))) + contract(d_mixed[...], heads[...], ((1,), (1,)))
    count, rows = out.shape[0], out.shape[1]
    for p in range(count):
        out[slots[p]] = value[p * rows : (p + 1) * rows].astype(BF)
    gain = jnp.sum(value * hat[...].astype(F32), axis=0, keepdims=True)
    bias = jnp.sum(value, axis=0, keepdims=True)
    row = lax.broadcasted_iota(jnp.int32, small.shape, 0)
    small[...] = jnp.where(row == 0, gain, jnp.where(row == 1, bias, 0.0)).astype(BF)


def norm_back(slots, d_inner, inner, d_mixed, heads, hat, count):
    length, width = hat.shape
    whole = lambda a: pl.BlockSpec(a.shape, lambda i, s: (0, 0))
    by_rows = lambda a: pl.BlockSpec((TILE, a.shape[1]), lambda i, s: (i, 0))
    return pl.pallas_call(
        norm_back_kernel,
        grid_spec=pltpu.PrefetchScalarGridSpec(
            num_scalar_prefetch=1,
            grid=(width // TILE,),
            in_specs=[
                whole(d_inner),
                by_rows(inner),
                whole(d_mixed),
                by_rows(heads),
                pl.BlockSpec((length, TILE), lambda i, s: (0, i)),
            ],
            out_specs=[
                pl.BlockSpec((count, length // count, TILE), lambda i, s: (0, 0, i)),
                pl.BlockSpec((16, TILE), lambda i, s: (0, i)),
            ],
        ),
        out_shape=[
            jax.ShapeDtypeStruct((count, length // count, width), BF),
            jax.ShapeDtypeStruct((16, width), BF),
        ],
        compiler_params=pltpu.CompilerParams(vmem_limit_bytes=50 * 2**20),
        cost_estimate=pl.CostEstimate(
            flops=2 * length * width * (d_inner.shape[1] + d_mixed.shape[1]), bytes_accessed=2**25, transcendentals=0
        ),
        name="norm_back",
    )(slots, d_inner, inner, d_mixed, heads, hat)


def rows_of(shard, part):
    return slice(shard * part, (shard + 1) * part)


def gradients_kernel(
    hid_t, att_t, cot, norm_t, d_inner, d_mixed, small, branch, d_normed, pieces, sums,
    partial, theirs, pair, landed, total,
    sum_from, sum_land,
    core_send, core_recv, chip_send, chip_recv, line_send, line_recv, own_sem, sum_send, sum_recv,
):
    count = pieces.shape[0]
    chunks = pieces.shape[1]
    shards = 2 * partial.shape[1]
    chips = shards // 2
    place, me = lax.axis_index("ctx"), lax.axis_index("fsdp")
    chip, core = me // 2, me % 2
    ff_part, attn_part = hid_t.shape[0] // shards, att_t.shape[0] // shards
    cot_chunks = cot.shape[1] // TILE
    inner_chunks = d_inner.shape[1] // TILE
    sum_parts = branch.shape[2] // TILE

    def core_copy(i):
        return pltpu.make_async_remote_copy(
            src_ref=partial.at[i % 2, :, 1 - core],
            dst_ref=theirs.at[i % DEEP],
            send_sem=core_send.at[i % 2],
            recv_sem=core_recv.at[i % DEEP],
            device_id=(place, me + 1 - 2 * core),
            device_id_type=MESH,
        )

    def chip_of(m):
        return chip_away(chip, m)

    def chip_copy(j, m):
        return pltpu.make_async_remote_copy(
            src_ref=pair.at[j % 2, chip_of(m)],
            dst_ref=landed.at[j % DEEP, m - 1],
            send_sem=chip_send.at[j % 2, m - 1],
            recv_sem=chip_recv.at[j % DEEP, m - 1],
            device_id=(place, 2 * chip_of(m) + core),
            device_id_type=MESH,
        )

    def line_copy(way, hop, k):
        ahead = 1 - 2 * way
        origin = place - (hop - 1) * ahead
        return pltpu.make_async_remote_copy(
            src_ref=total.at[k % DEEP] if hop == 1 else pieces.at[origin, k],
            dst_ref=pieces.at[origin, k],
            send_sem=line_send.at[way, hop - 1, k % DEEP],
            recv_sem=line_recv.at[way, k, hop - 1],
            device_id=(place + ahead, me),
            device_id_type=MESH,
        )

    def sends(way, hop):
        if way == 0:
            return (place >= hop - 1) & (place <= count - 2)
        return (place <= count - hop) & (place >= 1)

    def lands(way, hop):
        return place >= hop if way == 0 else place <= count - 1 - hop

    def forward(hop, k):
        for way in range(2):
            if hop > 1:
                @pl.when(lands(way, hop - 1))
                def _():
                    line_copy(way, hop - 1, k).wait_recv()

            if hop < count:
                @pl.when(sends(way, hop))
                def _():
                    @pl.when(k >= DEEP)
                    def _():
                        line_copy(way, hop, k - DEEP).wait_send()

                    line_copy(way, hop, k).start()

    def sum_copy(way, t, q):
        return pltpu.make_async_remote_copy(
            src_ref=sum_from.at[way, t - 1, q % 2],
            dst_ref=sum_land.at[way, t - 1, q],
            send_sem=sum_send.at[way, t - 1, q % 2],
            recv_sem=sum_recv.at[way, t - 1, q],
            device_id=(place + 1 - 2 * way, me),
            device_id_type=MESH,
        )

    def sum_sends(way, t):
        return place <= t - 1 if way == 0 else place >= count - t

    def both_terms(q, use):
        for which, terms in enumerate((branch, d_normed)):
            at = (q - which * sum_parts) * TILE

            @pl.when((q >= which * sum_parts) & (q < (which + 1) * sum_parts))
            def _(which=which, terms=terms, at=at):
                use(which, terms, pl.ds(pl.multiple_of(at, TILE), TILE))

    def sum_step(t, q):
        for way in range(2):
            @pl.when(sum_sends(way, t))
            def _(way=way):
                to = count - t + place if way == 0 else t + place - count
                first = place == 0 if way == 0 else place == count - 1

                @pl.when(q >= 2)
                def _():
                    sum_copy(way, t, q - 2).wait_send()

                @pl.when(first)
                def _():
                    def use(which, terms, at):
                        sum_from[way, t - 1, q % 2] = terms[to, :, at]

                    both_terms(q, use)

                if t > 1:
                    @pl.when(jnp.logical_not(first))
                    def _():
                        sum_copy(way, t - 1, q).wait_recv()

                        def use(which, terms, at):
                            value = terms[to, :, at].astype(F32) + sum_land[way, t - 2, q].astype(F32)
                            sum_from[way, t - 1, q % 2] = value.astype(BF)

                        both_terms(q, use)

                sum_copy(way, t, q).start()

    def sum_end(q):
        def use(which, terms, at):
            sums[which, :, at] = terms[place, :, at].astype(F32)

        both_terms(q, use)
        for way in range(2):
            @pl.when(place >= 1 if way == 0 else place <= count - 2)
            def _(way=way):
                sum_copy(way, count - 1, q).wait_recv()

                def use(which, terms, at):
                    sums[which, :, at] += sum_land[way, count - 2, q].astype(F32)

                both_terms(q, use)

    def own_copy(k):
        return pltpu.make_async_copy(total.at[k % DEEP], pieces.at[place, k], own_sem.at[k % DEEP])

    partners = [(place, me + 1 - 2 * core)]
    partners += [(place, 2 * chip_of(m) + core) for m in range(1, chips)]
    partners += [((place + 1) % count, me), ((place + count - 1) % count, me)]
    barrier = pltpu.get_barrier_semaphore()
    for partner in partners:
        pl.semaphore_signal(barrier, inc=1, device_id=partner, device_id_type=MESH)
    pl.semaphore_wait(barrier, len(partners))
    def store(i, shard, lo, value):
        partial[i % 2, shard // 2, shard % 2, lo : lo + value.shape[0], :] = value

    def from_norm(i, rhs):
        for s in range(0, shards, 2):
            rows = norm_t.shape[0] // shards
            value = contract(norm_t[s * rows : (s + 2) * rows, :], rhs, ((1,), (0,))).astype(BF)
            store(i, s, 0, value[:rows])
            store(i, s + 1, 0, value[rows:])

    def step(i, carry):
        @pl.when(i < cot_chunks)
        def _():
            rhs = cot[:, pl.ds(pl.multiple_of(i * TILE, TILE), TILE)]
            for s in range(0, shards, 4):
                value = contract(hid_t[s * ff_part : (s + 4) * ff_part, :], rhs, ((1,), (0,))).astype(BF)
                for t in range(4):
                    store(i, s + t, 0, value[rows_of(t, ff_part)])
            value = contract(att_t[...], rhs, ((1,), (0,))).astype(BF)
            for s in range(shards):
                store(i, s, ff_part, value[rows_of(s, attn_part)])
                store(i, s, ff_part + attn_part, small[:, s * TILE : (s + 1) * TILE])

        @pl.when((i >= cot_chunks) & (i < cot_chunks + inner_chunks))
        def _():
            at = pl.ds(pl.multiple_of((i - cot_chunks) * TILE, TILE), TILE)
            from_norm(i, d_inner[:, at])

        @pl.when((i >= cot_chunks + inner_chunks) & (i < chunks))
        def _():
            at = pl.multiple_of((i - cot_chunks - inner_chunks) * TILE, TILE)
            from_norm(i, d_mixed[:, pl.ds(at, TILE)])

        @pl.when(i < chunks)
        def _():
            core_copy(i).start()

        @pl.when((i >= 1) & (i < chunks + 1))
        def _():
            j = i - 1
            core_copy(j).wait()
            for m in range(chips):
                a = partial[j % 2, m, core].astype(F32) + theirs[j % DEEP, m].astype(F32)
                pair[j % 2, m] = a.astype(BF)
            for m in range(1, chips):
                chip_copy(j, m).start()

        @pl.when((i >= 2) & (i < chunks + 2))
        def _():
            k = i - 2
            for m in range(1, chips):
                chip_copy(k, m).wait()

            a = pair[k % 2, chip].astype(F32)
            for m in range(1, chips):
                a = a + landed[k % DEEP, m - 1].astype(F32)
            for way in range(2):
                @pl.when(sends(way, 1) & (k >= DEEP))
                def _():
                    line_copy(way, 1, k - DEEP).wait_send()

            @pl.when(k >= DEEP)
            def _():
                own_copy(k - DEEP).wait()

            total[k % DEEP] = a.astype(BF)
            for way in range(2):
                @pl.when(sends(way, 1))
                def _():
                    line_copy(way, 1, k).start()

            own_copy(k).start()

        for t in range(1, count + 1):
            q = i - LAG * (t - 1)

            @pl.when((q >= 0) & (q < 2 * sum_parts))
            def _(q=q, t=t):
                if t < count:
                    sum_step(t, q)
                else:
                    sum_end(q)

        for hop in range(2, count + 1):
            k = i - 2 - LAG * (hop - 1)

            @pl.when((k >= 0) & (k < chunks))
            def _(k=k, hop=hop):
                forward(hop, k)

        return carry

    lax.fori_loop(0, chunks + 2 + LAG * (count - 1), step, 0)

    def drain(k, carry):
        own_copy(k).wait()
        for way in range(2):
            for hop in range(1, count):
                @pl.when(sends(way, hop))
                def _():
                    line_copy(way, hop, k).wait_send()
        return carry

    lax.fori_loop(chunks - DEEP, chunks, drain, 0)
    for way in range(2):
        for t in range(1, count):
            @pl.when(sum_sends(way, t))
            def _(way=way, t=t):
                for q in range(2):
                    sum_copy(way, t, 2 * sum_parts - 2 + q).wait_send()


def gradients(hid_t, att_t, cot, norm_t, d_inner, d_mixed, small, branch, d_normed, count, shards):
    chips = shards // 2
    chunks = (cot.shape[1] + d_inner.shape[1] + d_mixed.shape[1]) // TILE
    rows = norm_t.shape[0] // shards
    dma = pltpu.SemaphoreType.DMA
    own_rows, width = branch.shape[1:]
    parts = 2 * width // TILE
    return pl.pallas_call(
        gradients_kernel,
        out_shape=[
            jax.ShapeDtypeStruct((count, chunks, rows, TILE), BF),
            jax.ShapeDtypeStruct((2, own_rows, width), F32),
        ],
        in_specs=[vmem_whole()] * 9,
        out_specs=[hbm_whole(), vmem_whole()],
        scratch_shapes=[
            pltpu.VMEM((2, chips, 2, rows, TILE), BF),
            pltpu.VMEM((DEEP, chips, rows, TILE), BF),
            pltpu.VMEM((2, chips, rows, TILE), BF),
            pltpu.VMEM((DEEP, chips - 1, rows, TILE), BF),
            pltpu.VMEM((DEEP, rows, TILE), BF),
            pltpu.VMEM((2, count - 1, 2, own_rows, TILE), BF),
            pltpu.VMEM((2, count - 1, parts, own_rows, TILE), BF),
            dma((2,)),
            dma((DEEP,)),
            dma((2, chips - 1)),
            dma((DEEP, chips - 1)),
            dma((2, count - 1, DEEP)),
            dma((2, chunks, count - 1)),
            dma((DEEP,)),
            dma((2, count - 1, 2)),
            dma((2, count - 1, parts)),
        ],
        compiler_params=pltpu.CompilerParams(
            collective_id=1, has_side_effects=True, vmem_limit_bytes=60 * 2**20
        ),
        cost_estimate=pl.CostEstimate(
            flops=2 * norm_t.shape[0] * norm_t.shape[1] * TILE * chunks, bytes_accessed=2**27, transcendentals=0
        ),
        name="gradients",
    )(hid_t, att_t, cot, norm_t, d_inner, d_mixed, small, branch, d_normed)


def column_runs(columns, source):
    out = []
    for block in range(columns // HALF):
        first = 0
        while first < HALF:
            key, lane = source(block * HALF + first)
            last = first + 1
            while last < HALF and source(block * HALF + last) == (key, lane + last - first):
                last += 1
            out.append((block, first, last, key, (first - lane) % HALF))
            first = last
    return out


def assemble_kernel(down_chunks, rows_in, cols_in, qkv_out, gate_out, up_out, down_out, attn_out, small_out):
    count, chunks, rows, _ = rows_in.shape
    cot_chunks_static = down_chunks
    ff = gate_out.shape[1]
    width = qkv_out.shape[1]
    ff_part = down_out.shape[0] // count
    attn_part = attn_out.shape[0] // count
    shards = ff // (count * ff_part)
    inner_chunks = ff // count // HALF
    lane = lax.broadcasted_iota(jnp.int32, (rows, HALF), 1)

    def gather(out, runs, load):
        for block, first, last, key, shift in runs:
            value = load(key).astype(F32)
            if shift:
                value = pltpu.roll(value, shift, 1)
            if first:
                value = jnp.where(lane >= first, value, held)
            held = value
            if last == HALF:
                out[:, block * HALF : (block + 1) * HALF] = value

    def inner_source(column):
        shard, rest = divmod(column, count * ff_part)
        unit = shard * ff_part + rest % ff_part
        return (rest // ff_part, unit // HALF), unit % HALF

    def head_source(column):
        part, rest = divmod(column, width // 3)
        head, dim = divmod(rest, HD)
        per = width // 3 // HD // shards // count
        shard, at = divmod(head, per * count)
        place, sub = divmod(at, per)
        pair, half = divmod(shard * per + sub, 2)
        return (place, 3 * pair + part), half * HD + dim

    runs = column_runs(ff, inner_source)
    gather(gate_out, runs, lambda key: rows_in[key[0], cot_chunks_static + key[1], :, :HALF])
    gather(up_out, runs, lambda key: rows_in[key[0], cot_chunks_static + key[1], :, HALF:])
    first_head = cot_chunks_static + inner_chunks

    def head_load(key):
        at = key[1] % 2 * HALF
        return rows_in[key[0], first_head + key[1] // 2, :, at : at + HALF]

    gather(qkv_out, column_runs(width, head_source), head_load)
    for p in range(count):
        down_out[p * ff_part : (p + 1) * ff_part, :] = cols_in[p, 0, :ff_part, :].astype(F32)
        attn_out[p * attn_part : (p + 1) * attn_part, :] = cols_in[
            p, 0, ff_part : ff_part + attn_part, :
        ].astype(F32)
    small = [cols_in[p, 0, ff_part + attn_part :, :].astype(F32) for p in range(count)]
    small_out[...] = functools.reduce(jnp.add, small)


def assemble_outputs(pieces, qkv, attn, gate, down):
    count, chunks, rows, _ = pieces.shape
    steps = down[1] // TILE
    part = rows // steps
    by_rows = lambda shape: pl.BlockSpec((part, shape[1]), lambda i: (i, 0))
    by_cols = lambda shape: pl.BlockSpec((shape[0], TILE), lambda i: (0, i))
    return pl.pallas_call(
        functools.partial(assemble_kernel, steps),
        grid=(steps,),
        in_specs=[
            pl.BlockSpec((count, chunks, part, TILE), lambda i: (0, 0, i, 0)),
            pl.BlockSpec((count, 1, rows, TILE), lambda i: (0, i, 0, 0)),
        ],
        out_specs=[by_rows(qkv), by_rows(gate), by_rows(gate), by_cols(down), by_cols(attn)]
        + [pl.BlockSpec((16, TILE), lambda i: (0, 0))],
        out_shape=[jax.ShapeDtypeStruct(s, F32) for s in (qkv, gate, gate, down, attn, (16, TILE))],
        compiler_params=pltpu.CompilerParams(vmem_limit_bytes=40 * 2**20),
        name="assemble",
    )(pieces, pieces)


def rotation_tables(length):
    half = ROT // 2
    inverse = 10000.0 ** (-jnp.arange(half, dtype=F32) / half)
    grid = jnp.arange(length, dtype=jnp.int32).astype(F32)[:, None] * inverse[None, :]
    cos, sin = jnp.cos(grid), jnp.sin(grid)
    zero = jnp.zeros((length, half), F32)
    rest = jnp.zeros((length, HD - ROT), F32)
    tables = (
        jnp.concatenate([cos, cos, rest + 1.0], axis=1),
        jnp.concatenate([-sin, zero, rest], axis=1),
        jnp.concatenate([zero, sin, rest], axis=1),
    )
    return tuple(jnp.tile(t, (1, 2)) for t in tables)


def body_general(tokens, block_order, ln_gain, ln_bias, w_qkv, w_out, w_gate, w_up, w_down, cotangent):
    rows, width = tokens.shape[1], tokens.shape[2]
    count = lax.axis_size("ctx")
    shards = lax.axis_size("fsdp")
    place = lax.axis_index("ctx")
    length = rows * count
    order = block_order[0]
    shard_rows = w_qkv.shape[0]
    ff_shard = w_down.shape[0]
    ff_part = ff_shard // count
    own_heads = H // count
    spread = (w_out.shape[0] // HD) % count == 0
    groups = shards if spread else 1
    head_cols = own_heads * HD // groups

    def my_cols(w, outer, group, part):
        w = w.reshape(w.shape[0], outer, group, count, part)
        return lax.dynamic_index_in_dim(w, place, 3, False).reshape(w.shape[0], outer * group * part)

    def all_cols(piece, outer, group, part):
        whole = gather_ctx(piece).reshape(count, piece.shape[0], outer, group, part)
        return whole.transpose(1, 2, 3, 0, 4).reshape(piece.shape[0], -1).astype(F32)

    def assemble(block, ready=None):
        whole = jnp.zeros((length, width), block.dtype)
        whole = lax.dynamic_update_slice_in_dim(whole, block, order[place] * rows, 0)
        last = None
        for k in range(1, count):
            last = ring_send(block, k)
            source = (place - k) % count
            whole = lax.dynamic_update_slice_in_dim(whole, last, order[source] * rows, 0)
        return whole, last

    gain = lax.all_gather(ln_gain, "fsdp", axis=0, tiled=True).astype(F32)
    bias = lax.all_gather(ln_bias, "fsdp", axis=0, tiled=True).astype(F32)
    tables = rotation_tables(length)

    block = tokens[0]
    x_all, arrived = assemble(block)
    grad_block = cotangent[0]
    cot_all, _ = assemble(after(grad_block, arrived))

    inner = jnp.concatenate(
        [my_cols(w_gate, 1, shards, ff_part), my_cols(w_up, 1, shards, ff_part)], axis=1
    )
    w_inner, sent = gather_rows(inner)
    w_heads, sent = gather_rows(after(my_cols(w_qkv, 3, groups, head_cols), sent))
    down = lax.dynamic_slice_in_dim(w_down, place * ff_part, ff_part, 0)
    w_hidden, sent = gather_rows(after(down, sent))
    if spread:
        part = w_out.shape[0] // count
        attn = lax.dynamic_slice_in_dim(w_out, place * part, part, 0)
        w_attn, sent = gather_rows(after(attn, sent))
    else:
        w_attn = lax.all_gather(after(w_out, sent), "fsdp", axis=0, tiled=True)
        w_attn = lax.dynamic_slice_in_dim(w_attn, place * own_heads * HD, own_heads * HD, 0)

    xf = x_all.astype(F32)
    average = jnp.mean(xf, axis=-1, keepdims=True)
    centered = xf - average
    variance = jnp.mean(centered * centered, axis=-1, keepdims=True)
    inv_std = lax.rsqrt(variance + EPS)
    x_hat = centered * inv_std
    normed = (x_hat * gain + bias).astype(BF)

    across = ((1,), (0,))
    over_tokens = ((0,), (0,))
    back = ((1,), (1,))
    ff_cols = shards * ff_part
    gate_value = dot(normed, w_inner[:, :ff_cols], across)
    up_value = dot(normed, w_inner[:, ff_cols:], across)
    sigmoid_gate = jax.nn.sigmoid(gate_value)
    hidden = (gate_value * sigmoid_gate * up_value).astype(BF)
    mixed = dot(normed, w_heads, across)
    q, k, v, attended, lse = attend(mixed, tables, own_heads)
    attended_low = attended.astype(BF)

    branch = dot(attended_low, w_attn, across) + dot(hidden, w_hidden, across)
    out = line_scatter(lambda j: lax.dynamic_slice_in_dim(branch, order[j] * rows, rows, 0))
    out = (block.astype(F32) + out).astype(BF)[None]

    d_hidden = dot(cot_all, w_hidden, back)
    grad_down = scatter_rows(dot(hidden, cot_all, over_tokens, BF))
    d_gate_act = (
        d_hidden * up_value * sigmoid_gate * (1.0 + gate_value * (1.0 - sigmoid_gate))
    ).astype(BF)
    d_up_act = (d_hidden * gate_value * sigmoid_gate).astype(BF)
    d_inner = jnp.concatenate([d_gate_act, d_up_act], axis=1)
    d_attended = dot(cot_all, w_attn, back, BF)
    d_mixed = attend_back(q, k, v, d_attended, attended, lse, tables, own_heads)
    d_mixed = jnp.concatenate(d_mixed, axis=1)
    grad_inner = scatter_rows(dot(normed, d_inner, over_tokens, BF))
    grad_attn = dot(attended_low, cot_all, over_tokens, BF)
    grad_heads = scatter_rows(dot(normed, d_mixed, over_tokens, BF))

    d_normed = dot(d_inner, w_inner, back) + dot(d_mixed, w_heads, back)
    small = jnp.stack([jnp.sum(d_normed * x_hat, axis=0), jnp.sum(d_normed, axis=0)])
    small = lax.psum(small, ("ctx", "fsdp"))
    small = lax.dynamic_slice_in_dim(small, lax.axis_index("fsdp") * shard_rows, shard_rows, 1)
    d_own = line_scatter(lambda j: lax.dynamic_slice_in_dim(d_normed, order[j] * rows, rows, 0))
    own = block.astype(F32)
    own_average = jnp.mean(own, axis=-1, keepdims=True)
    own = own - own_average
    own_std = lax.rsqrt(jnp.mean(own * own, axis=-1, keepdims=True) + EPS)
    own = own * own_std
    scaled = d_own * gain
    d_input = own_std * (
        scaled
        - jnp.mean(scaled, axis=-1, keepdims=True)
        - own * jnp.mean(scaled * own, axis=-1, keepdims=True)
    )
    grad_in = (grad_block.astype(F32) + d_input)[None]

    down_all = gather_ctx(grad_down).reshape(ff_shard, width).astype(F32)
    if spread:
        attn_all = gather_ctx(scatter_rows(grad_attn)).reshape(w_out.shape).astype(F32)
    else:
        full = jnp.zeros((H * HD, width), BF)
        full = lax.dynamic_update_slice_in_dim(full, grad_attn, place * own_heads * HD, 0)
        full = lax.psum_scatter(full, "fsdp", scatter_dimension=0, tiled=True)
        attn_all = lax.psum(full, "ctx").astype(F32)
    heads_all = all_cols(grad_heads, 3, groups, head_cols)
    inner_all = gather_ctx(grad_inner).reshape(count, shard_rows, 2, shards, ff_part)
    inner_all = inner_all.transpose(2, 1, 3, 0, 4).reshape(2, shard_rows, -1).astype(F32)
    return (
        out,
        grad_in,
        small[0],
        small[1],
        heads_all,
        attn_all,
        inner_all[0],
        inner_all[1],
        down_all,
    )


def body_fast(tokens, block_order, ln_gain, ln_bias, w_qkv, w_out, w_gate, w_up, w_down, cotangent):
    count, shards = lax.axis_size("ctx"), lax.axis_size("fsdp")
    place = lax.axis_index("ctx")
    block, grad_block = tokens[0], cotangent[0]
    rows, width = block.shape
    order = block_order[0]
    spots = jnp.arange(count, dtype=jnp.int32)
    slots = jnp.sum(jnp.where(order[None, :] == spots[:, None], spots[None, :], 0), axis=1)
    vectors = jnp.stack([ln_gain, ln_bias] + [jnp.zeros_like(ln_gain)] * 6).astype(F32)
    x_all, vectors, w_inner, w_heads = start(block, vectors, w_gate, w_up, w_qkv, count, shards)
    w_inner = w_inner.reshape(width, -1)
    w_heads = w_heads.reshape(width, -1)
    gain, bias = vectors[:, 0].reshape(1, width), vectors[:, 1].reshape(1, width)
    tables = rotation_tables(rows * count)

    (
        cot_all, w_hidden, w_attn, normed_t, hat, both, hidden_t, q, k, v, attended, low_t, lse, branch,
    ) = forward(
        order, slots, x_all, gain, bias, tables, grad_block, w_down, w_out, w_inner, w_heads, shards
    )
    cot_all = [lax.dynamic_index_in_dim(cot_all, slots[p], 0, False) for p in range(count)]
    cot_all = jnp.concatenate(cot_all, axis=0)
    w_hidden, w_attn = w_hidden.reshape(-1, width), w_attn.reshape(-1, width)
    d_inner, d_attended = feed_back(cot_all, w_hidden, w_attn, both)
    d_mixed = heads_back(q, k, v, d_attended, attended, lse, tables)
    d_normed, small = norm_back(slots, d_inner, w_inner, d_mixed, w_heads, hat, count)
    pieces, sums = gradients(
        hidden_t, low_t, cot_all, normed_t, d_inner, d_mixed, small, branch, d_normed, count, shards
    )
    d_qkv, d_gate, d_up, d_down, d_attn, small = assemble_outputs(
        pieces, w_qkv.shape, w_out.shape, w_gate.shape, w_down.shape
    )
    own = block.astype(F32)
    out = (own + sums[0]).astype(BF)[None]
    own = own - jnp.mean(own, axis=-1, keepdims=True)
    own_std = lax.rsqrt(jnp.mean(own * own, axis=-1, keepdims=True) + EPS)
    own = own * own_std
    scaled = sums[1] * gain
    d_input = own_std * (
        scaled
        - jnp.mean(scaled, axis=-1, keepdims=True)
        - own * jnp.mean(scaled * own, axis=-1, keepdims=True)
    )
    grad_in = (grad_block.astype(F32) + d_input)[None]
    return out, grad_in, small[0], small[1], d_qkv, d_attn, d_gate, d_up, d_down


def solution(mesh):
    whole, once = P("fsdp", "ctx", None), P("fsdp", None)
    count, shards = mesh.shape["ctx"], mesh.shape["fsdp"]

    def body(*args):
        w_out, w_down = args[5], args[8]
        fits = shards == 8 and w_out.shape[0] == count * HD and w_out.shape[0] == TILE
        fits = fits and w_down.shape[0] % (16 * count) == 0 and w_down.shape[0] // count <= 176
        return (body_fast if fits else body_general)(*args)

    return jax.shard_map(
        body,
        mesh=mesh,
        in_specs=(whole, once, P("fsdp"), P("fsdp")) + (once,) * 5 + (whole,),
        out_specs=(whole, whole, P("fsdp"), P("fsdp")) + (once,) * 5,
        check_vma=False,
    )
```

profile of v0, /device:TPU:0, one launch (start us, length us, event | category | flops | bytes accessed | tf_op | source)
XLA Modules:
  0.0 579.4 jit_solution(1509645848913305628)
XLA Ops:
  0.7 0.2 multiply_sine_fusion
  0.9 0.1 pad.12.clone
  1.0 0.1 pad.9.clone
  1.0 0.1 maximum_maximum_fusion.2
  1.2 0.0 copy-start.23
  1.2 0.0 copy-start.24
  1.2 0.0 copy-start.1
  1.3 1.0 copy.25.cos
  2.3 1.0 copy.26.first
  3.3 1.0 copy.27.second
  4.3 0.1 pad.15.clone
  4.4 0.1 pad.16.clone
  4.5 0.0 copy-done.23
  4.5 0.0 copy-done.24
  4.5 0.1 maximum_convert_fusion.vectors
  4.6 0.0 copy-done.1
  4.6 0.0 copy-start.4
  4.6 1.9 copy-done.4
  6.5 1.8 copy-done.5
  8.3 1.8 copy-done.6
  10.1 83.4 %start.1 = (bf16[4,256,2048]{2,1,0:T(8,128)(2,1)S(1)}, f32[8,8,256]{2,1,0:T(8,128)S(1)}, bf16[8,256,2816]{2,1,0:T(8,128)(2,1)}, bf16[8,256,1536]{2,1,0:T(8,128)(2,1)S(1)}) custom-call(bf16[256,2048]{1,0:T(8,128)(2,1)S(1)} %bitcast.36, f32[8,256]{1,0:T(8,128)S(1)} %maximum_convert_fusion.vectors, bf16[256,5632]{1,0:T(8,128)(2,1)S(1)} %copy-done.5, ...), custom_call_target="tpu_custom_call" | custom-call | tf_op jit(solution)/shard_map/start/pallas_call | solution.py:446
  93.6 0.0 copy-start.2
  93.6 2.7 copy-done.2
  96.3 2.0 copy-done.3
  98.3 0.6 fusion.13
  98.9 0.0 copy-done.22
  98.9 0.6 select_reduce_fusion.slots
  99.5 80.6 %forward.1 = (bf16[4,256,2048]{2,1,0:T(8,128)(2,1)}, bf16[8,176,2048]{2,1,0:T(8,128)(2,1)}, bf16[8,64,2048]{2,1,0:T(8,128)(2,1)}, bf16[2048,1024]{1,0:T(8,128)(2...) custom-call(s32[4]{0:T(128)} %bitcast.52, ...), custom_call_target="tpu_custom_call" | custom-call | tf_op jit(solution)/shard_map/forward/pallas_call | solution.py:702
  180.2 0.0 copy-done.10
  180.2 0.6 fusion.15
  188.6 2.8 dynamic-slice_bitcast_fusion.3
  191.3 0.0 copy-start.13
  191.3 2.3 pad_maximum_fusion.cot
  193.6 0.1 copy-done.13
  193.8 0.0 copy-start.12
  193.8 0.0 copy-start.14
  193.8 0.0 copy-start.15
  193.8 0.0 copy-start.16
  193.8 15.9 %feed_back.1 = (bf16[1024,2816]{1,0:T(8,128)(2,1)}, bf16[1024,512]{1,0:T(8,128)(2,1)S(1)}) custom-call(bf16[1024,2048]{1,0:T(8,128)(2,1)} %pad_maximum_fusion.cot, bf16[1408,2048]{1,0:T(8,128)(2,1)} %bitcast.54, bf16[512,2048]{1,0:T(8,128)(2,1)S(1)} %bitcast.39, bf16[1024,2816]{1,0:T(8,128)(2,1)} %get-tuple-element.49.both), custom_call_target="tpu_custom_call" | custom-call | flops 8053063680 | bytes 33554432 | tf_op jit(solution)/shard_map/feed_back/pallas_call | solution.py:763
  209.7 0.0 copy-done.7
  209.7 0.0 copy-done.8
  209.7 0.0 copy-done.9
  209.7 0.0 copy-done.11
  209.7 0.0 copy-done.12
  209.7 0.0 copy-done.14
  209.7 0.0 copy-done.15
  209.8 0.0 copy-done.16
  209.8 33.2 %heads_back.1.d_mixed = bf16[1024,1536]{1,0:T(8,128)(2,1)S(1)} custom-call(bf16[1024,512]{1,0:T(8,128)(2,1)S(1)} %copy-done.14, bf16[1024,512]{1,0:T(8,128)(2,1)S(1)} %copy-done.15, bf16[1024,512]{1,0:T(8,128)(2,1)S(1)} %copy-done.16, bf16[1024,512]{1,0:T(8,128)(2,1)S(1)} %get-tuple-element.54.do_in, f32[1024,512]{1,0:T(8,128)S(1)} %copy-done.11, ...), custom_call_target="tpu_custom_call" | custom-call | flops 10737418240 | bytes 11534336 | tf_op jit(solution)/shard_map/heads_back/pallas_call | solution.py:815
  243.0 0.0 copy-start.17
  243.0 25.9 %norm_back.1 = (bf16[4,256,2048]{2,1,0:T(8,128)(2,1)}, bf16[16,2048]{1,0:T(8,128)(2,1)S(1)}) custom-call(s32[4]{0:T(128)S(1)} %copy-done.10, bf16[1024,2816]{1,0:T(8,128)(2,1)} %get-tuple-element.50.d_inner, bf16[2048,2816]{1,0:T(8,128)(2,1)} %bitcast.41, bf16[1024,1536]{1,0:T(8,128)(2,1)S(1)} %heads_back.1.d_mixed, bf16[2048,1536]{1,0:T(8,128)(2,1)} %bitcast.38, ...), custom_call_target="tpu_custom_call" | custom-call | flops 18253611008 | bytes 33554432 | tf_op jit(solution)/shard_map/norm_back/pallas_call | solution.py:847
  268.9 0.0 copy-done.17
  268.9 0.6 copy-done.18
  269.5 290.0 %gradients.1 = (bf16[4,25,256,256]{3,2,1,0:T(8,128)(2,1)}, f32[2,256,2048]{2,1,0:T(8,128)}) custom-call(bf16[1408,1024]{1,0:T(8,128)(2,1)} %get-tuple-element.43.hid_t, bf16[512,1024]{1,0:T(8,128)(2,1)} %get-tuple-element.44.att_t, bf16[1024,2048]{1,0:T(8,128)(2,1)} %pad_maximum_fusion.cot, bf16[2048,1024]{1,0:T(8,128)(2,1)} %get-tuple-element.46.norm_t, ...), custom_call_target="tpu_custom_call" | custom-call | flops 26843545600 | bytes 134217728 | tf_op jit(solution)/shard_map/gradients/pallas_call | solution.py:1152
  559.5 0.0 copy-start
  559.5 4.7 copy-done
  564.3 10.2 %assemble.1 = (f32[256,6144]{1,0:T(8,128)}, f32[256,5632]{1,0:T(8,128)}, f32[256,5632]{1,0:T(8,128)}, f32[704,2048]{1,0:T(8,128)}, f32[256,2048]{1,0:T(8,128)}, /*index=5*/f32[16,256]{1,0:T(8,128)S(1)}) custom-call(bf16[4,25,256,256]{3,2,1,0:T(8,128)(2,1)S(1)} %copy-done, bf16[4,25,256,256]{3,2,1,0:T(8,128)(2,1)S(1)} %copy-done), custom_call_target="tpu_custom_call" | custom-call | tf_op jit(solution)/shard_map/assemble/pallas_call | solution.py:1263
  574.5 0.6 fusion.14
  575.0 0.2 convert_reduce_fusion
  575.3 0.4 fusion.2
  575.7 0.0 copy-done.19
  575.7 0.0 copy-done.21
  575.7 0.6 fusion.11
  576.3 0.0 copy-done.20
  576.4 2.6 fusion.10
  (29 shorter events, 0.2 us)
Async XLA Ops:
  1.2 3.3 copy-start.23
  1.2 3.3 copy-start.24
  1.2 3.4 copy-start.1
  4.6 1.9 copy-start.4
  6.5 1.8 copy-start.5
  8.3 1.8 copy-start.6
  10.1 88.8 %copy-start.22 = (s32[1,4]{1,0:T(1,128)S(1)}, s32[1,4]{1,0:T(1,128)}, u32[]{:S(2)}) copy-start(s32[1,4]{1,0:T(1,128)} %param.11) | copy-start | bytes 52
  93.6 2.7 copy-start.2
  96.3 2.0 copy-start.3
  99.5 80.7 %copy-start.10 = (s32[4]{0:T(128)S(1)}, s32[4]{0:T(128)}, u32[]{:S(2)}) copy-start(s32[4]{0:T(128)} %select_reduce_fusion.slots) | copy-start | bytes 52
  191.3 2.4 copy-start.13
  193.8 15.9 %copy-start.7 = (f32[1024,128]{1,0:T(8,128)S(1)}, f32[1024,128]{1,0:T(8,128)}, u32[]{:S(2)}) copy-start(f32[1024,128]{1,0:T(8,128)} %copy.25.cos) | copy-start | bytes 1572868
  193.8 15.9 %copy-start.8 = (f32[1024,128]{1,0:T(8,128)S(1)}, f32[1024,128]{1,0:T(8,128)}, u32[]{:S(2)}) copy-start(f32[1024,128]{1,0:T(8,128)} %copy.26.first) | copy-start | bytes 1572868
  193.8 15.9 %copy-start.9 = (f32[1024,128]{1,0:T(8,128)S(1)}, f32[1024,128]{1,0:T(8,128)}, u32[]{:S(2)}) copy-start(f32[1024,128]{1,0:T(8,128)} %copy.27.second) | copy-start | bytes 1572868
  193.8 16.0 %copy-start.11 = (f32[1024,512]{1,0:T(8,128)S(1)}, f32[1024,512]{1,0:T(8,128)}, u32[]{:S(2)}) copy-start(f32[1024,512]{1,0:T(8,128)} %get-tuple-element.55.att) | copy-start | bytes 6291460
  193.8 16.0 %copy-start.12 = (f32[1024,512]{1,0:T(8,128)S(1)}, f32[1024,512]{1,0:T(8,128)}, u32[]{:S(2)}) copy-start(f32[1024,512]{1,0:T(8,128)} %get-tuple-element.56.lse) | copy-start | bytes 6291460
  193.8 16.0 %copy-start.14 = (bf16[1024,512]{1,0:T(8,128)(2,1)S(1)}, bf16[1024,512]{1,0:T(8,128)(2,1)}, u32[]{:S(2)}) copy-start(bf16[1024,512]{1,0:T(8,128)(2,1)} %get-tuple-element.51.q_in) | copy-start | bytes 3145732
  193.8 16.0 %copy-start.15 = (bf16[1024,512]{1,0:T(8,128)(2,1)S(1)}, bf16[1024,512]{1,0:T(8,128)(2,1)}, u32[]{:S(2)}) copy-start(bf16[1024,512]{1,0:T(8,128)(2,1)} %get-tuple-element.52.k_in) | copy-start | bytes 3145732
  193.8 16.0 %copy-start.16 = (bf16[1024,512]{1,0:T(8,128)(2,1)S(1)}, bf16[1024,512]{1,0:T(8,128)(2,1)}, u32[]{:S(2)}) copy-start(bf16[1024,512]{1,0:T(8,128)(2,1)} %get-tuple-element.53.v_in) | copy-start | bytes 3145732
  243.0 25.9 %copy-start.17 = (bf16[1024,1536]{1,0:T(8,128)(2,1)}, bf16[1024,1536]{1,0:T(8,128)(2,1)S(1)}, u32[]{:S(2)}) copy-start(bf16[1024,1536]{1,0:T(8,128)(2,1)S(1)} %heads_back.1.d_mixed) | copy-start | bytes 9437188
  268.9 0.6 copy-start.18
  559.5 4.7 copy-start
  564.3 11.4 %copy-start.19 = (f32[2,256,2048]{2,1,0:T(8,128)S(1)}, f32[2,256,2048]{2,1,0:T(8,128)}, u32[]{:S(2)}) copy-start(f32[2,256,2048]{2,1,0:T(8,128)} %get-tuple-element.61) | copy-start | bytes 12582916
  564.3 11.4 %copy-start.21 = (f32[8,1,256]{2,1,0:T(1,128)S(1)}, f32[8,1,256]{2,1,0:T(1,128)}, u32[]{:S(2)}) copy-start(f32[8,1,256]{2,1,0:T(1,128)} %get-tuple-element.78) | copy-start | bytes 24580
  574.5 1.9 copy-start.20
where the time goes:
time: 587 us; the launch traced here: 579 us
  Pallas kernels  539 us (92%)
  local copies, waits for them, and re-layouts  23.8 us (4%)
  between operations  9.16 us (2%)
  other arithmetic  7.2 us (1%)
    pallas_call x1, Pallas kernels, gradients(): pl.pallas_call(gradients_kernel, out_shape=[jax.ShapeDtypeStruct((count,...  290 us
    pallas_call x1, Pallas kernels, start(): pl.pallas_call(start_kernel, out_shape=[jax.ShapeDtypeStruct((count, rows...  83.4 us
    pallas_call x1, Pallas kernels, forward(): pl.pallas_call(forward_kernel, out_shape=out_shape, in_specs=[smem] * 2 +...  80.6 us
    pallas_call x1, Pallas kernels, heads_back(): pl.pallas_call(heads_back_kernel, grid=(heads // 2,), in_specs=[block] *...  33.2 us
    pallas_call x1, Pallas kernels, norm_back(): pl.pallas_call(norm_back_kernel, grid_spec=pltpu.PrefetchScalarGridSpec(n...  25.9 us
    pallas_call x1, Pallas kernels, feed_back(): pl.pallas_call(feed_back_kernel, grid=(length // rows,), in_specs=[by_row...  15.9 us
    unnamed x50, local copies, waits for them, and re-layouts  15.8 us

commit v1 on v0

--- a/solution.py
+++ b/solution.py
@@ -469,7 +469,7 @@
             dma((4,)),
         ],
         compiler_params=pltpu.CompilerParams(
-            collective_id=2, has_side_effects=True, vmem_limit_bytes=30 * 2**20
+            collective_id=2, has_side_effects=True, vmem_limit_bytes=60 * 2**20
         ),
         name="start",
     )(tokens, vectors, w_gate, w_up, w_qkv)
@@ -737,15 +737,17 @@
             dma((2,)),
         ],
         compiler_params=pltpu.CompilerParams(
-            collective_id=3, has_side_effects=True, vmem_limit_bytes=58 * 2**20
+            collective_id=3, has_side_effects=True, vmem_limit_bytes=60 * 2**20
         ),
         name="forward",
     )(order, slots, x_all, gain, bias, *tables, cot, w_down, w_out, w_inner, w_heads)
 
 
-def feed_back_kernel(cot, down, attn, both, inner, d_att):
-    d_att[...] = contract(cot[...], attn[...], ((1,), (1,))).astype(BF)
-    d_hidden = contract(cot[...], down[...], ((1,), (1,)))
+def feed_back_kernel(slots, *refs):
+    *cots, down, attn, both, inner, d_att = refs
+    cot = jnp.concatenate([c[0] for c in cots], axis=0)
+    d_att[...] = contract(cot, attn[...], ((1,), (1,))).astype(BF)
+    d_hidden = contract(cot, down[...], ((1,), (1,)))
     for b in range(down.shape[0] // HALF):
         d = d_hidden[:, b * HALF : (b + 1) * HALF]
         gate = both[:, b * TILE : b * TILE + HALF].astype(F32)
@@ -755,29 +757,38 @@
         inner[:, b * TILE + HALF : (b + 1) * TILE] = (d * gate * sig).astype(BF)
 
 
-def feed_back(cot, down, attn, both):
-    length, width = cot.shape
-    rows = length // 4
-    whole = lambda a: pl.BlockSpec(a.shape, lambda i: (0, 0))
-    by_rows = lambda columns: pl.BlockSpec((rows, columns), lambda i: (i, 0))
+def feed_back(slots, cot, down, attn, both):
+    count, rows, width = cot.shape
+    whole = lambda a: pl.BlockSpec(a.shape, lambda i, s: (0, 0))
+    by_rows = lambda columns: pl.BlockSpec((2 * rows, columns), lambda i, s: (i, 0))
     return pl.pallas_call(
         feed_back_kernel,
-        grid=(length // rows,),
-        in_specs=[by_rows(width), whole(down), whole(attn), by_rows(both.shape[1])],
-        out_specs=[by_rows(both.shape[1]), by_rows(attn.shape[0])],
+        grid_spec=pltpu.PrefetchScalarGridSpec(
+            num_scalar_prefetch=1,
+            grid=(count // 2,),
+            in_specs=[
+                pl.BlockSpec((1, rows, width), lambda i, s: (s[2 * i], 0, 0)),
+                pl.BlockSpec((1, rows, width), lambda i, s: (s[2 * i + 1], 0, 0)),
+                whole(down),
+                whole(attn),
+                by_rows(both.shape[1]),
+            ],
+            out_specs=[by_rows(both.shape[1]), by_rows(attn.shape[0])],
+        ),
         out_shape=[
             jax.ShapeDtypeStruct(both.shape, BF),
-            jax.ShapeDtypeStruct((length, attn.shape[0]), BF),
+            jax.ShapeDtypeStruct((count * rows, attn.shape[0]), BF),
         ],
-        compiler_params=pltpu.CompilerParams(vmem_limit_bytes=50 * 2**20),
-        cost_estimate=pl.CostEstimate(
-            flops=2 * length * width * (down.shape[0] + attn.shape[0]), bytes_accessed=2**25, transcendentals=2**20
-        ),
+        compiler_params=pltpu.CompilerParams(vmem_limit_bytes=58 * 2**20),
         name="feed_back",
-    )(cot, down, attn, both)
-
-
-def heads_back_kernel(q_in, k_in, v_in, do_in, att, lse, cos, first, second, out, dk, dv):
+    )(slots, cot, cot, down, attn, both)
+
+
+def rows_of(shard, part):
+    return slice(shard * part, (shard + 1) * part)
+
+
+def heads_back_pair(q_in, k_in, v_in, do_in, att, lse, cos, first, second, out, dk, dv):
     length = q_in.shape[0]
     scale = HD ** (-0.5)
     row = lax.broadcasted_iota(jnp.int32, (CHUNK, CHUNK), 0)
@@ -802,97 +813,38 @@
             dk[:hi, lanes] += contract(ds, q, ((0,), (0,)))
             dv[:hi, lanes] += contract(p.astype(BF), do, ((0,), (0,)))
         dq = jnp.concatenate(dqs, axis=1)
-        out[lo:hi, :HALF] = turn(dq, cos[lo:hi, :], -first[lo:hi, :], -second[lo:hi, :]).astype(BF)
-    out[:, HALF : 2 * HALF] = turn(dk[...], cos[...], -first[...], -second[...]).astype(BF)
-    out[:, 2 * HALF :] = dv[...].astype(BF)
-
-
-def heads_back(q, k, v, d_attended, attended, lse, tables):
-    length, width = q.shape
-    heads = width // HD
-    block = pl.BlockSpec((length, HALF), lambda h: (0, h))
-    table = pl.BlockSpec((length, HALF), lambda h: (0, 0))
-    return pl.pallas_call(
-        heads_back_kernel,
-        grid=(heads // 2,),
-        in_specs=[block] * 6 + [table] * 3,
-        out_specs=pl.BlockSpec((length, 3 * HALF), lambda h: (0, h)),
-        out_shape=jax.ShapeDtypeStruct((length, 3 * width), BF),
-        scratch_shapes=[pltpu.VMEM((length, HALF), F32)] * 2,
-        compiler_params=pltpu.CompilerParams(vmem_limit_bytes=40 * 2**20),
-        cost_estimate=pl.CostEstimate(
-            flops=40 * heads * length * length * HD // 2,
-            bytes_accessed=22 * length * width,
-            transcendentals=heads * length * length // 2,
-        ),
-        name="heads_back",
-    )(q, k, v, d_attended, attended, lse, *tables)
-
-
-def norm_back_kernel(slots, d_inner, inner, d_mixed, heads, hat, out, small):
-    value = contract(d_inner[...], inner[...], ((1,), (1,))) + contract(d_mixed[...], heads[...], ((1,), (1,)))
-    count, rows = out.shape[0], out.shape[1]
-    for p in range(count):
-        out[slots[p]] = value[p * rows : (p + 1) * rows].astype(BF)
-    gain = jnp.sum(value * hat[...].astype(F32), axis=0, keepdims=True)
-    bias = jnp.sum(value, axis=0, keepdims=True)
-    row = lax.broadcasted_iota(jnp.int32, small.shape, 0)
-    small[...] = jnp.where(row == 0, gain, jnp.where(row == 1, bias, 0.0)).astype(BF)
-
-
-def norm_back(slots, d_inner, inner, d_mixed, heads, hat, count):
-    length, width = hat.shape
-    whole = lambda a: pl.BlockSpec(a.shape, lambda i, s: (0, 0))
-    by_rows = lambda a: pl.BlockSpec((TILE, a.shape[1]), lambda i, s: (i, 0))
-    return pl.pallas_call(
-        norm_back_kernel,
-        grid_spec=pltpu.PrefetchScalarGridSpec(
-            num_scalar_prefetch=1,
-            grid=(width // TILE,),
-            in_specs=[
-                whole(d_inner),
-                by_rows(inner),
-                whole(d_mixed),
-                by_rows(heads),
-                pl.BlockSpec((length, TILE), lambda i, s: (0, i)),
-            ],
-            out_specs=[
-                pl.BlockSpec((count, length // count, TILE), lambda i, s: (0, 0, i)),
-                pl.BlockSpec((16, TILE), lambda i, s: (0, i)),
-            ],
-        ),
-        out_shape=[
-            jax.ShapeDtypeStruct((count, length // count, width), BF),
-            jax.ShapeDtypeStruct((16, width), BF),
-        ],
-        compiler_params=pltpu.CompilerParams(vmem_limit_bytes=50 * 2**20),
-        cost_estimate=pl.CostEstimate(
-            flops=2 * length * width * (d_inner.shape[1] + d_mixed.shape[1]), bytes_accessed=2**25, transcendentals=0
-        ),
-        name="norm_back",
-    )(slots, d_inner, inner, d_mixed, heads, hat)
-
-
-def rows_of(shard, part):
-    return slice(shard * part, (shard + 1) * part)
-
-
-def gradients_kernel(
-    hid_t, att_t, cot, norm_t, d_inner, d_mixed, small, branch, d_normed, pieces, sums,
-    partial, theirs, pair, landed, total,
-    sum_from, sum_land,
+        out[0, lo:hi, :] = turn(dq, cos[lo:hi, :], -first[lo:hi, :], -second[lo:hi, :]).astype(BF)
+    out[1] = turn(dk[...], cos[...], -first[...], -second[...]).astype(BF)
+    out[2] = dv[...].astype(BF)
+
+
+def tile_at(i, size=TILE):
+    return pl.ds(pl.multiple_of(i * size, size), size)
+
+
+def backward_kernel(
+    order, slots, hid_t, att_t, cos, first, second,
+    cot, norm_hbm, inner_hbm, branch, w_inner, w_heads, hat, q_in, k_in, v_in, do_in, att_in, lse_in,
+    pieces, sums,
+    cot_tile, norm_t, d_inner, d_mixed, terms, term, small, w_tile, h_tile, hat_tile,
+    q_tile, k_tile, v_tile, do_tile, att_tile, lse_tile, turned, dk, dv,
+    partial, theirs, pair, landed, total, sum_from, sum_land,
     core_send, core_recv, chip_send, chip_recv, line_send, line_recv, own_sem, sum_send, sum_recv,
+    cot_sem, load_sem, back_sem, head_sem,
 ):
-    count = pieces.shape[0]
-    chunks = pieces.shape[1]
+    count, chunks = pieces.shape[0], pieces.shape[1]
     shards = 2 * partial.shape[1]
     chips = shards // 2
+    rows = terms.shape[1]
     place, me = lax.axis_index("ctx"), lax.axis_index("fsdp")
     chip, core = me // 2, me % 2
     ff_part, attn_part = hid_t.shape[0] // shards, att_t.shape[0] // shards
-    cot_chunks = cot.shape[1] // TILE
-    inner_chunks = d_inner.shape[1] // TILE
-    sum_parts = branch.shape[2] // TILE
+    sum_parts = terms.shape[2] // TILE
+    early = cot.shape[2] // TILE - 1
+    inner_end = early + d_inner.shape[1] // TILE
+
+    def chunk_name(i):
+        return jnp.where(i < early, i, jnp.where(i == chunks - 1, early, i + 1))
 
     def core_copy(i):
         return pltpu.make_async_remote_copy(
@@ -904,25 +856,23 @@
             device_id_type=MESH,
         )
 
-    def chip_of(m):
-        return chip_away(chip, m)
-
     def chip_copy(j, m):
         return pltpu.make_async_remote_copy(
-            src_ref=pair.at[j % 2, chip_of(m)],
+            src_ref=pair.at[j % 2, chip_away(chip, m)],
             dst_ref=landed.at[j % DEEP, m - 1],
             send_sem=chip_send.at[j % 2, m - 1],
             recv_sem=chip_recv.at[j % DEEP, m - 1],
-            device_id=(place, 2 * chip_of(m) + core),
+            device_id=(place, 2 * chip_away(chip, m) + core),
             device_id_type=MESH,
         )
 
     def line_copy(way, hop, k):
         ahead = 1 - 2 * way
         origin = place - (hop - 1) * ahead
+        target = pieces.at[origin, chunk_name(k)]
         return pltpu.make_async_remote_copy(
-            src_ref=total.at[k % DEEP] if hop == 1 else pieces.at[origin, k],
-            dst_ref=pieces.at[origin, k],
+            src_ref=total.at[k % DEEP] if hop == 1 else target,
+            dst_ref=target,
             send_sem=line_send.at[way, hop - 1, k % DEEP],
             recv_sem=line_recv.at[way, k, hop - 1],
             device_id=(place + ahead, me),
@@ -937,26 +887,29 @@
     def lands(way, hop):
         return place >= hop if way == 0 else place <= count - 1 - hop
 
-    def forward(hop, k):
+    def forward_chunk(hop, k):
         for way in range(2):
             if hop > 1:
                 @pl.when(lands(way, hop - 1))
-                def _():
+                def _(way=way):
                     line_copy(way, hop - 1, k).wait_recv()
 
             if hop < count:
                 @pl.when(sends(way, hop))
-                def _():
+                def _(way=way):
                     @pl.when(k >= DEEP)
                     def _():
                         line_copy(way, hop, k - DEEP).wait_send()
 
                     line_copy(way, hop, k).start()
 
+    def own_copy(k):
+        return pltpu.make_async_copy(total.at[k % DEEP], pieces.at[place, chunk_name(k)], own_sem.at[k % DEEP])
+
     def sum_copy(way, t, q):
         return pltpu.make_async_remote_copy(
             src_ref=sum_from.at[way, t - 1, q % 2],
-            dst_ref=sum_land.at[way, t - 1, q],
+            dst_ref=sum_land.at[way, t - 1, q % sum_parts],
             send_sem=sum_send.at[way, t - 1, q % 2],
             recv_sem=sum_recv.at[way, t - 1, q],
             device_id=(place + 1 - 2 * way, me),
@@ -966,84 +919,95 @@
     def sum_sends(way, t):
         return place <= t - 1 if way == 0 else place >= count - t
 
-    def both_terms(q, use):
-        for which, terms in enumerate((branch, d_normed)):
-            at = (q - which * sum_parts) * TILE
-
-            @pl.when((q >= which * sum_parts) & (q < (which + 1) * sum_parts))
-            def _(which=which, terms=terms, at=at):
-                use(which, terms, pl.ds(pl.multiple_of(at, TILE), TILE))
-
     def sum_step(t, q):
+        at = tile_at(q % sum_parts)
         for way in range(2):
             @pl.when(sum_sends(way, t))
             def _(way=way):
                 to = count - t + place if way == 0 else t + place - count
-                first = place == 0 if way == 0 else place == count - 1
+                starts = place == 0 if way == 0 else place == count - 1
 
                 @pl.when(q >= 2)
                 def _():
                     sum_copy(way, t, q - 2).wait_send()
 
-                @pl.when(first)
+                @pl.when(starts)
                 def _():
-                    def use(which, terms, at):
-                        sum_from[way, t - 1, q % 2] = terms[to, :, at]
-
-                    both_terms(q, use)
+                    sum_from[way, t - 1, q % 2] = terms[to, :, at]
 
                 if t > 1:
-                    @pl.when(jnp.logical_not(first))
+                    @pl.when(jnp.logical_not(starts))
                     def _():
                         sum_copy(way, t - 1, q).wait_recv()
-
-                        def use(which, terms, at):
-                            value = terms[to, :, at].astype(F32) + sum_land[way, t - 2, q].astype(F32)
-                            sum_from[way, t - 1, q % 2] = value.astype(BF)
-
-                        both_terms(q, use)
+                        value = terms[to, :, at].astype(F32) + sum_land[way, t - 2, q % sum_parts].astype(F32)
+                        sum_from[way, t - 1, q % 2] = value.astype(BF)
 
                 sum_copy(way, t, q).start()
 
     def sum_end(q):
-        def use(which, terms, at):
-            sums[which, :, at] = terms[place, :, at].astype(F32)
-
-        both_terms(q, use)
+        at = tile_at(q % sum_parts)
+        which = q // sum_parts
+        sums[which, :, at] = terms[place, :, at].astype(F32)
         for way in range(2):
             @pl.when(place >= 1 if way == 0 else place <= count - 2)
             def _(way=way):
                 sum_copy(way, count - 1, q).wait_recv()
-
-                def use(which, terms, at):
-                    sums[which, :, at] += sum_land[way, count - 2, q].astype(F32)
-
-                both_terms(q, use)
-
-    def own_copy(k):
-        return pltpu.make_async_copy(total.at[k % DEEP], pieces.at[place, k], own_sem.at[k % DEEP])
-
-    partners = [(place, me + 1 - 2 * core)]
-    partners += [(place, 2 * chip_of(m) + core) for m in range(1, chips)]
-    partners += [((place + 1) % count, me), ((place + count - 1) % count, me)]
-    barrier = pltpu.get_barrier_semaphore()
-    for partner in partners:
-        pl.semaphore_signal(barrier, inc=1, device_id=partner, device_id_type=MESH)
-    pl.semaphore_wait(barrier, len(partners))
+                sums[which, :, at] += sum_land[way, count - 2, q % sum_parts].astype(F32)
+
+    def cot_load(c):
+        return pltpu.make_async_copy(cot.at[:, :, tile_at(c)], cot_tile.at[c % 2], cot_sem.at[c % 2])
+
+    loads = [
+        pltpu.make_async_copy(branch, terms, load_sem.at[0]),
+        pltpu.make_async_copy(norm_hbm, norm_t, load_sem.at[1]),
+        pltpu.make_async_copy(inner_hbm, d_inner, load_sem.at[2]),
+    ]
+
+    def back_loads(q):
+        moves = (
+            (w_inner.at[tile_at(q)], w_tile.at[q % 2]),
+            (w_heads.at[tile_at(q)], h_tile.at[q % 2]),
+            (hat.at[:, tile_at(q)], hat_tile.at[q % 2]),
+        )
+        return [pltpu.make_async_copy(a, b, back_sem.at[n, q % 2]) for n, (a, b) in enumerate(moves)]
+
+    def head_loads(h):
+        moves = ((q_in, q_tile), (k_in, k_tile), (v_in, v_tile), (do_in, do_tile), (att_in, att_tile), (lse_in, lse_tile))
+        at = tile_at(h, HALF)
+        return [
+            pltpu.make_async_copy(a.at[:, at], b.at[h % 2], head_sem.at[n, h % 2]) for n, (a, b) in enumerate(moves)
+        ]
+
+    pairs = q_in.shape[1] // HALF
+    for c in [loads[0], cot_load(0)] + head_loads(0) + head_loads(1) + loads[1:] + back_loads(0) + back_loads(1):
+        c.start()
+    peers = [(place, me + 1 - 2 * core)]
+    peers += [(place, 2 * chip_away(chip, m) + core) for m in range(1, chips)]
+    greet(peers + [((place + 1) % count, me), ((place + count - 1) % count, me)])
+    loads[0].wait()
+
     def store(i, shard, lo, value):
         partial[i % 2, shard // 2, shard % 2, lo : lo + value.shape[0], :] = value
 
     def from_norm(i, rhs):
         for s in range(0, shards, 2):
-            rows = norm_t.shape[0] // shards
-            value = contract(norm_t[s * rows : (s + 2) * rows, :], rhs, ((1,), (0,))).astype(BF)
-            store(i, s, 0, value[:rows])
-            store(i, s + 1, 0, value[rows:])
+            part = norm_t.shape[0] // shards
+            value = contract(norm_t[s * part : (s + 2) * part, :], rhs, ((1,), (0,))).astype(BF)
+            store(i, s, 0, value[:part])
+            store(i, s + 1, 0, value[part:])
 
     def step(i, carry):
-        @pl.when(i < cot_chunks)
+        @pl.when((i < early) | (i == chunks - 1))
         def _():
-            rhs = cot[:, pl.ds(pl.multiple_of(i * TILE, TILE), TILE)]
+            c = jnp.where(i < early, i, early)
+            cot_load(c).wait()
+
+            rhs = jnp.concatenate([cot_tile[c % 2, slots[p]] for p in range(count)], axis=0)
+
+            @pl.when(c < early)
+            def _():
+                cot_load(c + 1).start()
+
             for s in range(0, shards, 4):
                 value = contract(hid_t[s * ff_part : (s + 4) * ff_part, :], rhs, ((1,), (0,))).astype(BF)
                 for t in range(4):
@@ -1051,17 +1015,25 @@
             value = contract(att_t[...], rhs, ((1,), (0,))).astype(BF)
             for s in range(shards):
                 store(i, s, ff_part, value[rows_of(s, attn_part)])
-                store(i, s, ff_part + attn_part, small[:, s * TILE : (s + 1) * TILE])
-
-        @pl.when((i >= cot_chunks) & (i < cot_chunks + inner_chunks))
+
+        @pl.when(i == chunks - 1)
         def _():
-            at = pl.ds(pl.multiple_of((i - cot_chunks) * TILE, TILE), TILE)
-            from_norm(i, d_inner[:, at])
-
-        @pl.when((i >= cot_chunks + inner_chunks) & (i < chunks))
+            for s in range(shards):
+                store(i, s, ff_part + attn_part, small[s])
+
+        @pl.when(i == early)
         def _():
-            at = pl.multiple_of((i - cot_chunks - inner_chunks) * TILE, TILE)
-            from_norm(i, d_mixed[:, pl.ds(at, TILE)])
+            loads[1].wait()
+            loads[2].wait()
+
+        @pl.when((i >= early) & (i < inner_end))
+        def _():
+            from_norm(i, d_inner[:, tile_at(i - early)])
+
+        @pl.when((i >= inner_end) & (i < chunks - 1))
+        def _():
+            at = i - inner_end
+            from_norm(i, d_mixed[:, tile_at(at)])
 
         @pl.when(i < chunks)
         def _():
@@ -1088,7 +1060,7 @@
                 a = a + landed[k % DEEP, m - 1].astype(F32)
             for way in range(2):
                 @pl.when(sends(way, 1) & (k >= DEEP))
-                def _():
+                def _(way=way):
                     line_copy(way, 1, k - DEEP).wait_send()
 
             @pl.when(k >= DEEP)
@@ -1098,10 +1070,30 @@
             total[k % DEEP] = a.astype(BF)
             for way in range(2):
                 @pl.when(sends(way, 1))
-                def _():
+                def _(way=way):
                     line_copy(way, 1, k).start()
 
             own_copy(k).start()
+
+        @pl.when((i >= sum_parts) & (i < 2 * sum_parts))
+        def _():
+            q = i - sum_parts
+            for c in back_loads(q):
+                c.wait()
+            value = contract(d_inner[...], w_tile[q % 2], ((1,), (1,)))
+            value = value + contract(d_mixed[...], h_tile[q % 2], ((1,), (1,)))
+            term[...] = value.reshape(term.shape)
+            gain = jnp.sum(value * hat_tile[q % 2].astype(F32), axis=0, keepdims=True)
+            bias = jnp.sum(value, axis=0, keepdims=True)
+            row = lax.broadcasted_iota(jnp.int32, small.shape[1:], 0)
+            small[q] = jnp.where(row == 0, gain, jnp.where(row == 1, bias, 0.0)).astype(BF)
+            for j in range(count):
+                terms[j, :, tile_at(q)] = term[order[j]].astype(BF)
+
+            @pl.when(q + 2 < sum_parts)
+            def _():
+                for c in back_loads(q + 2):
+                    c.start()
 
         for t in range(1, count + 1):
             q = i - LAG * (t - 1)
@@ -1118,7 +1110,25 @@
 
             @pl.when((k >= 0) & (k < chunks))
             def _(k=k, hop=hop):
-                forward(hop, k)
+                forward_chunk(hop, k)
+
+        @pl.when((i == 2) | (i == 3) | (i == 5) | (i == 6))
+        def _():
+            h = i - 2 - i // 5
+            for c in head_loads(h):
+                c.wait()
+            slot = h % 2
+            heads_back_pair(
+                q_tile.at[slot], k_tile.at[slot], v_tile.at[slot], do_tile.at[slot], att_tile.at[slot],
+                lse_tile.at[slot], cos, first, second, turned, dk, dv,
+            )
+            for n in range(3):
+                d_mixed[:, tile_at(3 * h + n, HALF)] = turned[n]
+
+            @pl.when(h + 2 < pairs)
+            def _():
+                for c in head_loads(h + 2):
+                    c.start()
 
         return carry
 
@@ -1129,7 +1139,7 @@
         for way in range(2):
             for hop in range(1, count):
                 @pl.when(sends(way, hop))
-                def _():
+                def _(way=way, hop=hop):
                     line_copy(way, hop, k).wait_send()
         return carry
 
@@ -1142,29 +1152,50 @@
                     sum_copy(way, t, 2 * sum_parts - 2 + q).wait_send()
 
 
-def gradients(hid_t, att_t, cot, norm_t, d_inner, d_mixed, small, branch, d_normed, count, shards):
+def backward(
+    order, slots, hid_t, att_t, tables, cot, norm_t, d_inner, branch, w_inner, w_heads, hat, heads, shards
+):
+    count, rows, width = cot.shape
+    length = count * rows
     chips = shards // 2
-    chunks = (cot.shape[1] + d_inner.shape[1] + d_mixed.shape[1]) // TILE
-    rows = norm_t.shape[0] // shards
+    cols = heads[0].shape[1]
+    chunks = (width + d_inner.shape[1] + 3 * cols) // TILE
+    part = width // shards
+    parts = width // TILE
     dma = pltpu.SemaphoreType.DMA
-    own_rows, width = branch.shape[1:]
-    parts = 2 * width // TILE
+    smem = pl.BlockSpec(memory_space=pltpu.SMEM)
     return pl.pallas_call(
-        gradients_kernel,
+        backward_kernel,
         out_shape=[
-            jax.ShapeDtypeStruct((count, chunks, rows, TILE), BF),
-            jax.ShapeDtypeStruct((2, own_rows, width), F32),
+            jax.ShapeDtypeStruct((count, chunks, part, TILE), BF),
+            jax.ShapeDtypeStruct((2, rows, width), F32),
         ],
-        in_specs=[vmem_whole()] * 9,
+        in_specs=[smem] * 2 + [vmem_whole()] * 5 + [hbm_whole()] * 13,
         out_specs=[hbm_whole(), vmem_whole()],
         scratch_shapes=[
-            pltpu.VMEM((2, chips, 2, rows, TILE), BF),
-            pltpu.VMEM((DEEP, chips, rows, TILE), BF),
-            pltpu.VMEM((2, chips, rows, TILE), BF),
-            pltpu.VMEM((DEEP, chips - 1, rows, TILE), BF),
-            pltpu.VMEM((DEEP, rows, TILE), BF),
-            pltpu.VMEM((2, count - 1, 2, own_rows, TILE), BF),
-            pltpu.VMEM((2, count - 1, parts, own_rows, TILE), BF),
+            pltpu.VMEM((2, count, rows, TILE), BF),
+            pltpu.VMEM((width, length), BF),
+            pltpu.VMEM(d_inner.shape, BF),
+            pltpu.VMEM((length, 3 * cols), BF),
+            pltpu.VMEM((count, rows, width), BF),
+            pltpu.VMEM((count, rows, TILE), F32),
+            pltpu.VMEM((parts, 16, TILE), BF),
+            pltpu.VMEM((2, TILE, d_inner.shape[1]), BF),
+            pltpu.VMEM((2, TILE, 3 * cols), BF),
+            pltpu.VMEM((2, length, TILE), BF),
+        ]
+        + [pltpu.VMEM((2, length, HALF), BF)] * 4
+        + [pltpu.VMEM((2, length, HALF), F32)] * 2
+        + [pltpu.VMEM((3, length, HALF), BF)]
+        + [pltpu.VMEM((length, HALF), F32)] * 2
+        + [
+            pltpu.VMEM((2, chips, 2, part, TILE), BF),
+            pltpu.VMEM((DEEP, chips, part, TILE), BF),
+            pltpu.VMEM((2, chips, part, TILE), BF),
+            pltpu.VMEM((DEEP, chips - 1, part, TILE), BF),
+            pltpu.VMEM((DEEP, part, TILE), BF),
+            pltpu.VMEM((2, count - 1, 2, rows, TILE), BF),
+            pltpu.VMEM((2, count - 1, parts, rows, TILE), BF),
             dma((2,)),
             dma((DEEP,)),
             dma((2, chips - 1)),
@@ -1173,16 +1204,17 @@
             dma((2, chunks, count - 1)),
             dma((DEEP,)),
             dma((2, count - 1, 2)),
-            dma((2, count - 1, parts)),
+            dma((2, count - 1, 2 * parts)),
+            dma((2,)),
+            dma((3,)),
+            dma((3, 2)),
+            dma((6, 2)),
         ],
         compiler_params=pltpu.CompilerParams(
-            collective_id=1, has_side_effects=True, vmem_limit_bytes=60 * 2**20
+            collective_id=1, has_side_effects=True, vmem_limit_bytes=62 * 2**20
         ),
-        cost_estimate=pl.CostEstimate(
-            flops=2 * norm_t.shape[0] * norm_t.shape[1] * TILE * chunks, bytes_accessed=2**27, transcendentals=0
-        ),
-        name="gradients",
-    )(hid_t, att_t, cot, norm_t, d_inner, d_mixed, small, branch, d_normed)
+        name="backward",
+    )(order, slots, hid_t, att_t, *tables, cot, norm_t, d_inner, branch, w_inner, w_heads, hat, *heads)
 
 
 def column_runs(columns, source):
@@ -1447,14 +1479,11 @@
     ) = forward(
         order, slots, x_all, gain, bias, tables, grad_block, w_down, w_out, w_inner, w_heads, shards
     )
-    cot_all = [lax.dynamic_index_in_dim(cot_all, slots[p], 0, False) for p in range(count)]
-    cot_all = jnp.concatenate(cot_all, axis=0)
     w_hidden, w_attn = w_hidden.reshape(-1, width), w_attn.reshape(-1, width)
-    d_inner, d_attended = feed_back(cot_all, w_hidden, w_attn, both)
-    d_mixed = heads_back(q, k, v, d_attended, attended, lse, tables)
-    d_normed, small = norm_back(slots, d_inner, w_inner, d_mixed, w_heads, hat, count)
-    pieces, sums = gradients(
-        hidden_t, low_t, cot_all, normed_t, d_inner, d_mixed, small, branch, d_normed, count, shards
+    d_inner, d_attended = feed_back(slots, cot_all, w_hidden, w_attn, both)
+    pieces, sums = backward(
+        order, slots, hidden_t, low_t, tables, cot_all, normed_t, d_inner, branch, w_inner, w_heads, hat,
+        (q, k, v, d_attended, attended, lse), shards,
     )
     d_qkv, d_gate, d_up, d_down, d_attn, small = assemble_outputs(
         pieces, w_qkv.shape, w_out.shape, w_gate.shape, w_down.shape

time: 587 us -> 514 us (0.88)
  Pallas kernels: 539 us -> 488 us
  local copies, waits for them, and re-layouts: 23.8 us -> 10.4 us
  between operations: 9.16 us -> 1.23 us
    pallas_call x4 -> x2, Pallas kernels: 365 us -> 313 us  [the longest x1 295 us: backward(): pl.pallas_call(backward_kernel, out_shape=[jax.ShapeDtypeStruct((count, c...]
    unnamed x50 -> x16, local copies, waits for them, and re-layouts: 15.8 us -> 4.87 us
where the time goes in v1:
time: 514 us; the launch traced here: 505 us
  Pallas kernels  488 us (95%)
  local copies, waits for them, and re-layouts  10.4 us (2%)
  other arithmetic  5.58 us (1%)
    pallas_call x1, Pallas kernels, backward(): pl.pallas_call(backward_kernel, out_shape=[jax.ShapeDtypeStruct((count, c...  295 us
    pallas_call x1, Pallas kernels, start(): pl.pallas_call(start_kernel, out_shape=[jax.ShapeDtypeStruct((count, rows...  83.3 us
    pallas_call x1, Pallas kernels, forward(): pl.pallas_call(forward_kernel, out_shape=out_shape, in_specs=[smem] * 2 +...  81.3 us
    pallas_call x1, Pallas kernels, feed_back(): pl.pallas_call(feed_back_kernel, grid_spec=pltpu.PrefetchScalarGridSpec(n...  18.2 us
    pallas_call x1, Pallas kernels, assemble_outputs(): pl.pallas_call(functools.partial(assemble_kernel, steps), grid=(steps,),...  10.4 us

profile of v1, /device:TPU:0, one launch (start us, length us, event | category | flops | bytes accessed | tf_op | source)
XLA Modules:
  0.0 505.5 jit_solution(8507547387599923738)
XLA Ops:
  0.7 0.2 multiply_sine_fusion
  0.9 0.1 pad.5.clone
  1.0 0.1 pad.8.clone
  1.0 0.1 maximum_maximum_fusion.2
  1.2 1.0 copy.25.cos
  2.2 0.0 copy-start.6
  2.2 0.0 copy-start.7
  2.3 1.0 copy.26.first
  3.3 1.0 copy.27.second
  4.3 0.1 pad.11.clone
  4.4 0.1 pad.12.clone
  4.5 0.0 copy-done.6
  4.5 0.0 copy-done.7
  4.5 0.7 maximum_convert_fusion.vectors
  5.2 0.0 copy-start.5
  5.2 83.3 %start.1 = (bf16[4,256,2048]{2,1,0:T(8,128)(2,1)}, f32[8,8,256]{2,1,0:T(8,128)}, bf16[8,256,2816]{2,1,0:T(8,128)(2,1)}, bf16[8,256,1536]{2,1,0:T(8,128)(2,1)}) custom-call(bf16[256,2048]{1,0:T(8,128)(2,1)} %bitcast.26, f32[8,256]{1,0:T(8,128)} %maximum_convert_fusion.vectors, bf16[256,5632]{1,0:T(8,128)(2,1)} %w_gate.1, bf16[256,5632]{1,0:T(8,128)(2,1)} %w_up.1, ...), custom_call_target="tpu_custom_call" | custom-call | tf_op jit(solution)/shard_map/start/pallas_call | solution.py:446
  88.5 1.5 fusion.13
  90.0 0.0 copy-done.5
  90.1 0.6 select_reduce_fusion.slots
  90.7 81.3 %forward.1 = (bf16[4,256,2048]{2,1,0:T(8,128)(2,1)}, bf16[8,176,2048]{2,1,0:T(8,128)(2,1)}, bf16[8,64,2048]{2,1,0:T(8,128)(2,1)}, bf16[2048,1024]{1,0:T(8,128)(2...) custom-call(s32[4]{0:T(128)} %bitcast.39, ...), custom_call_target="tpu_custom_call" | custom-call | tf_op jit(solution)/shard_map/forward/pallas_call | solution.py:702
  172.0 18.2 %feed_back.1 = (bf16[1024,2816]{1,0:T(8,128)(2,1)}, bf16[1024,512]{1,0:T(8,128)(2,1)}) custom-call(s32[4]{0:T(128)} %select_reduce_fusion.slots, bf16[4,256,2048]{2,1,0:T(8,128)(2,1)} %get-tuple-element.43.refs_0_.refs_1_.cot, bf16[4,256,2048]{2,1,0:T(8,128)(2,1)} %get-tuple-element.43.refs_0_.refs_1_.cot, bf16[1408,2048]{1,0:T(8,128)(2,1)} %bitcast.29, ...), custom_call_target="tpu_custom_call" | custom-call | tf_op jit(solution)/shard_map/feed_back/pallas_call | solution.py:764
  190.2 295.1 %backward.1 = (bf16[4,25,256,256]{3,2,1,0:T(8,128)(2,1)}, f32[2,256,2048]{2,1,0:T(8,128)}) custom-call(s32[4]{0:T(128)} %bitcast.40, s32[4]{0:T(128)} %select_reduce_fusion.slots, bf16[1408,1024]{1,0:T(8,128)(2,1)} %get-tuple-element.41.hid_t, bf16[512,1024]{1,0:T(8,128)(2,1)} %get-tuple-element.42.att_t, f32[1024,128]{1,0:T(8,128)} %copy.25.cos, ...), custom_call_target="tpu_custom_call" | custom-call | tf_op jit(solution)/shard_map/backward/pallas_call | solution.py:1167
  485.3 0.0 copy-start
  485.3 4.7 copy-done
  490.0 0.0 copy-start.1
  490.0 0.0 copy-start.2
  490.0 10.4 %assemble.1 = (f32[256,6144]{1,0:T(8,128)}, f32[256,5632]{1,0:T(8,128)}, f32[256,5632]{1,0:T(8,128)}, f32[704,2048]{1,0:T(8,128)}, f32[256,2048]{1,0:T(8,128)}, /*index=5*/f32[16,256]{1,0:T(8,128)S(1)}) custom-call(bf16[4,25,256,256]{3,2,1,0:T(8,128)(2,1)S(1)} %copy-done, bf16[4,25,256,256]{3,2,1,0:T(8,128)(2,1)S(1)} %copy-done), custom_call_target="tpu_custom_call" | custom-call | tf_op jit(solution)/shard_map/assemble/pallas_call | solution.py:1295
  500.4 0.0 copy-start.4
  500.4 0.6 fusion.14
  500.9 0.0 copy-done.1
  500.9 0.2 convert_reduce_fusion
  501.2 0.0 copy-start.3
  501.2 0.4 fusion.2
  501.6 0.0 copy-done.2
  501.6 0.0 copy-done.4
  501.6 0.6 fusion.11
  502.3 0.1 copy-done.3
  502.4 2.7 fusion.10
  (16 shorter events, 0.2 us)
Async XLA Ops:
  2.2 2.3 copy-start.6
  2.2 2.3 copy-start.7
  5.2 84.9 %copy-start.5 = (s32[1,4]{1,0:T(1,128)S(1)}, s32[1,4]{1,0:T(1,128)}, u32[]{:S(2)}) copy-start(s32[1,4]{1,0:T(1,128)} %param.11) | copy-start | bytes 52
  485.3 4.7 copy-start
  490.0 10.9 %copy-start.1 = (bf16[1,256,2048]{2,1,0:T(8,128)(2,1)S(1)}, bf16[1,256,2048]{2,1,0:T(8,128)(2,1)}, u32[]{:S(2)}) copy-start(bf16[1,256,2048]{2,1,0:T(8,128)(2,1)} %param.10) | copy-start | bytes 3145732
  490.0 11.6 %copy-start.2 = (f32[2,256,2048]{2,1,0:T(8,128)S(1)}, f32[2,256,2048]{2,1,0:T(8,128)}, u32[]{:S(2)}) copy-start(f32[2,256,2048]{2,1,0:T(8,128)} %get-tuple-element.57) | copy-start | bytes 12582916
  500.4 1.3 copy-start.4
  501.2 1.2 copy-start.3

commit v2 on v1

--- a/solution.py
+++ b/solution.py
@@ -2,6 +2,7 @@
 
 import jax
 import jax.numpy as jnp
+import numpy as np
 from jax import lax
 from jax.experimental import pallas as pl
 from jax.experimental.pallas import tpu as pltpu
@@ -208,7 +209,7 @@
 TILE = 256
 HALF = 128
 DEEP = 4
-LAG = 2
+LAG = 1
 
 
 def vmem_whole():
@@ -338,6 +339,16 @@
             self.across(which, a).wait_send()
 
 
+class Own:
+    def __init__(self, source, stage, target, sem, n):
+        self.load = pltpu.make_async_copy(source, stage, sem.at[n, 0])
+        self.store = pltpu.make_async_copy(stage, target, sem.at[n, 1])
+
+    def turn(self):
+        self.load.wait()
+        self.store.start()
+
+
 def greet(peers):
     barrier = pltpu.get_barrier_semaphore()
     for peer in peers:
@@ -346,9 +357,9 @@
 
 
 def start_kernel(
-    tokens, vectors, w_gate, w_up, w_qkv, x_all, vectors_all, inner, heads,
-    raw_gate, raw_up, raw_qkv, my_inner, my_heads,
-    load_sem, line_send, line_recv, part_send, part_recv, vector_send, vector_recv, own_sem,
+    tokens, vectors, w_gate, w_up, w_qkv, w_out, x_all, vectors_all, inner, heads_own, attn,
+    raw_gate, raw_up, raw_qkv, my_inner, my_heads, tokens_stage, my_attn,
+    load_sem, line_send, line_recv, part_send, part_recv, vector_send, vector_recv, own_sem, turn_sem,
 ):
     count, shards = x_all.shape[0], inner.shape[0]
     place, me = lax.axis_index("ctx"), lax.axis_index("fsdp")
@@ -357,21 +368,26 @@
         pltpu.make_async_copy(w_up, raw_up, load_sem.at[1]),
         pltpu.make_async_copy(w_qkv, raw_qkv, load_sem.at[2]),
     ]
+    at = pl.ds(pl.multiple_of(place * attn.shape[1], 16), attn.shape[1])
+    own_attn = Own(w_out.at[at], my_attn, attn.at[me], turn_sem, 1)
+    own_attn.load.start()
     for load in loads:
         load.start()
     peers = [(place, (me + s) % shards) for s in range(1, shards)]
     greet(peers + [((place + 1) % count, me), ((place + count - 1) % count, me)])
     line = Line(tokens, x_all, line_send, line_recv)
-    plane = Plane((my_inner, my_heads), (inner, heads), part_send, part_recv)
+    plane = Plane((my_inner, my_attn), (inner, attn), part_send, part_recv)
     line.pass_on(1)
+    own_attn.turn()
+    plane.begin(1)
     own_copies = [
         pltpu.make_async_copy(my_inner, inner.at[me], own_sem.at[0]),
-        pltpu.make_async_copy(my_heads, heads.at[me], own_sem.at[1]),
+        pltpu.make_async_copy(my_heads, heads_own, own_sem.at[1]),
         pltpu.make_async_copy(vectors, vectors_all.at[me], own_sem.at[2]),
-        pltpu.make_async_copy(tokens, x_all.at[place], own_sem.at[3]),
     ]
     own_copies[2].start()
-    own_copies[3].start()
+    own_tokens = Own(tokens, tokens_stage, x_all.at[place], turn_sem, 0)
+    own_tokens.load.start()
     vector_copies = [
         pltpu.make_async_remote_copy(
             src_ref=vectors,
@@ -397,6 +413,7 @@
         at = pl.ds(pl.multiple_of(base, HALF), TILE)
         return [contract(raw[:, at], choose, ((1,), (0,))) for raw in raws]
 
+    own_tokens.turn()
     part = raw_gate.shape[1] // shards // count
     loads[0].wait()
     loads[1].wait()
@@ -421,24 +438,23 @@
                 value = value + picked((raw_qkv,), h * HD, (h + 1) * HD, start)[0]
             at = (pair * 3 + kind) * HALF
             my_heads[:, at : at + HALF] = value.astype(BF)
-    plane.begin(1)
     own_copies[1].start()
+    plane.relay(1)
     line.pass_on(2)
     plane.relay(0)
+    plane.last(1)
     line.pass_on(3)
-    plane.relay(1)
+    plane.last(0)
+    for which in range(2):
+        plane.finish(which)
     for hop in range(4, count + 1):
         line.pass_on(hop)
-    for which in range(2):
-        plane.last(which)
-    for which in range(2):
-        plane.finish(which)
-    for c in vector_copies + own_copies:
+    for c in vector_copies + own_copies + [own_tokens.store, own_attn.store]:
         c.wait()
     line.finish()
 
 
-def start(tokens, vectors, w_gate, w_up, w_qkv, count, shards):
+def start(tokens, vectors, w_gate, w_up, w_qkv, w_out, count, shards):
     rows, width = tokens.shape
     shard_rows, ff = w_gate.shape
     inner, heads = 2 * ff // count, 3 * width // count
@@ -449,16 +465,19 @@
             jax.ShapeDtypeStruct((count, rows, width), BF),
             jax.ShapeDtypeStruct((shards,) + vectors.shape, F32),
             jax.ShapeDtypeStruct((shards, shard_rows, inner), BF),
-            jax.ShapeDtypeStruct((shards, shard_rows, heads), BF),
+            jax.ShapeDtypeStruct((shard_rows, heads), BF),
+            jax.ShapeDtypeStruct((shards, w_out.shape[0] // count, width), BF),
         ],
-        in_specs=[hbm_whole()] * 5,
-        out_specs=[hbm_whole()] * 4,
+        in_specs=[hbm_whole()] * 6,
+        out_specs=[hbm_whole()] * 5,
         scratch_shapes=[
             pltpu.VMEM(w_gate.shape, BF),
             pltpu.VMEM(w_up.shape, BF),
             pltpu.VMEM(w_qkv.shape, BF),
             pltpu.VMEM((shard_rows, inner), BF),
             pltpu.VMEM((shard_rows, heads), BF),
+            pltpu.VMEM(tokens.shape, BF),
+            pltpu.VMEM((w_out.shape[0] // count, width), BF),
             dma((3,)),
             dma((2, count - 1)),
             dma((2, count - 1)),
@@ -466,20 +485,21 @@
             dma((2, 8)),
             dma((shards - 1,)),
             dma((shards - 1,)),
-            dma((4,)),
+            dma((3,)),
+            dma((2, 2)),
         ],
         compiler_params=pltpu.CompilerParams(
             collective_id=2, has_side_effects=True, vmem_limit_bytes=60 * 2**20
         ),
         name="start",
-    )(tokens, vectors, w_gate, w_up, w_qkv)
+    )(tokens, vectors, w_gate, w_up, w_qkv, w_out)
 
 
 def forward_kernel(
-    order, slots, x_all, gain, bias, cos, first, second, cot, w_down, w_out, w_inner, w_heads,
-    cot_all, down, attn, normed_t, hat, both, hidden_t, q_out, k_out, v_out, att_out, low_t, lse_out, branch,
+    order, slots, x_all, gain, bias, cos, first, second, cot, w_down, attn, w_inner, heads_own,
+    cot_all, heads_all, down, normed_t, hat, both, hidden_t, q_out, k_out, v_out, att_out, low_t, lse_out, branch,
     inner, heads, normed, hidden, low, hat_stage, turned_stage, both_stage, hidden_stage,
-    q_buf, k_buf, v_buf, att_buf, low_stage, lse_buf, down_tile, attn_tile, term, branch_stage,
+    q_buf, k_buf, v_buf, att_buf, low_stage, lse_buf, down_tile, attn_tile, term, branch_stage, down_stage, cot_stage, heads_stage,
     load_sem, line_send, line_recv, part_send, part_recv, own_sem, norm_sem, feed_sem, head_sem, tile_sem, branch_sem,
 ):
     count, rows = cot_all.shape[0], cot_all.shape[1]
@@ -488,26 +508,27 @@
     chip, core = me // 2, me % 2
     loads = [
         pltpu.make_async_copy(w_inner, inner, load_sem.at[0]),
-        pltpu.make_async_copy(w_heads, heads, load_sem.at[1]),
     ]
-    for load in loads:
-        load.start()
+    part = heads_all.shape[1]
+    loads += [
+        pltpu.make_async_copy(heads_all.at[s], heads.at[s * part : (s + 1) * part], load_sem.at[1 + s])
+        for s in range(shards)
+    ]
+    loads[0].start()
     peers = [(place, 2 * chip + 1 - core)] + [(place, 2 * chip_away(chip, m) + core) for m in range(1, 3)]
     greet(peers + [((place + 1) % count, me), ((place + count - 1) % count, me)])
     my_down = w_down.at[pl.ds(pl.multiple_of(place * down.shape[1], 16), down.shape[1])]
-    my_attn = w_out.at[pl.ds(pl.multiple_of(place * attn.shape[1], 16), attn.shape[1])]
     line = Line(cot, cot_all, line_send, line_recv)
-    plane = Plane((my_down, my_attn), (down, attn), part_send, part_recv)
+    plane = Plane((heads_own, my_down), (heads_all, down), part_send, part_recv)
     line.pass_on(1)
-    for which in range(2):
-        plane.begin(which)
-    own_copies = [
-        pltpu.make_async_copy(my_down, down.at[me], own_sem.at[0]),
-        pltpu.make_async_copy(my_attn, attn.at[me], own_sem.at[1]),
-        pltpu.make_async_copy(cot, cot_all.at[place], own_sem.at[2]),
+    plane.begin(0)
+    owns = [
+        Own(heads_own, heads_stage, heads_all.at[me], own_sem, 0),
+        Own(cot, cot_stage, cot_all.at[place], own_sem, 1),
+        Own(my_down, down_stage, down.at[me], own_sem, 2),
     ]
-    for c in own_copies:
-        c.start()
+    for own in owns:
+        own.load.start()
 
     def norm_copies(p):
         at = pl.ds(pl.multiple_of(p * rows, rows), rows)
@@ -536,6 +557,8 @@
         return carry
 
     lax.fori_loop(0, count, norm_step, 0)
+    for own in owns:
+        own.turn()
     loads[0].wait()
 
     def feed_copies(i):
@@ -563,11 +586,18 @@
         return carry
 
     tiles = inner.shape[1] // TILE
-    lax.fori_loop(0, tiles, feed_step, 0)
+    lax.fori_loop(0, tiles // 2, feed_step, 0)
+    plane.relay(0)
+    plane.begin(1)
+    lax.fori_loop(tiles // 2, tiles, feed_step, 0)
     line.pass_on(2)
-    for which in range(2):
-        plane.relay(which)
-    loads[1].wait()
+    plane.last(0)
+    plane.finish(0)
+    owns[0].store.wait()
+    for load in loads[1:]:
+        load.start()
+    for load in loads[1:]:
+        load.wait()
     row = lax.broadcasted_iota(jnp.int32, (CHUNK, CHUNK), 0)
     col = lax.broadcasted_iota(jnp.int32, (CHUNK, CHUNK), 1)
     pairs = heads.shape[1] // (3 * HALF)
@@ -587,9 +617,8 @@
                 c.wait()
 
         slot = h % 2
-        mixed = contract(
-            normed[...], heads[:, pl.ds(pl.multiple_of(h * 3 * HALF, HALF), 3 * HALF)], ((1,), (0,))
-        )
+        w = heads[:, pl.ds(pl.multiple_of(h * 3 * HALF, HALF), 3 * HALF)]
+        mixed = contract(normed[...], w, ((1,), (0,)))
         q = turn(mixed[:, :HALF], cos[...], first[...], second[...]).astype(BF).astype(F32)
         q_buf[slot] = (q * HD ** (-0.5)).astype(BF)
         k_buf[slot] = turn(mixed[:, HALF : 2 * HALF], cos[...], first[...], second[...]).astype(BF)
@@ -616,15 +645,14 @@
             c.start()
         return carry
 
-    lax.fori_loop(0, pairs // 2, head_step, 0)
-    for which in range(2):
-        plane.last(which)
+    lax.fori_loop(0, pairs - 1, head_step, 0)
+    plane.relay(1)
     line.pass_on(3)
-    lax.fori_loop(pairs // 2, pairs, head_step, 0)
-    for which in range(2):
-        plane.finish(which)
-    for c in own_copies:
-        c.wait()
+    lax.fori_loop(pairs - 1, pairs, head_step, 0)
+    plane.last(1)
+    plane.finish(1)
+    for own in owns[1:]:
+        own.store.wait()
 
     def tile_copies(i):
         at = pl.ds(pl.multiple_of(i * TILE, TILE), TILE)
@@ -674,10 +702,10 @@
         branch_copy(steps - 1 - back).wait()
 
 
-def forward(order, slots, x_all, gain, bias, tables, cot, w_down, w_out, w_inner, w_heads, shards):
+def forward(order, slots, x_all, gain, bias, tables, cot, w_down, attn, w_inner, heads_own, shards):
     count, rows, width = x_all.shape
     length = count * rows
-    ff_part, attn_part = w_down.shape[0] // count, w_out.shape[0] // count
+    ff_part, attn_part = w_down.shape[0] // count, attn.shape[1]
     ff, cols = shards * ff_part, shards * attn_part
     dma = pltpu.SemaphoreType.DMA
     smem = pl.BlockSpec(memory_space=pltpu.SMEM)
@@ -685,8 +713,8 @@
     f32 = lambda *shape: jax.ShapeDtypeStruct(shape, F32)
     out_shape = [
         bf(count, rows, width),
+        bf(shards, *heads_own.shape),
         bf(shards, ff_part, width),
-        bf(shards, attn_part, width),
         bf(width, length),
         bf(length, width),
         bf(length, 2 * ff),
@@ -706,7 +734,7 @@
         out_specs=[hbm_whole()] * len(out_shape),
         scratch_shapes=[
             pltpu.VMEM(w_inner.shape, BF),
-            pltpu.VMEM(w_heads.shape, BF),
+            pltpu.VMEM((width, heads_own.shape[1]), BF),
             pltpu.VMEM((length, width), BF),
             pltpu.VMEM((length, ff), BF),
             pltpu.VMEM((length, cols), BF),
@@ -724,12 +752,15 @@
             pltpu.VMEM((2, shards, attn_part, TILE), BF),
             pltpu.VMEM((count, rows, TILE), F32),
             pltpu.VMEM((2, count, rows, TILE), BF),
-            dma((2,)),
+            pltpu.VMEM((ff_part, width), BF),
+            pltpu.VMEM((rows, width), BF),
+            pltpu.VMEM(heads_own.shape, BF),
+            dma((1 + shards,)),
             dma((2, count - 1)),
             dma((2, count - 1)),
             dma((2, 8)),
             dma((2, 8)),
-            dma((3,)),
+            dma((3, 2)),
             dma((2, 2)),
             dma((2, 2)),
             dma((6, 2)),
@@ -740,48 +771,17 @@
             collective_id=3, has_side_effects=True, vmem_limit_bytes=60 * 2**20
         ),
         name="forward",
-    )(order, slots, x_all, gain, bias, *tables, cot, w_down, w_out, w_inner, w_heads)
-
-
-def feed_back_kernel(slots, *refs):
-    *cots, down, attn, both, inner, d_att = refs
-    cot = jnp.concatenate([c[0] for c in cots], axis=0)
-    d_att[...] = contract(cot, attn[...], ((1,), (1,))).astype(BF)
-    d_hidden = contract(cot, down[...], ((1,), (1,)))
-    for b in range(down.shape[0] // HALF):
-        d = d_hidden[:, b * HALF : (b + 1) * HALF]
-        gate = both[:, b * TILE : b * TILE + HALF].astype(F32)
-        up = both[:, b * TILE + HALF : (b + 1) * TILE].astype(F32)
-        sig = jax.nn.sigmoid(gate)
-        inner[:, b * TILE : b * TILE + HALF] = (d * up * sig * (1.0 + gate * (1.0 - sig))).astype(BF)
-        inner[:, b * TILE + HALF : (b + 1) * TILE] = (d * gate * sig).astype(BF)
-
-
-def feed_back(slots, cot, down, attn, both):
-    count, rows, width = cot.shape
-    whole = lambda a: pl.BlockSpec(a.shape, lambda i, s: (0, 0))
-    by_rows = lambda columns: pl.BlockSpec((2 * rows, columns), lambda i, s: (i, 0))
-    return pl.pallas_call(
-        feed_back_kernel,
-        grid_spec=pltpu.PrefetchScalarGridSpec(
-            num_scalar_prefetch=1,
-            grid=(count // 2,),
-            in_specs=[
-                pl.BlockSpec((1, rows, width), lambda i, s: (s[2 * i], 0, 0)),
-                pl.BlockSpec((1, rows, width), lambda i, s: (s[2 * i + 1], 0, 0)),
-                whole(down),
-                whole(attn),
-                by_rows(both.shape[1]),
-            ],
-            out_specs=[by_rows(both.shape[1]), by_rows(attn.shape[0])],
-        ),
-        out_shape=[
-            jax.ShapeDtypeStruct(both.shape, BF),
-            jax.ShapeDtypeStruct((count * rows, attn.shape[0]), BF),
-        ],
-        compiler_params=pltpu.CompilerParams(vmem_limit_bytes=58 * 2**20),
-        name="feed_back",
-    )(slots, cot, cot, down, attn, both)
+    )(order, slots, x_all, gain, bias, *tables, cot, w_down, attn, w_inner, heads_own)
+
+
+def fixed_tables(length):
+    half = ROT // 2
+    inverse = np.float32(10000.0) ** (-np.arange(half, dtype=np.float32) / np.float32(half))
+    grid = np.arange(length, dtype=np.float32)[:, None] * inverse.astype(np.float32)[None, :]
+    cos, sin = np.cos(grid, dtype=np.float32), np.sin(grid, dtype=np.float32)
+    zero, rest = np.zeros((length, half), np.float32), np.zeros((length, HD - ROT), np.float32)
+    tables = ([cos, cos, rest + 1], [-sin, zero, rest], [zero, sin, rest])
+    return [jnp.asarray(np.tile(np.concatenate(t, axis=1), (1, 2))) for t in tables]
 
 
 def rows_of(shard, part):
@@ -824,13 +824,13 @@
 
 def backward_kernel(
     order, slots, hid_t, att_t, cos, first, second,
-    cot, norm_hbm, inner_hbm, branch, w_inner, w_heads, hat, q_in, k_in, v_in, do_in, att_in, lse_in,
+    cot, norm_hbm, down, attn, both, branch, w_inner, w_heads, hat, q_in, k_in, v_in, att_in, lse_in,
     pieces, sums,
-    cot_tile, norm_t, d_inner, d_mixed, terms, term, small, w_tile, h_tile, hat_tile,
-    q_tile, k_tile, v_tile, do_tile, att_tile, lse_tile, turned, dk, dv,
+    cot_own, norm_t, d_inner, d_mixed, terms, term, small, w_tile, h_tile, hat_tile,
+    attn_tile, q_tile, k_tile, v_tile, att_tile, lse_tile, d_att, turned, dk, dv, sums_stage,
     partial, theirs, pair, landed, total, sum_from, sum_land,
     core_send, core_recv, chip_send, chip_recv, line_send, line_recv, own_sem, sum_send, sum_recv,
-    cot_sem, load_sem, back_sem, head_sem,
+    cot_sem, load_sem, feed_sem, back_sem, head_sem, sums_sem,
 ):
     count, chunks = pieces.shape[0], pieces.shape[1]
     shards = 2 * partial.shape[1]
@@ -840,11 +840,11 @@
     chip, core = me // 2, me % 2
     ff_part, attn_part = hid_t.shape[0] // shards, att_t.shape[0] // shards
     sum_parts = terms.shape[2] // TILE
-    early = cot.shape[2] // TILE - 1
+    early = cot_own.shape[1] // TILE - 1
     inner_end = early + d_inner.shape[1] // TILE
 
     def chunk_name(i):
-        return jnp.where(i < early, i, jnp.where(i == chunks - 1, early, i + 1))
+        return jnp.where(i < early, i + chunks - 1 - early, jnp.where(i == chunks - 1, i, i - early))
 
     def core_copy(i):
         return pltpu.make_async_remote_copy(
@@ -944,23 +944,38 @@
 
                 sum_copy(way, t, q).start()
 
+    def sums_copy(q):
+        return pltpu.make_async_copy(
+            sums_stage.at[q % 2], sums.at[q // sum_parts, :, tile_at(q % sum_parts)], sums_sem.at[q % 2]
+        )
+
     def sum_end(q):
-        at = tile_at(q % sum_parts)
-        which = q // sum_parts
-        sums[which, :, at] = terms[place, :, at].astype(F32)
+        @pl.when(q >= 2)
+        def _():
+            sums_copy(q - 2).wait()
+
+        sums_stage[q % 2] = terms[place, :, tile_at(q % sum_parts)].astype(F32)
         for way in range(2):
             @pl.when(place >= 1 if way == 0 else place <= count - 2)
             def _(way=way):
                 sum_copy(way, count - 1, q).wait_recv()
-                sums[which, :, at] += sum_land[way, count - 2, q % sum_parts].astype(F32)
-
-    def cot_load(c):
-        return pltpu.make_async_copy(cot.at[:, :, tile_at(c)], cot_tile.at[c % 2], cot_sem.at[c % 2])
+                sums_stage[q % 2] += sum_land[way, count - 2, q % sum_parts].astype(F32)
+
+        sums_copy(q).start()
+
+    cot_load = pltpu.make_async_copy(cot, terms, cot_sem)
+
+    def feed_load(b, size):
+        at = pl.ds(pl.multiple_of(b * TILE, TILE), size)
+        return pltpu.make_async_copy(
+            down.at[at], w_tile.at[b % 2, :size, : cot_own.shape[1]], feed_sem.at[b % 2]
+        )
+
+    both_load = pltpu.make_async_copy(both, d_inner, load_sem.at[2])
 
     loads = [
         pltpu.make_async_copy(branch, terms, load_sem.at[0]),
         pltpu.make_async_copy(norm_hbm, norm_t, load_sem.at[1]),
-        pltpu.make_async_copy(inner_hbm, d_inner, load_sem.at[2]),
     ]
 
     def back_loads(q):
@@ -972,19 +987,58 @@
         return [pltpu.make_async_copy(a, b, back_sem.at[n, q % 2]) for n, (a, b) in enumerate(moves)]
 
     def head_loads(h):
-        moves = ((q_in, q_tile), (k_in, k_tile), (v_in, v_tile), (do_in, do_tile), (att_in, att_tile), (lse_in, lse_tile))
+        moves = ((q_in, q_tile), (k_in, k_tile), (v_in, v_tile), (att_in, att_tile), (lse_in, lse_tile))
         at = tile_at(h, HALF)
-        return [
+        copies = [
             pltpu.make_async_copy(a.at[:, at], b.at[h % 2], head_sem.at[n, h % 2]) for n, (a, b) in enumerate(moves)
         ]
+        return copies
+
+    def attn_load(h):
+        return pltpu.make_async_copy(attn.at[tile_at(h // 2)], attn_tile, load_sem.at[3])
 
     pairs = q_in.shape[1] // HALF
-    for c in [loads[0], cot_load(0)] + head_loads(0) + head_loads(1) + loads[1:] + back_loads(0) + back_loads(1):
+    tiles = d_inner.shape[1] // TILE
+    for c in [cot_load, both_load, feed_load(0, TILE), feed_load(1, TILE), attn_load(0)] + head_loads(0) + head_loads(1) + loads[1:]:
         c.start()
     peers = [(place, me + 1 - 2 * core)]
     peers += [(place, 2 * chip_away(chip, m) + core) for m in range(1, chips)]
     greet(peers + [((place + 1) % count, me), ((place + count - 1) % count, me)])
+    cot_load.wait()
+    for p in range(count):
+        cot_own[p * rows : (p + 1) * rows, :] = terms[slots[p]]
+    loads[0].start()
     loads[0].wait()
+
+    ff = down.shape[0]
+    whole_tiles = ff // TILE
+
+    def feed_tile(b, size):
+        feed_load(b, size).wait()
+        d_hidden = contract(cot_own[...], w_tile[b % 2, :size, : cot_own.shape[1]], ((1,), (1,)))
+        for n in range(size // HALF):
+            d = d_hidden[:, n * HALF : (n + 1) * HALF]
+            at = tile_at(2 * b + n)
+            value = d_inner[:, at]
+            gate = value[:, :HALF].astype(F32)
+            up = value[:, HALF:].astype(F32)
+            sig = jax.nn.sigmoid(gate)
+            d_gate = d * up * sig * (1.0 + gate * (1.0 - sig))
+            d_inner[:, at] = jnp.concatenate([d_gate, d * gate * sig], axis=1).astype(BF)
+
+    def feed_step(b, carry):
+        feed_tile(b, TILE)
+
+        @pl.when(b + 2 < whole_tiles)
+        def _():
+            feed_load(b + 2, TILE).start()
+
+        if ff % TILE:
+            @pl.when(b + 2 == whole_tiles)
+            def _():
+                feed_load(whole_tiles, ff % TILE).start()
+
+        return carry
 
     def store(i, shard, lo, value):
         partial[i % 2, shard // 2, shard % 2, lo : lo + value.shape[0], :] = value
@@ -1000,14 +1054,7 @@
         @pl.when((i < early) | (i == chunks - 1))
         def _():
             c = jnp.where(i < early, i, early)
-            cot_load(c).wait()
-
-            rhs = jnp.concatenate([cot_tile[c % 2, slots[p]] for p in range(count)], axis=0)
-
-            @pl.when(c < early)
-            def _():
-                cot_load(c + 1).start()
-
+            rhs = cot_own[:, tile_at(c)]
             for s in range(0, shards, 4):
                 value = contract(hid_t[s * ff_part : (s + 4) * ff_part, :], rhs, ((1,), (0,))).astype(BF)
                 for t in range(4):
@@ -1024,7 +1071,6 @@
         @pl.when(i == early)
         def _():
             loads[1].wait()
-            loads[2].wait()
 
         @pl.when((i >= early) & (i < inner_end))
         def _():
@@ -1112,14 +1158,46 @@
             def _(k=k, hop=hop):
                 forward_chunk(hop, k)
 
+        @pl.when(i == 0)
+        def _():
+            both_load.wait()
+
+        @pl.when((i == 0) | (i == 1) | (i == 4))
+        def _():
+            first_tile = jnp.where(i == 0, 0, jnp.where(i == 1, 1, 3))
+            last_tile = jnp.where(i == 0, 1, jnp.where(i == 1, 3, whole_tiles))
+            lax.fori_loop(first_tile, last_tile, feed_step, 0)
+
+        if ff % TILE:
+            @pl.when(i == 4)
+            def _():
+                feed_tile(whole_tiles, ff % TILE)
+
+        @pl.when(i == 5)
+        def _():
+            for c in back_loads(0) + back_loads(1):
+                c.start()
+
         @pl.when((i == 2) | (i == 3) | (i == 5) | (i == 6))
         def _():
             h = i - 2 - i // 5
             for c in head_loads(h):
                 c.wait()
             slot = h % 2
+
+            @pl.when(slot == 0)
+            def _():
+                attn_load(h).wait()
+                value = contract(cot_own[...], attn_tile[...], ((1,), (1,)))
+                for n in range(2):
+                    d_att[n] = value[:, n * HALF : (n + 1) * HALF].astype(BF)
+
+                @pl.when(h + 2 < pairs)
+                def _():
+                    attn_load(h + 2).start()
+
             heads_back_pair(
-                q_tile.at[slot], k_tile.at[slot], v_tile.at[slot], do_tile.at[slot], att_tile.at[slot],
+                q_tile.at[slot], k_tile.at[slot], v_tile.at[slot], d_att.at[slot], att_tile.at[slot],
                 lse_tile.at[slot], cos, first, second, turned, dk, dv,
             )
             for n in range(3):
@@ -1144,6 +1222,8 @@
         return carry
 
     lax.fori_loop(chunks - DEEP, chunks, drain, 0)
+    for q in range(2):
+        sums_copy(2 * sum_parts - 2 + q).wait()
     for way in range(2):
         for t in range(1, count):
             @pl.when(sum_sends(way, t))
@@ -1153,13 +1233,14 @@
 
 
 def backward(
-    order, slots, hid_t, att_t, tables, cot, norm_t, d_inner, branch, w_inner, w_heads, hat, heads, shards
+    order, slots, hid_t, att_t, tables, cot, norm_t, down, attn, both, branch, w_inner, w_heads, hat, heads, shards
 ):
     count, rows, width = cot.shape
     length = count * rows
     chips = shards // 2
     cols = heads[0].shape[1]
-    chunks = (width + d_inner.shape[1] + 3 * cols) // TILE
+    inner = both.shape[1]
+    chunks = (width + inner + 3 * cols) // TILE
     part = width // shards
     parts = width // TILE
     dma = pltpu.SemaphoreType.DMA
@@ -1170,24 +1251,27 @@
             jax.ShapeDtypeStruct((count, chunks, part, TILE), BF),
             jax.ShapeDtypeStruct((2, rows, width), F32),
         ],
-        in_specs=[smem] * 2 + [vmem_whole()] * 5 + [hbm_whole()] * 13,
-        out_specs=[hbm_whole(), vmem_whole()],
+        in_specs=[smem] * 2 + [vmem_whole()] * 5 + [hbm_whole()] * 14,
+        out_specs=[hbm_whole()] * 2,
         scratch_shapes=[
-            pltpu.VMEM((2, count, rows, TILE), BF),
+            pltpu.VMEM((length, width), BF),
             pltpu.VMEM((width, length), BF),
-            pltpu.VMEM(d_inner.shape, BF),
+            pltpu.VMEM((length, inner), BF),
             pltpu.VMEM((length, 3 * cols), BF),
             pltpu.VMEM((count, rows, width), BF),
             pltpu.VMEM((count, rows, TILE), F32),
             pltpu.VMEM((parts, 16, TILE), BF),
-            pltpu.VMEM((2, TILE, d_inner.shape[1]), BF),
+            pltpu.VMEM((2, TILE, inner), BF),
             pltpu.VMEM((2, TILE, 3 * cols), BF),
             pltpu.VMEM((2, length, TILE), BF),
         ]
-        + [pltpu.VMEM((2, length, HALF), BF)] * 4
+        + [pltpu.VMEM((TILE, width), BF)]
+        + [pltpu.VMEM((2, length, HALF), BF)] * 3
         + [pltpu.VMEM((2, length, HALF), F32)] * 2
+        + [pltpu.VMEM((2, length, HALF), BF)]
         + [pltpu.VMEM((3, length, HALF), BF)]
         + [pltpu.VMEM((length, HALF), F32)] * 2
+        + [pltpu.VMEM((2, rows, TILE), F32)]
         + [
             pltpu.VMEM((2, chips, 2, part, TILE), BF),
             pltpu.VMEM((DEEP, chips, part, TILE), BF),
@@ -1205,16 +1289,18 @@
             dma((DEEP,)),
             dma((2, count - 1, 2)),
             dma((2, count - 1, 2 * parts)),
+            pltpu.SemaphoreType.DMA,
+            dma((4,)),
             dma((2,)),
-            dma((3,)),
             dma((3, 2)),
-            dma((6, 2)),
+            dma((5, 2)),
+            dma((2,)),
         ],
         compiler_params=pltpu.CompilerParams(
             collective_id=1, has_side_effects=True, vmem_limit_bytes=62 * 2**20
         ),
         name="backward",
-    )(order, slots, hid_t, att_t, *tables, cot, norm_t, d_inner, branch, w_inner, w_heads, hat, *heads)
+    )(order, slots, hid_t, att_t, *tables, cot, norm_t, down, attn, both, branch, w_inner, w_heads, hat, *heads)
 
 
 def column_runs(columns, source):
@@ -1231,9 +1317,8 @@
     return out
 
 
-def assemble_kernel(down_chunks, rows_in, cols_in, qkv_out, gate_out, up_out, down_out, attn_out, small_out):
+def assemble_kernel(rows_in, cols_in, sums, tokens, cot, gain, out, grad, qkv_out, gate_out, up_out, down_out, attn_out, small_out):
     count, chunks, rows, _ = rows_in.shape
-    cot_chunks_static = down_chunks
     ff = gate_out.shape[1]
     width = qkv_out.shape[1]
     ff_part = down_out.shape[0] // count
@@ -1241,6 +1326,14 @@
     shards = ff // (count * ff_part)
     inner_chunks = ff // count // HALF
     lane = lax.broadcasted_iota(jnp.int32, (rows, HALF), 1)
+    own = tokens[...].astype(F32)
+    out[...] = (own + sums[0]).astype(BF)
+    own = own - jnp.mean(own, axis=1, keepdims=True)
+    inv_std = lax.rsqrt(jnp.mean(own * own, axis=1, keepdims=True) + EPS)
+    own = own * inv_std
+    scaled = sums[1] * gain[...]
+    scaled = scaled - jnp.mean(scaled, axis=1, keepdims=True) - own * jnp.mean(scaled * own, axis=1, keepdims=True)
+    grad[...] = cot[...].astype(F32) + inv_std * scaled
 
     def gather(out, runs, load):
         for block, first, last, key, shift in runs:
@@ -1268,9 +1361,9 @@
         return (place, 3 * pair + part), half * HD + dim
 
     runs = column_runs(ff, inner_source)
-    gather(gate_out, runs, lambda key: rows_in[key[0], cot_chunks_static + key[1], :, :HALF])
-    gather(up_out, runs, lambda key: rows_in[key[0], cot_chunks_static + key[1], :, HALF:])
-    first_head = cot_chunks_static + inner_chunks
+    gather(gate_out, runs, lambda key: rows_in[key[0], key[1], :, :HALF])
+    gather(up_out, runs, lambda key: rows_in[key[0], key[1], :, HALF:])
+    first_head = inner_chunks
 
     def head_load(key):
         at = key[1] % 2 * HALF
@@ -1286,25 +1379,32 @@
     small_out[...] = functools.reduce(jnp.add, small)
 
 
-def assemble_outputs(pieces, qkv, attn, gate, down):
+def assemble_outputs(pieces, sums, tokens, cot, gain, qkv, attn, gate, down):
     count, chunks, rows, _ = pieces.shape
     steps = down[1] // TILE
     part = rows // steps
+    width = tokens.shape[1]
     by_rows = lambda shape: pl.BlockSpec((part, shape[1]), lambda i: (i, 0))
     by_cols = lambda shape: pl.BlockSpec((shape[0], TILE), lambda i: (0, i))
     return pl.pallas_call(
-        functools.partial(assemble_kernel, steps),
+        assemble_kernel,
         grid=(steps,),
         in_specs=[
-            pl.BlockSpec((count, chunks, part, TILE), lambda i: (0, 0, i, 0)),
-            pl.BlockSpec((count, 1, rows, TILE), lambda i: (0, i, 0, 0)),
+            pl.BlockSpec((count, chunks - steps, part, TILE), lambda i: (0, 0, i, 0)),
+            pl.BlockSpec((count, 1, rows, TILE), lambda i: (0, chunks - steps + i, 0, 0)),
+            pl.BlockSpec((2, part, width), lambda i: (0, i, 0)),
+            by_rows(tokens.shape),
+            by_rows(tokens.shape),
+            pl.BlockSpec((1, width), lambda i: (0, 0)),
         ],
-        out_specs=[by_rows(qkv), by_rows(gate), by_rows(gate), by_cols(down), by_cols(attn)]
+        out_specs=[by_rows(tokens.shape)] * 2
+        + [by_rows(qkv), by_rows(gate), by_rows(gate), by_cols(down), by_cols(attn)]
         + [pl.BlockSpec((16, TILE), lambda i: (0, 0))],
-        out_shape=[jax.ShapeDtypeStruct(s, F32) for s in (qkv, gate, gate, down, attn, (16, TILE))],
-        compiler_params=pltpu.CompilerParams(vmem_limit_bytes=40 * 2**20),
+        out_shape=[jax.ShapeDtypeStruct(tokens.shape, BF), jax.ShapeDtypeStruct(tokens.shape, F32)]
+        + [jax.ShapeDtypeStruct(s, F32) for s in (qkv, gate, gate, down, attn, (16, TILE))],
+        compiler_params=pltpu.CompilerParams(vmem_limit_bytes=60 * 2**20),
         name="assemble",
-    )(pieces, pieces)
+    )(pieces, pieces, sums, tokens, cot, gain)
 
 
 def rotation_tables(length):
@@ -1468,38 +1568,28 @@
     spots = jnp.arange(count, dtype=jnp.int32)
     slots = jnp.sum(jnp.where(order[None, :] == spots[:, None], spots[None, :], 0), axis=1)
     vectors = jnp.stack([ln_gain, ln_bias] + [jnp.zeros_like(ln_gain)] * 6).astype(F32)
-    x_all, vectors, w_inner, w_heads = start(block, vectors, w_gate, w_up, w_qkv, count, shards)
+    x_all, vectors, w_inner, heads_own, w_attn = start(
+        block, vectors, w_gate, w_up, w_qkv, w_out, count, shards
+    )
     w_inner = w_inner.reshape(width, -1)
-    w_heads = w_heads.reshape(width, -1)
     gain, bias = vectors[:, 0].reshape(1, width), vectors[:, 1].reshape(1, width)
-    tables = rotation_tables(rows * count)
+    tables = fixed_tables(rows * count)
 
     (
-        cot_all, w_hidden, w_attn, normed_t, hat, both, hidden_t, q, k, v, attended, low_t, lse, branch,
+        cot_all, w_heads, w_hidden, normed_t, hat, both, hidden_t, q, k, v, attended, low_t, lse, branch,
     ) = forward(
-        order, slots, x_all, gain, bias, tables, grad_block, w_down, w_out, w_inner, w_heads, shards
+        order, slots, x_all, gain, bias, tables, grad_block, w_down, w_attn, w_inner, heads_own, shards
     )
     w_hidden, w_attn = w_hidden.reshape(-1, width), w_attn.reshape(-1, width)
-    d_inner, d_attended = feed_back(slots, cot_all, w_hidden, w_attn, both)
+    w_heads = w_heads.reshape(width, -1)
     pieces, sums = backward(
-        order, slots, hidden_t, low_t, tables, cot_all, normed_t, d_inner, branch, w_inner, w_heads, hat,
-        (q, k, v, d_attended, attended, lse), shards,
+        order, slots, hidden_t, low_t, tables, cot_all, normed_t, w_hidden, w_attn, both, branch, w_inner,
+        w_heads, hat, (q, k, v, attended, lse), shards,
     )
-    d_qkv, d_gate, d_up, d_down, d_attn, small = assemble_outputs(
-        pieces, w_qkv.shape, w_out.shape, w_gate.shape, w_down.shape
+    out, grad_in, d_qkv, d_gate, d_up, d_down, d_attn, small = assemble_outputs(
+        pieces, sums, block, grad_block, gain, w_qkv.shape, w_out.shape, w_gate.shape, w_down.shape
     )
-    own = block.astype(F32)
-    out = (own + sums[0]).astype(BF)[None]
-    own = own - jnp.mean(own, axis=-1, keepdims=True)
-    own_std = lax.rsqrt(jnp.mean(own * own, axis=-1, keepdims=True) + EPS)
-    own = own * own_std
-    scaled = sums[1] * gain
-    d_input = own_std * (
-        scaled
-        - jnp.mean(scaled, axis=-1, keepdims=True)
-        - own * jnp.mean(scaled * own, axis=-1, keepdims=True)
-    )
-    grad_in = (grad_block.astype(F32) + d_input)[None]
+    out, grad_in = out[None], grad_in[None]
     return out, grad_in, small[0], small[1], d_qkv, d_attn, d_gate, d_up, d_down
 
 

time: 514 us -> 480 us (0.934); the launches traced: 505 us -> 479 us
  Pallas kernels: 488 us -> 472 us
  local copies, waits for them, and re-layouts: 10.4 us -> 4.35 us
    pallas_call x2 -> x1, Pallas kernels: 28.5 us -> 18 us  [assemble_outputs(): pl.pallas_call(assemble_kernel, grid=(steps,), in_specs=[pl.BlockSpec((co...]
where the time goes in v2:
time: 480 us; the launch traced here: 479 us
  Pallas kernels  472 us (98%)
    pallas_call x1, Pallas kernels, backward(): pl.pallas_call(backward_kernel, out_shape=[jax.ShapeDtypeStruct((count, c...  293 us
    pallas_call x1, Pallas kernels, forward(): pl.pallas_call(forward_kernel, out_shape=out_shape, in_specs=[smem] * 2 +...  81.9 us
    pallas_call x1, Pallas kernels, start(): pl.pallas_call(start_kernel, out_shape=[jax.ShapeDtypeStruct((count, rows...  79 us
    pallas_call x1, Pallas kernels, assemble_outputs(): pl.pallas_call(assemble_kernel, grid=(steps,), in_specs=[pl.BlockSpec((co...  18 us

profile of v2, /device:TPU:0, one launch (start us, length us, event | category | flops | bytes accessed | tf_op | source)
XLA Modules:
  0.0 479.4 jit_solution(14553243810123135186)
XLA Ops:
  0.6 1.3 select_reduce_fusion.slots
  1.9 0.1 pad.3.clone
  2.0 0.1 pad.2.clone
  2.1 0.7 stack.15
  2.7 0.7 stack.16
  3.4 0.7 maximum_convert_fusion.vectors
  4.1 79.0 %start.1 = (bf16[4,256,2048]{2,1,0:T(8,128)(2,1)}, f32[8,8,256]{2,1,0:T(8,128)}, bf16[8,256,2816]{2,1,0:T(8,128)(2,1)}, bf16[256,1536]{1,0:T(8,128)(2,1)}, bf16[8,64,2048]{2,1,0:T(8,128)(2,1)}) custom-call(bf16[256,2048]{1,0:T(8,128)(2,1)} %bitcast.18, f32[8,256]{1,0:T(8,128)} %maximum_convert_fusion.vectors, bf16[256,5632]{1,0:T(8,128)(2,1)} %w_gate.1, ...), custom_call_target="tpu_custom_call" | custom-call | tf_op jit(solution)/shard_map/start/pallas_call | solution.py:462
  83.1 1.5 fusion
  84.6 81.9 %forward.1 = (bf16[4,256,2048]{2,1,0:T(8,128)(2,1)}, bf16[8,256,1536]{2,1,0:T(8,128)(2,1)}, bf16[8,176,2048]{2,1,0:T(8,128)(2,1)}, bf16[2048,1024]{1,0:T(8,128)(...) custom-call(s32[4]{0:T(128)} %bitcast.26, ...), custom_call_target="tpu_custom_call" | custom-call | tf_op jit(solution)/shard_map/forward/pallas_call | solution.py:730
  166.5 293.5 %backward.1 = (bf16[4,25,256,256]{3,2,1,0:T(8,128)(2,1)}, f32[2,256,2048]{2,1,0:T(8,128)}) custom-call(s32[4]{0:T(128)} %bitcast.27, s32[4]{0:T(128)} %select_reduce_fusion.slots, bf16[1408,1024]{1,0:T(8,128)(2,1)} %get-tuple-element.43.hid_t, bf16[512,1024]{1,0:T(8,128)(2,1)} %get-tuple-element.44.att_t, f32[1024,128]{1,0:T(8,128)} %constant.4.clone.cos, ...), custom_call_target="tpu_custom_call" | custom-call | tf_op jit(solution)/shard_map/backward/pallas_call | solution.py:1248
  460.0 18.0 %assemble.1 = (bf16[256,2048]{1,0:T(8,128)(2,1)}, f32[256,2048]{1,0:T(8,128)}, f32[256,6144]{1,0:T(8,128)}, f32[256,5632]{1,0:T(8,128)}, f32[256,5632]{1,0:T(8,1...) custom-call(bf16[4,25,256,256]{3,2,1,0:T(8,128)(2,1)} %get-tuple-element.57.rows_in.cols_in, ...), custom_call_target="tpu_custom_call" | custom-call | tf_op jit(solution)/shard_map/assemble/pallas_call | solution.py:1389
  478.1 1.3 fusion.1
  (2 shorter events, 0.0 us)

commit v3 on v2

--- a/solution.py
+++ b/solution.py
@@ -212,6 +212,10 @@
 LAG = 1
 
 
+def tile_at(i, size=TILE):
+    return pl.ds(pl.multiple_of(i * size, size), size)
+
+
 def vmem_whole():
     return pl.BlockSpec(memory_space=pltpu.VMEM)
 
@@ -356,38 +360,44 @@
     pl.semaphore_wait(barrier, len(peers))
 
 
-def start_kernel(
-    tokens, vectors, w_gate, w_up, w_qkv, w_out, x_all, vectors_all, inner, heads_own, attn,
-    raw_gate, raw_up, raw_qkv, my_inner, my_heads, tokens_stage, my_attn,
-    load_sem, line_send, line_recv, part_send, part_recv, vector_send, vector_recv, own_sem, turn_sem,
+def forward_kernel(
+    order, slots, cos, first, second, tokens, cot, vectors, w_gate, w_up, w_qkv, w_out, w_down,
+    cot_all, rows_out, inner_out, heads_out, attn_out, down, normed_t, hat, both, hidden_t,
+    q_out, k_out, v_out, att_out, low_t, lse_out, branch,
+    raw, x_all, vectors_all, scales, inner, heads, attn,
+    normed, hidden, low, hat_stage, turned_stage, both_stage, hidden_stage,
+    q_buf, k_buf, v_buf, att_buf, low_stage, lse_buf, down_tile, term, branch_stage,
+    load_sem, x_send, x_recv, line_send, line_recv, part_send, part_recv, vector_send, vector_recv,
+    own_sem, out_sem, norm_sem, feed_sem, head_sem, tile_sem, branch_sem,
 ):
-    count, shards = x_all.shape[0], inner.shape[0]
+    count, rows = x_all.shape[0], x_all.shape[1]
+    shards = inner.shape[0]
     place, me = lax.axis_index("ctx"), lax.axis_index("fsdp")
+    width = w_gate.shape[1]
+    my_attn = w_out.at[pl.ds(pl.multiple_of(place * attn.shape[1], 16), attn.shape[1])]
+    my_down = w_down.at[pl.ds(pl.multiple_of(place * down.shape[1], 16), down.shape[1])]
     loads = [
-        pltpu.make_async_copy(w_gate, raw_gate, load_sem.at[0]),
-        pltpu.make_async_copy(w_up, raw_up, load_sem.at[1]),
-        pltpu.make_async_copy(w_qkv, raw_qkv, load_sem.at[2]),
+        pltpu.make_async_copy(my_attn, attn.at[me], load_sem.at[0]),
+        pltpu.make_async_copy(w_gate, raw.at[0, :, :width], load_sem.at[1]),
+        pltpu.make_async_copy(w_up, raw.at[1, :, :width], load_sem.at[2]),
+        pltpu.make_async_copy(tokens, x_all.at[place], load_sem.at[3]),
+        pltpu.make_async_copy(vectors, vectors_all.at[me], load_sem.at[4]),
     ]
-    at = pl.ds(pl.multiple_of(place * attn.shape[1], 16), attn.shape[1])
-    own_attn = Own(w_out.at[at], my_attn, attn.at[me], turn_sem, 1)
-    own_attn.load.start()
-    for load in loads:
-        load.start()
+    owns = [
+        Own(cot, hat_stage.at[0], cot_all.at[place], own_sem, 0),
+        Own(my_down, hat_stage.at[1, : down.shape[1]], down.at[me], own_sem, 1),
+    ]
+    for c in loads + [own.load for own in owns]:
+        c.start()
+    qkv_load = pltpu.make_async_copy(w_qkv, raw.at[0], load_sem.at[5])
     peers = [(place, (me + s) % shards) for s in range(1, shards)]
     greet(peers + [((place + 1) % count, me), ((place + count - 1) % count, me)])
-    line = Line(tokens, x_all, line_send, line_recv)
-    plane = Plane((my_inner, my_attn), (inner, attn), part_send, part_recv)
-    line.pass_on(1)
-    own_attn.turn()
-    plane.begin(1)
-    own_copies = [
-        pltpu.make_async_copy(my_inner, inner.at[me], own_sem.at[0]),
-        pltpu.make_async_copy(my_heads, heads_own, own_sem.at[1]),
-        pltpu.make_async_copy(vectors, vectors_all.at[me], own_sem.at[2]),
-    ]
-    own_copies[2].start()
-    own_tokens = Own(tokens, tokens_stage, x_all.at[place], turn_sem, 0)
-    own_tokens.load.start()
+    x_line = Line(tokens, x_all, x_send, x_recv)
+    line = Line(cot, cot_all, line_send, line_recv)
+    plane = Plane(
+        (inner.at[me], attn.at[me], heads.at[me], my_down), (inner, attn, heads, down), part_send, part_recv
+    )
+    x_line.pass_on(1)
     vector_copies = [
         pltpu.make_async_remote_copy(
             src_ref=vectors,
@@ -401,134 +411,68 @@
     ]
     for c in vector_copies:
         c.start()
+    loads[0].wait()
+    plane.begin(1)
 
     row = lax.broadcasted_iota(jnp.int32, (TILE, HALF), 0)
     col = lax.broadcasted_iota(jnp.int32, (TILE, HALF), 1)
 
-    def picked(raws, first, last, start):
-        width = raws[0].shape[1]
-        base = jnp.minimum((start + first) // HALF, width // HALF - TILE // HALF) * HALF
+    def picked(sources, size, first, last, start):
+        base = jnp.minimum((start + first) // HALF, size // HALF - TILE // HALF) * HALF
         choose = (row + base == col + start) & (col >= first) & (col < last)
         choose = choose.astype(F32).astype(BF)
         at = pl.ds(pl.multiple_of(base, HALF), TILE)
-        return [contract(raw[:, at], choose, ((1,), (0,))) for raw in raws]
-
-    own_tokens.turn()
-    part = raw_gate.shape[1] // shards // count
-    loads[0].wait()
+        return [contract(raw[source, :, at], choose, ((1,), (0,))) for source in sources]
+
+    part = width // shards // count
     loads[1].wait()
+    loads[2].wait()
     held = None
-    for block, first, last, start in inner_runs(shards, count, part):
-        values = picked((raw_gate, raw_up), first, last, start + place * part)
-        held = values if first == 0 else [a + b for a, b in zip(held, values)]
-        if last == HALF:
+    for block, first_col, last_col, start in inner_runs(shards, count, part):
+        values = picked((0, 1), width, first_col, last_col, start + place * part)
+        held = values if first_col == 0 else [a + b for a, b in zip(held, values)]
+        if last_col == HALF:
             for k in range(2):
                 at = block * TILE + k * HALF
-                my_inner[:, at : at + HALF] = held[k].astype(BF)
+                inner[me, :, at : at + HALF] = held[k].astype(BF)
     plane.begin(0)
-    own_copies[0].start()
-    loads[2].wait()
-    width = raw_qkv.shape[1] // 3
+    qkv_load.start()
+    qkv_load.wait()
+    third = raw.shape[2] // 3
     for pair in range(shards // 2):
         for kind in range(3):
             value = 0.0
             for h in range(2):
                 head = count * (2 * pair + h) + place
-                start = kind * width + head * HD - h * HD
-                value = value + picked((raw_qkv,), h * HD, (h + 1) * HD, start)[0]
+                start = kind * third + head * HD - h * HD
+                value = value + picked((0,), raw.shape[2], h * HD, (h + 1) * HD, start)[0]
             at = (pair * 3 + kind) * HALF
-            my_heads[:, at : at + HALF] = value.astype(BF)
-    own_copies[1].start()
+            heads[me, :, at : at + HALF] = value.astype(BF)
+    plane.begin(2)
+    for own in owns:
+        own.turn()
     plane.relay(1)
-    line.pass_on(2)
+    x_line.pass_on(2)
     plane.relay(0)
     plane.last(1)
-    line.pass_on(3)
+    x_line.pass_on(3)
+    line.pass_on(1)
+    plane.relay(2)
     plane.last(0)
-    for which in range(2):
-        plane.finish(which)
-    for hop in range(4, count + 1):
-        line.pass_on(hop)
-    for c in vector_copies + own_copies + [own_tokens.store, own_attn.store]:
+    plane.finish(1)
+    for c in loads[3:] + vector_copies:
         c.wait()
-    line.finish()
-
-
-def start(tokens, vectors, w_gate, w_up, w_qkv, w_out, count, shards):
-    rows, width = tokens.shape
-    shard_rows, ff = w_gate.shape
-    inner, heads = 2 * ff // count, 3 * width // count
-    dma = pltpu.SemaphoreType.DMA
-    return pl.pallas_call(
-        start_kernel,
-        out_shape=[
-            jax.ShapeDtypeStruct((count, rows, width), BF),
-            jax.ShapeDtypeStruct((shards,) + vectors.shape, F32),
-            jax.ShapeDtypeStruct((shards, shard_rows, inner), BF),
-            jax.ShapeDtypeStruct((shard_rows, heads), BF),
-            jax.ShapeDtypeStruct((shards, w_out.shape[0] // count, width), BF),
-        ],
-        in_specs=[hbm_whole()] * 6,
-        out_specs=[hbm_whole()] * 5,
-        scratch_shapes=[
-            pltpu.VMEM(w_gate.shape, BF),
-            pltpu.VMEM(w_up.shape, BF),
-            pltpu.VMEM(w_qkv.shape, BF),
-            pltpu.VMEM((shard_rows, inner), BF),
-            pltpu.VMEM((shard_rows, heads), BF),
-            pltpu.VMEM(tokens.shape, BF),
-            pltpu.VMEM((w_out.shape[0] // count, width), BF),
-            dma((3,)),
-            dma((2, count - 1)),
-            dma((2, count - 1)),
-            dma((2, 8)),
-            dma((2, 8)),
-            dma((shards - 1,)),
-            dma((shards - 1,)),
-            dma((3,)),
-            dma((2, 2)),
-        ],
-        compiler_params=pltpu.CompilerParams(
-            collective_id=2, has_side_effects=True, vmem_limit_bytes=60 * 2**20
-        ),
-        name="start",
-    )(tokens, vectors, w_gate, w_up, w_qkv, w_out)
-
-
-def forward_kernel(
-    order, slots, x_all, gain, bias, cos, first, second, cot, w_down, attn, w_inner, heads_own,
-    cot_all, heads_all, down, normed_t, hat, both, hidden_t, q_out, k_out, v_out, att_out, low_t, lse_out, branch,
-    inner, heads, normed, hidden, low, hat_stage, turned_stage, both_stage, hidden_stage,
-    q_buf, k_buf, v_buf, att_buf, low_stage, lse_buf, down_tile, attn_tile, term, branch_stage, down_stage, cot_stage, heads_stage,
-    load_sem, line_send, line_recv, part_send, part_recv, own_sem, norm_sem, feed_sem, head_sem, tile_sem, branch_sem,
-):
-    count, rows = cot_all.shape[0], cot_all.shape[1]
-    shards = down.shape[0]
-    place, me = lax.axis_index("ctx"), lax.axis_index("fsdp")
-    chip, core = me // 2, me % 2
-    loads = [
-        pltpu.make_async_copy(w_inner, inner, load_sem.at[0]),
+    scales[...] = jnp.concatenate([vectors_all[s] for s in range(shards)], axis=1)
+    x_line.pass_on(4)
+    plane.begin(3)
+    outs = [
+        pltpu.make_async_copy(attn, attn_out, out_sem.at[0]),
+        pltpu.make_async_copy(scales, rows_out, out_sem.at[1]),
+        pltpu.make_async_copy(inner, inner_out, out_sem.at[2]),
+        pltpu.make_async_copy(heads, heads_out, out_sem.at[3]),
     ]
-    part = heads_all.shape[1]
-    loads += [
-        pltpu.make_async_copy(heads_all.at[s], heads.at[s * part : (s + 1) * part], load_sem.at[1 + s])
-        for s in range(shards)
-    ]
-    loads[0].start()
-    peers = [(place, 2 * chip + 1 - core)] + [(place, 2 * chip_away(chip, m) + core) for m in range(1, 3)]
-    greet(peers + [((place + 1) % count, me), ((place + count - 1) % count, me)])
-    my_down = w_down.at[pl.ds(pl.multiple_of(place * down.shape[1], 16), down.shape[1])]
-    line = Line(cot, cot_all, line_send, line_recv)
-    plane = Plane((heads_own, my_down), (heads_all, down), part_send, part_recv)
-    line.pass_on(1)
-    plane.begin(0)
-    owns = [
-        Own(heads_own, heads_stage, heads_all.at[me], own_sem, 0),
-        Own(cot, cot_stage, cot_all.at[place], own_sem, 1),
-        Own(my_down, down_stage, down.at[me], own_sem, 2),
-    ]
-    for own in owns:
-        own.load.start()
+    outs[0].start()
+    outs[1].start()
 
     def norm_copies(p):
         at = pl.ds(pl.multiple_of(p * rows, rows), rows)
@@ -549,17 +493,19 @@
         variance = jnp.mean(centered * centered, axis=1, keepdims=True)
         x_hat = centered * lax.rsqrt(variance + EPS)
         hat_stage[p % 2] = x_hat.astype(BF)
-        value = x_hat * gain[...] + bias[...]
+        value = x_hat * scales[0:1, :] + scales[1:2, :]
         normed[pl.ds(pl.multiple_of(p * rows, rows), rows), :] = value.astype(BF)
         turned_stage[p % 2] = value.T.astype(BF)
         for c in norm_copies(p):
             c.start()
         return carry
 
+    for own in owns:
+        own.store.wait()
     lax.fori_loop(0, count, norm_step, 0)
-    for own in owns:
-        own.turn()
-    loads[0].wait()
+    plane.finish(0)
+    outs[2].start()
+    model = normed.shape[1]
 
     def feed_copies(i):
         wide = pl.ds(pl.multiple_of(i * TILE, TILE), TILE)
@@ -575,7 +521,7 @@
             for c in feed_copies(i - 2):
                 c.wait()
 
-        value = contract(normed[...], inner[:, pl.ds(pl.multiple_of(i * TILE, TILE), TILE)], ((1,), (0,)))
+        value = contract(normed[...], inner[:, :, tile_at(i)].reshape(model, TILE), ((1,), (0,)))
         both_stage[i % 2] = value.astype(BF)
         gate, up = value[:, :HALF], value[:, HALF:]
         value = gate * jax.nn.sigmoid(gate) * up
@@ -585,22 +531,16 @@
             c.start()
         return carry
 
-    tiles = inner.shape[1] // TILE
-    lax.fori_loop(0, tiles // 2, feed_step, 0)
-    plane.relay(0)
-    plane.begin(1)
-    lax.fori_loop(tiles // 2, tiles, feed_step, 0)
+    tiles = inner.shape[2] // TILE
+    lax.fori_loop(0, tiles, feed_step, 0)
     line.pass_on(2)
-    plane.last(0)
-    plane.finish(0)
-    owns[0].store.wait()
-    for load in loads[1:]:
-        load.start()
-    for load in loads[1:]:
-        load.wait()
+    plane.relay(3)
+    plane.last(2)
+    plane.finish(2)
+    outs[3].start()
     row = lax.broadcasted_iota(jnp.int32, (CHUNK, CHUNK), 0)
     col = lax.broadcasted_iota(jnp.int32, (CHUNK, CHUNK), 1)
-    pairs = heads.shape[1] // (3 * HALF)
+    pairs = heads.shape[2] // (3 * HALF)
 
     def head_copies(h):
         at = pl.ds(pl.multiple_of(h * HALF, HALF), HALF)
@@ -617,7 +557,7 @@
                 c.wait()
 
         slot = h % 2
-        w = heads[:, pl.ds(pl.multiple_of(h * 3 * HALF, HALF), 3 * HALF)]
+        w = heads[:, :, tile_at(h, 3 * HALF)].reshape(model, 3 * HALF)
         mixed = contract(normed[...], w, ((1,), (0,)))
         q = turn(mixed[:, :HALF], cos[...], first[...], second[...]).astype(BF).astype(F32)
         q_buf[slot] = (q * HD ** (-0.5)).astype(BF)
@@ -646,20 +586,13 @@
         return carry
 
     lax.fori_loop(0, pairs - 1, head_step, 0)
-    plane.relay(1)
+    plane.last(3)
     line.pass_on(3)
     lax.fori_loop(pairs - 1, pairs, head_step, 0)
-    plane.last(1)
-    plane.finish(1)
-    for own in owns[1:]:
-        own.store.wait()
-
+    plane.finish(3)
     def tile_copies(i):
         at = pl.ds(pl.multiple_of(i * TILE, TILE), TILE)
-        return (
-            pltpu.make_async_copy(down.at[:, :, at], down_tile.at[i % 2], tile_sem.at[0, i % 2]),
-            pltpu.make_async_copy(attn.at[:, :, at], attn_tile.at[i % 2], tile_sem.at[1, i % 2]),
-        )
+        return [pltpu.make_async_copy(down.at[:, :, at], down_tile.at[i % 2], tile_sem.at[i % 2])]
 
     def branch_copy(i):
         at = pl.ds(pl.multiple_of(i * TILE, TILE), TILE)
@@ -683,7 +616,7 @@
             branch_copy(i - 2).wait()
 
         value = contract(hidden[...], down_tile[i % 2].reshape(hidden.shape[1], TILE), ((1,), (0,)))
-        value = value + contract(low[...], attn_tile[i % 2].reshape(low.shape[1], TILE), ((1,), (0,)))
+        value = value + contract(low[...], attn[:, :, tile_at(i)].reshape(low.shape[1], TILE), ((1,), (0,)))
         term[...] = value.reshape(term.shape)
         for j in range(count):
             branch_stage[i % 2, j] = term[order[j]].astype(BF)
@@ -694,6 +627,9 @@
     for hop in range(4, count + 1):
         line.pass_on(hop)
     line.finish()
+    x_line.finish()
+    for c in outs:
+        c.wait()
     for back in range(2):
         for c in norm_copies(count - 1 - back) + feed_copies(tiles - 1 - back):
             c.wait()
@@ -702,10 +638,11 @@
         branch_copy(steps - 1 - back).wait()
 
 
-def forward(order, slots, x_all, gain, bias, tables, cot, w_down, attn, w_inner, heads_own, shards):
-    count, rows, width = x_all.shape
+def forward(order, slots, tables, tokens, cot, vectors, w_gate, w_up, w_qkv, w_out, w_down, count, shards):
+    rows, width = tokens.shape
     length = count * rows
-    ff_part, attn_part = w_down.shape[0] // count, attn.shape[1]
+    shard_rows = w_gate.shape[0]
+    ff_part, attn_part = w_down.shape[0] // count, w_out.shape[0] // count
     ff, cols = shards * ff_part, shards * attn_part
     dma = pltpu.SemaphoreType.DMA
     smem = pl.BlockSpec(memory_space=pltpu.SMEM)
@@ -713,7 +650,10 @@
     f32 = lambda *shape: jax.ShapeDtypeStruct(shape, F32)
     out_shape = [
         bf(count, rows, width),
-        bf(shards, *heads_own.shape),
+        f32(vectors.shape[0], width),
+        bf(shards, shard_rows, 2 * ff),
+        bf(shards, shard_rows, 3 * cols),
+        bf(shards, attn_part, width),
         bf(shards, ff_part, width),
         bf(width, length),
         bf(length, width),
@@ -727,14 +667,20 @@
         f32(length, cols),
         bf(count, rows, width),
     ]
+    hops = (2, count - 1)
     return pl.pallas_call(
         forward_kernel,
         out_shape=out_shape,
-        in_specs=[smem] * 2 + [vmem_whole()] * 6 + [hbm_whole()] * 5,
+        in_specs=[smem] * 2 + [vmem_whole()] * 3 + [hbm_whole()] * 8,
         out_specs=[hbm_whole()] * len(out_shape),
         scratch_shapes=[
-            pltpu.VMEM(w_inner.shape, BF),
-            pltpu.VMEM((width, heads_own.shape[1]), BF),
+            pltpu.VMEM((2,) + w_qkv.shape, BF),
+            pltpu.VMEM((count, rows, width), BF),
+            pltpu.VMEM((shards,) + vectors.shape, F32),
+            pltpu.VMEM((vectors.shape[0], width), F32),
+            pltpu.VMEM((shards, shard_rows, 2 * ff), BF),
+            pltpu.VMEM((shards, shard_rows, 3 * cols), BF),
+            pltpu.VMEM((shards, attn_part, width), BF),
             pltpu.VMEM((length, width), BF),
             pltpu.VMEM((length, ff), BF),
             pltpu.VMEM((length, cols), BF),
@@ -749,29 +695,30 @@
             pltpu.VMEM((2, HALF, length), BF),
             pltpu.VMEM((2, length, HALF), F32),
             pltpu.VMEM((2, shards, ff_part, TILE), BF),
-            pltpu.VMEM((2, shards, attn_part, TILE), BF),
             pltpu.VMEM((count, rows, TILE), F32),
             pltpu.VMEM((2, count, rows, TILE), BF),
-            pltpu.VMEM((ff_part, width), BF),
-            pltpu.VMEM((rows, width), BF),
-            pltpu.VMEM(heads_own.shape, BF),
-            dma((1 + shards,)),
-            dma((2, count - 1)),
-            dma((2, count - 1)),
-            dma((2, 8)),
-            dma((2, 8)),
-            dma((3, 2)),
+            dma((6,)),
+            dma(hops),
+            dma(hops),
+            dma(hops),
+            dma(hops),
+            dma((4, 8)),
+            dma((4, 8)),
+            dma((shards - 1,)),
+            dma((shards - 1,)),
+            dma((2, 2)),
+            dma((4,)),
             dma((2, 2)),
             dma((2, 2)),
             dma((6, 2)),
-            dma((2, 2)),
+            dma((2,)),
             dma((2,)),
         ],
         compiler_params=pltpu.CompilerParams(
-            collective_id=3, has_side_effects=True, vmem_limit_bytes=60 * 2**20
+            collective_id=3, has_side_effects=True, vmem_limit_bytes=62 * 2**20
         ),
         name="forward",
-    )(order, slots, x_all, gain, bias, *tables, cot, w_down, attn, w_inner, heads_own)
+    )(order, slots, *tables, tokens, cot, vectors, w_gate, w_up, w_qkv, w_out, w_down)
 
 
 def fixed_tables(length):
@@ -818,10 +765,6 @@
     out[2] = dv[...].astype(BF)
 
 
-def tile_at(i, size=TILE):
-    return pl.ds(pl.multiple_of(i * size, size), size)
-
-
 def backward_kernel(
     order, slots, hid_t, att_t, cos, first, second,
     cot, norm_hbm, down, attn, both, branch, w_inner, w_heads, hat, q_in, k_in, v_in, att_in, lse_in,
@@ -908,9 +851,9 @@
 
     def sum_copy(way, t, q):
         return pltpu.make_async_remote_copy(
-            src_ref=sum_from.at[way, t - 1, q % 2],
+            src_ref=sum_from.at[way, t - 1, q // sum_parts],
             dst_ref=sum_land.at[way, t - 1, q % sum_parts],
-            send_sem=sum_send.at[way, t - 1, q % 2],
+            send_sem=sum_send.at[way, t - 1, q // sum_parts],
             recv_sem=sum_recv.at[way, t - 1, q],
             device_id=(place + 1 - 2 * way, me),
             device_id_type=MESH,
@@ -927,39 +870,41 @@
                 to = count - t + place if way == 0 else t + place - count
                 starts = place == 0 if way == 0 else place == count - 1
 
-                @pl.when(q >= 2)
+                @pl.when(q % sum_parts >= 1)
                 def _():
-                    sum_copy(way, t, q - 2).wait_send()
+                    sum_copy(way, t, q - 1).wait_send()
 
                 @pl.when(starts)
                 def _():
-                    sum_from[way, t - 1, q % 2] = terms[to, :, at]
+                    sum_from[way, t - 1, q // sum_parts] = terms[to, :, at]
 
                 if t > 1:
                     @pl.when(jnp.logical_not(starts))
                     def _():
                         sum_copy(way, t - 1, q).wait_recv()
                         value = terms[to, :, at].astype(F32) + sum_land[way, t - 2, q % sum_parts].astype(F32)
-                        sum_from[way, t - 1, q % 2] = value.astype(BF)
+                        sum_from[way, t - 1, q // sum_parts] = value.astype(BF)
 
                 sum_copy(way, t, q).start()
 
     def sums_copy(q):
         return pltpu.make_async_copy(
-            sums_stage.at[q % 2], sums.at[q // sum_parts, :, tile_at(q % sum_parts)], sums_sem.at[q % 2]
+            sums_stage.at[q // sum_parts],
+            sums.at[q // sum_parts, :, tile_at(q % sum_parts)],
+            sums_sem.at[q // sum_parts],
         )
 
     def sum_end(q):
-        @pl.when(q >= 2)
-        def _():
-            sums_copy(q - 2).wait()
-
-        sums_stage[q % 2] = terms[place, :, tile_at(q % sum_parts)].astype(F32)
+        @pl.when(q % sum_parts >= 1)
+        def _():
+            sums_copy(q - 1).wait()
+
+        sums_stage[q // sum_parts] = terms[place, :, tile_at(q % sum_parts)].astype(F32)
         for way in range(2):
             @pl.when(place >= 1 if way == 0 else place <= count - 2)
             def _(way=way):
                 sum_copy(way, count - 1, q).wait_recv()
-                sums_stage[q % 2] += sum_land[way, count - 2, q % sum_parts].astype(F32)
+                sums_stage[q // sum_parts] += sum_land[way, count - 2, q % sum_parts].astype(F32)
 
         sums_copy(q).start()
 
@@ -1121,9 +1066,9 @@
 
             own_copy(k).start()
 
-        @pl.when((i >= sum_parts) & (i < 2 * sum_parts))
-        def _():
-            q = i - sum_parts
+        @pl.when((i >= 9) & (i < 9 + 2 * sum_parts) & (i % 2 == 1))
+        def _():
+            q = (i - 9) // 2
             for c in back_loads(q):
                 c.wait()
             value = contract(d_inner[...], w_tile[q % 2], ((1,), (1,)))
@@ -1142,9 +1087,11 @@
                     c.start()
 
         for t in range(1, count + 1):
-            q = i - LAG * (t - 1)
-
-            @pl.when((q >= 0) & (q < 2 * sum_parts))
+            when = i - LAG * (t - 1)
+            q = jnp.where(when % 2 == 0, when // 2, sum_parts + (when - 9) // 2)
+            begins = jnp.where(when % 2 == 0, when, jnp.where(when >= 9, when - 9, -1))
+
+            @pl.when((begins >= 0) & (begins < 2 * sum_parts))
             def _(q=q, t=t):
                 if t < count:
                     sum_step(t, q)
@@ -1222,14 +1169,14 @@
         return carry
 
     lax.fori_loop(chunks - DEEP, chunks, drain, 0)
-    for q in range(2):
-        sums_copy(2 * sum_parts - 2 + q).wait()
+    for kind in range(1, 3):
+        sums_copy(kind * sum_parts - 1).wait()
     for way in range(2):
         for t in range(1, count):
             @pl.when(sum_sends(way, t))
             def _(way=way, t=t):
-                for q in range(2):
-                    sum_copy(way, t, 2 * sum_parts - 2 + q).wait_send()
+                for kind in range(1, 3):
+                    sum_copy(way, t, kind * sum_parts - 1).wait_send()
 
 
 def backward(
@@ -1331,7 +1278,7 @@
     own = own - jnp.mean(own, axis=1, keepdims=True)
     inv_std = lax.rsqrt(jnp.mean(own * own, axis=1, keepdims=True) + EPS)
     own = own * inv_std
-    scaled = sums[1] * gain[...]
+    scaled = sums[1] * gain[0:1, :]
     scaled = scaled - jnp.mean(scaled, axis=1, keepdims=True) - own * jnp.mean(scaled * own, axis=1, keepdims=True)
     grad[...] = cot[...].astype(F32) + inv_std * scaled
 
@@ -1395,7 +1342,7 @@
             pl.BlockSpec((2, part, width), lambda i: (0, i, 0)),
             by_rows(tokens.shape),
             by_rows(tokens.shape),
-            pl.BlockSpec((1, width), lambda i: (0, 0)),
+            pl.BlockSpec(gain.shape, lambda i: (0, 0)),
         ],
         out_specs=[by_rows(tokens.shape)] * 2
         + [by_rows(qkv), by_rows(gate), by_rows(gate), by_cols(down), by_cols(attn)]
@@ -1568,18 +1515,14 @@
     spots = jnp.arange(count, dtype=jnp.int32)
     slots = jnp.sum(jnp.where(order[None, :] == spots[:, None], spots[None, :], 0), axis=1)
     vectors = jnp.stack([ln_gain, ln_bias] + [jnp.zeros_like(ln_gain)] * 6).astype(F32)
-    x_all, vectors, w_inner, heads_own, w_attn = start(
-        block, vectors, w_gate, w_up, w_qkv, w_out, count, shards
+    tables = fixed_tables(rows * count)
+    (
+        cot_all, scales, w_inner, w_heads, w_attn, w_hidden, normed_t, hat, both, hidden_t,
+        q, k, v, attended, low_t, lse, branch,
+    ) = forward(
+        order, slots, tables, block, grad_block, vectors, w_gate, w_up, w_qkv, w_out, w_down, count, shards
     )
     w_inner = w_inner.reshape(width, -1)
-    gain, bias = vectors[:, 0].reshape(1, width), vectors[:, 1].reshape(1, width)
-    tables = fixed_tables(rows * count)
-
-    (
-        cot_all, w_heads, w_hidden, normed_t, hat, both, hidden_t, q, k, v, attended, low_t, lse, branch,
-    ) = forward(
-        order, slots, x_all, gain, bias, tables, grad_block, w_down, w_attn, w_inner, heads_own, shards
-    )
     w_hidden, w_attn = w_hidden.reshape(-1, width), w_attn.reshape(-1, width)
     w_heads = w_heads.reshape(width, -1)
     pieces, sums = backward(
@@ -1587,7 +1530,7 @@
         w_heads, hat, (q, k, v, attended, lse), shards,
     )
     out, grad_in, d_qkv, d_gate, d_up, d_down, d_attn, small = assemble_outputs(
-        pieces, sums, block, grad_block, gain, w_qkv.shape, w_out.shape, w_gate.shape, w_down.shape
+        pieces, sums, block, grad_block, scales, w_qkv.shape, w_out.shape, w_gate.shape, w_down.shape
     )
     out, grad_in = out[None], grad_in[None]
     return out, grad_in, small[0], small[1], d_qkv, d_attn, d_gate, d_up, d_down

time: 480 us -> 471 us (0.981)
  Pallas kernels: 472 us -> 465 us
    pallas_call x1 -> x0, Pallas kernels: 79 us -> none  [start(): pl.pallas_call(start_kernel, out_shape=[jax.ShapeDtypeStruct((count, rows...]
    pallas_call x1, Pallas kernels: 81.9 us -> 157 us  [forward(): pl.pallas_call(forward_kernel, out_shape=out_shape, in_specs=[smem] * 2 +...]
where the time goes in v3:
time: 471 us; the launch traced here: 470 us
  Pallas kernels  465 us (99%)
    pallas_call x1, Pallas kernels, backward(): pl.pallas_call(backward_kernel, out_shape=[jax.ShapeDtypeStruct((count, c...  290 us
    pallas_call x1, Pallas kernels, forward(): pl.pallas_call(forward_kernel, out_shape=out_shape, in_specs=[smem] * 2 +...  157 us
    pallas_call x1, Pallas kernels, assemble_outputs(): pl.pallas_call(assemble_kernel, grid=(steps,), in_specs=[pl.BlockSpec((co...  18 us

profile of v3, /device:TPU:0, one launch (start us, length us, event | category | flops | bytes accessed | tf_op | source)
XLA Modules:
  0.0 470.5 jit_solution(8704754229153230144)
XLA Ops:
  0.6 1.3 select_reduce_fusion.slots
  1.9 0.1 pad.3.clone
  2.0 0.1 pad.2.clone
  2.1 0.7 stack.15
  2.7 0.7 stack.16
  3.4 0.7 maximum_convert_fusion.vectors
  4.1 157.5 %forward.1 = (bf16[4,256,2048]{2,1,0:T(8,128)(2,1)}, f32[8,2048]{1,0:T(8,128)}, bf16[8,256,2816]{2,1,0:T(8,128)(2,1)}, bf16[8,256,1536]{2,1,0:T(8,128)(2,1)}, bf...) custom-call(s32[4]{0:T(128)} %bitcast.20, ...), custom_call_target="tpu_custom_call" | custom-call | tf_op jit(solution)/shard_map/forward/pallas_call | solution.py:671
  161.5 289.6 %backward.1 = (bf16[4,25,256,256]{3,2,1,0:T(8,128)(2,1)}, f32[2,256,2048]{2,1,0:T(8,128)}) custom-call(s32[4]{0:T(128)} %bitcast.21, s32[4]{0:T(128)} %select_reduce_fusion.slots, bf16[1408,1024]{1,0:T(8,128)(2,1)} %get-tuple-element.36.hid_t, bf16[512,1024]{1,0:T(8,128)(2,1)} %get-tuple-element.37.att_t, f32[1024,128]{1,0:T(8,128)} %constant.4.clone.cos, ...), custom_call_target="tpu_custom_call" | custom-call | tf_op jit(solution)/shard_map/backward/pallas_call | solution.py:1195
  451.1 18.0 %assemble.1 = (bf16[256,2048]{1,0:T(8,128)(2,1)}, f32[256,2048]{1,0:T(8,128)}, f32[256,6144]{1,0:T(8,128)}, f32[256,5632]{1,0:T(8,128)}, f32[256,5632]{1,0:T(8,1...) custom-call(bf16[4,25,256,256]{3,2,1,0:T(8,128)(2,1)} %get-tuple-element.52.rows_in.cols_in, ...), custom_call_target="tpu_custom_call" | custom-call | tf_op jit(solution)/shard_map/assemble/pallas_call | solution.py:1336
  469.1 1.3 fusion
  (2 shorter events, 0.0 us)

commit v4 on v3

--- a/solution.py
+++ b/solution.py
@@ -353,10 +353,11 @@
         self.store.start()
 
 
-def greet(peers):
+def greet(peers, meanwhile):
     barrier = pltpu.get_barrier_semaphore()
     for peer in peers:
         pl.semaphore_signal(barrier, inc=1, device_id=peer, device_id_type=MESH)
+    meanwhile()
     pl.semaphore_wait(barrier, len(peers))
 
 
@@ -387,11 +388,15 @@
         Own(cot, hat_stage.at[0], cot_all.at[place], own_sem, 0),
         Own(my_down, hat_stage.at[1, : down.shape[1]], down.at[me], own_sem, 1),
     ]
-    for c in loads + [own.load for own in owns]:
-        c.start()
     qkv_load = pltpu.make_async_copy(w_qkv, raw.at[0], load_sem.at[5])
     peers = [(place, (me + s) % shards) for s in range(1, shards)]
-    greet(peers + [((place + 1) % count, me), ((place + count - 1) % count, me)])
+    peers += [((place + 1) % count, me), ((place + count - 1) % count, me)]
+
+    def meanwhile():
+        for c in loads + [own.load for own in owns]:
+            c.start()
+
+    greet(peers, meanwhile)
     x_line = Line(tokens, x_all, x_send, x_recv)
     line = Line(cot, cot_all, line_send, line_recv)
     plane = Plane(
@@ -809,12 +814,12 @@
             device_id_type=MESH,
         )
 
-    def line_copy(way, hop, k):
+    def line_copy(way, hop, k, size):
         ahead = 1 - 2 * way
         origin = place - (hop - 1) * ahead
-        target = pieces.at[origin, chunk_name(k)]
+        target = pieces.at[origin, chunk_name(k), :size]
         return pltpu.make_async_remote_copy(
-            src_ref=total.at[k % DEEP] if hop == 1 else target,
+            src_ref=total.at[k % DEEP, :size] if hop == 1 else target,
             dst_ref=target,
             send_sem=line_send.at[way, hop - 1, k % DEEP],
             recv_sem=line_recv.at[way, k, hop - 1],
@@ -822,6 +827,15 @@
             device_id_type=MESH,
         )
 
+    def on_line(way, hop, k, act):
+        @pl.when(k < early)
+        def _():
+            act(line_copy(way, hop, k, ff_part + attn_part))
+
+        @pl.when(k >= early)
+        def _():
+            act(line_copy(way, hop, k, total.shape[1]))
+
     def sends(way, hop):
         if way == 0:
             return (place >= hop - 1) & (place <= count - 2)
@@ -835,16 +849,16 @@
             if hop > 1:
                 @pl.when(lands(way, hop - 1))
                 def _(way=way):
-                    line_copy(way, hop - 1, k).wait_recv()
+                    on_line(way, hop - 1, k, lambda c: c.wait_recv())
 
             if hop < count:
                 @pl.when(sends(way, hop))
                 def _(way=way):
                     @pl.when(k >= DEEP)
                     def _():
-                        line_copy(way, hop, k - DEEP).wait_send()
-
-                    line_copy(way, hop, k).start()
+                        on_line(way, hop, k - DEEP, lambda c: c.wait_send())
+
+                    on_line(way, hop, k, lambda c: c.start())
 
     def own_copy(k):
         return pltpu.make_async_copy(total.at[k % DEEP], pieces.at[place, chunk_name(k)], own_sem.at[k % DEEP])
@@ -948,13 +962,16 @@
         c.start()
     peers = [(place, me + 1 - 2 * core)]
     peers += [(place, 2 * chip_away(chip, m) + core) for m in range(1, chips)]
-    greet(peers + [((place + 1) % count, me), ((place + count - 1) % count, me)])
-    cot_load.wait()
-    for p in range(count):
-        cot_own[p * rows : (p + 1) * rows, :] = terms[slots[p]]
-    loads[0].start()
-    loads[0].wait()
-
+    peers += [((place + 1) % count, me), ((place + count - 1) % count, me)]
+
+    def meanwhile():
+        cot_load.wait()
+        for p in range(count):
+            cot_own[p * rows : (p + 1) * rows, :] = terms[slots[p]]
+        loads[0].start()
+        loads[0].wait()
+
+    greet(peers, meanwhile)
     ff = down.shape[0]
     whole_tiles = ff // TILE
 
@@ -1052,7 +1069,7 @@
             for way in range(2):
                 @pl.when(sends(way, 1) & (k >= DEEP))
                 def _(way=way):
-                    line_copy(way, 1, k - DEEP).wait_send()
+                    on_line(way, 1, k - DEEP, lambda c: c.wait_send())
 
             @pl.when(k >= DEEP)
             def _():
@@ -1062,7 +1079,7 @@
             for way in range(2):
                 @pl.when(sends(way, 1))
                 def _(way=way):
-                    line_copy(way, 1, k).start()
+                    on_line(way, 1, k, lambda c: c.start())
 
             own_copy(k).start()
 
@@ -1165,7 +1182,7 @@
             for hop in range(1, count):
                 @pl.when(sends(way, hop))
                 def _(way=way, hop=hop):
-                    line_copy(way, hop, k).wait_send()
+                    line_copy(way, hop, k, total.shape[1]).wait_send()
         return carry
 
     lax.fori_loop(chunks - DEEP, chunks, drain, 0)
@@ -1264,7 +1281,7 @@
     return out
 
 
-def assemble_kernel(rows_in, cols_in, sums, tokens, cot, gain, out, grad, qkv_out, gate_out, up_out, down_out, attn_out, small_out):
+def assemble_kernel(rows_in, cols_in, sums, tokens, cot, gain, out, grad, qkv_out, gate_out, up_out, down_out, attn_out, gain_out, bias_out):
     count, chunks, rows, _ = rows_in.shape
     ff = gate_out.shape[1]
     width = qkv_out.shape[1]
@@ -1323,7 +1340,9 @@
             p, 0, ff_part : ff_part + attn_part, :
         ].astype(F32)
     small = [cols_in[p, 0, ff_part + attn_part :, :].astype(F32) for p in range(count)]
-    small_out[...] = functools.reduce(jnp.add, small)
+    small = functools.reduce(jnp.add, small)
+    gain_out[...] = small[0:1]
+    bias_out[...] = small[1:2]
 
 
 def assemble_outputs(pieces, sums, tokens, cot, gain, qkv, attn, gate, down):
@@ -1346,9 +1365,9 @@
         ],
         out_specs=[by_rows(tokens.shape)] * 2
         + [by_rows(qkv), by_rows(gate), by_rows(gate), by_cols(down), by_cols(attn)]
-        + [pl.BlockSpec((16, TILE), lambda i: (0, 0))],
+        + [pl.BlockSpec((1, TILE), lambda i: (0, 0))] * 2,
         out_shape=[jax.ShapeDtypeStruct(tokens.shape, BF), jax.ShapeDtypeStruct(tokens.shape, F32)]
-        + [jax.ShapeDtypeStruct(s, F32) for s in (qkv, gate, gate, down, attn, (16, TILE))],
+        + [jax.ShapeDtypeStruct(s, F32) for s in (qkv, gate, gate, down, attn, (1, TILE), (1, TILE))],
         compiler_params=pltpu.CompilerParams(vmem_limit_bytes=60 * 2**20),
         name="assemble",
     )(pieces, pieces, sums, tokens, cot, gain)
@@ -1529,11 +1548,11 @@
         order, slots, hidden_t, low_t, tables, cot_all, normed_t, w_hidden, w_attn, both, branch, w_inner,
         w_heads, hat, (q, k, v, attended, lse), shards,
     )
-    out, grad_in, d_qkv, d_gate, d_up, d_down, d_attn, small = assemble_outputs(
+    out, grad_in, d_qkv, d_gate, d_up, d_down, d_attn, d_gain, d_bias = assemble_outputs(
         pieces, sums, block, grad_block, scales, w_qkv.shape, w_out.shape, w_gate.shape, w_down.shape
     )
     out, grad_in = out[None], grad_in[None]
-    return out, grad_in, small[0], small[1], d_qkv, d_attn, d_gate, d_up, d_down
+    return out, grad_in, d_gain.reshape(-1), d_bias.reshape(-1), d_qkv, d_attn, d_gate, d_up, d_down
 
 
 def solution(mesh):

time: 471 us -> 467 us (level)
  no operation moved by 1% of the time
where the time goes in v4:
time: 467 us
  Pallas kernels  463 us (99%)
    pallas_call x1, Pallas kernels, backward(): pl.pallas_call(backward_kernel, out_shape=[jax.ShapeDtypeStruct((count, c...  287 us
    pallas_call x1, Pallas kernels, forward(): pl.pallas_call(forward_kernel, out_shape=out_shape, in_specs=[smem] * 2 +...  157 us
    pallas_call x1, Pallas kernels, assemble_outputs(): pl.pallas_call(assemble_kernel, grid=(steps,), in_specs=[pl.BlockSpec((co...  18 us

profile of v4, /device:TPU:0, one launch (start us, length us, event | category | flops | bytes accessed | tf_op | source)
XLA Modules:
  0.0 466.8 jit_solution(7015388213324064267)
XLA Ops:
  0.6 1.3 select_reduce_fusion.slots
  1.9 0.1 pad.3.clone
  2.0 0.1 pad.2.clone
  2.1 0.7 stack.15
  2.7 0.7 stack.16
  3.4 0.7 maximum_convert_fusion.vectors
  4.1 157.5 %forward.1 = (bf16[4,256,2048]{2,1,0:T(8,128)(2,1)}, f32[8,2048]{1,0:T(8,128)}, bf16[8,256,2816]{2,1,0:T(8,128)(2,1)}, bf16[8,256,1536]{2,1,0:T(8,128)(2,1)}, bf...) custom-call(s32[4]{0:T(128)} %bitcast.20, ...), custom_call_target="tpu_custom_call" | custom-call | tf_op jit(solution)/shard_map/forward/pallas_call | solution.py:676
  161.5 287.1 %backward.1 = (bf16[4,25,256,256]{3,2,1,0:T(8,128)(2,1)}, f32[2,256,2048]{2,1,0:T(8,128)}) custom-call(s32[4]{0:T(128)} %bitcast.21, s32[4]{0:T(128)} %select_reduce_fusion.slots, bf16[1408,1024]{1,0:T(8,128)(2,1)} %get-tuple-element.37.hid_t, bf16[512,1024]{1,0:T(8,128)(2,1)} %get-tuple-element.38.att_t, f32[1024,128]{1,0:T(8,128)} %constant.4.clone.cos, ...), custom_call_target="tpu_custom_call" | custom-call | tf_op jit(solution)/shard_map/backward/pallas_call | solution.py:1212
  448.6 18.0 %assemble.1 = (bf16[256,2048]{1,0:T(8,128)(2,1)}, f32[256,2048]{1,0:T(8,128)}, f32[256,6144]{1,0:T(8,128)}, f32[256,5632]{1,0:T(8,128)}, f32[256,5632]{1,0:T(8,1...) custom-call(bf16[4,25,256,256]{3,2,1,0:T(8,128)(2,1)} %get-tuple-element.53.rows_in.cols_i, ...), custom_call_target="tpu_custom_call" | custom-call | tf_op jit(solution)/shard_map/assemble/pallas_call | solution.py:1355
  (2 shorter events, 0.0 us)

commit v5 on v4

--- a/solution.py
+++ b/solution.py
@@ -268,15 +268,18 @@
 
     def pass_on(self, hop):
         for way in range(2):
-            if hop > 1:
-                @pl.when(self.lands(way, hop - 1))
-                def _(way=way):
+            @pl.when(self.sends(way, hop))
+            def _(way=way):
+                if hop > 1:
                     self.copy(way, hop - 1).wait_recv()
-
-            if hop < self.count:
-                @pl.when(self.sends(way, hop))
-                def _(way=way):
-                    self.copy(way, hop).start()
+                self.copy(way, hop).start()
+
+    def land(self):
+        for way in range(2):
+            @pl.when(self.place == (self.count - 1 if way == 0 else 0))
+            def _(way=way):
+                for hop in range(1, self.count):
+                    self.copy(way, hop).wait_recv()
 
     def finish(self):
         for way in range(2):
@@ -468,7 +471,7 @@
     for c in loads[3:] + vector_copies:
         c.wait()
     scales[...] = jnp.concatenate([vectors_all[s] for s in range(shards)], axis=1)
-    x_line.pass_on(4)
+    x_line.land()
     plane.begin(3)
     outs = [
         pltpu.make_async_copy(attn, attn_out, out_sem.at[0]),
@@ -507,6 +510,7 @@
 
     for own in owns:
         own.store.wait()
+    line.pass_on(2)
     lax.fori_loop(0, count, norm_step, 0)
     plane.finish(0)
     outs[2].start()
@@ -538,7 +542,7 @@
 
     tiles = inner.shape[2] // TILE
     lax.fori_loop(0, tiles, feed_step, 0)
-    line.pass_on(2)
+    line.pass_on(3)
     plane.relay(3)
     plane.last(2)
     plane.finish(2)
@@ -592,7 +596,6 @@
 
     lax.fori_loop(0, pairs - 1, head_step, 0)
     plane.last(3)
-    line.pass_on(3)
     lax.fori_loop(pairs - 1, pairs, head_step, 0)
     plane.finish(3)
     def tile_copies(i):
@@ -629,8 +632,7 @@
         return carry
 
     lax.fori_loop(0, steps, branch_step, 0)
-    for hop in range(4, count + 1):
-        line.pass_on(hop)
+    line.land()
     line.finish()
     x_line.finish()
     for c in outs:

time: 467 us -> 467 us (level)
  no operation moved by 1% of the time
where the time goes in v5:
time: 467 us
  Pallas kernels  463 us (99%)
    pallas_call x1, Pallas kernels, backward(): pl.pallas_call(backward_kernel, out_shape=[jax.ShapeDtypeStruct((count, c...  287 us
    pallas_call x1, Pallas kernels, forward(): pl.pallas_call(forward_kernel, out_shape=out_shape, in_specs=[smem] * 2 +...  157 us
    pallas_call x1, Pallas kernels, assemble_outputs(): pl.pallas_call(assemble_kernel, grid=(steps,), in_specs=[pl.BlockSpec((co...  18 us

profile of v5, /device:TPU:0, one launch (start us, length us, event | category | flops | bytes accessed | tf_op | source)
XLA Modules:
  0.0 466.8 jit_solution(2199109858711064592)
XLA Ops:
  0.6 1.3 select_reduce_fusion.slots
  1.9 0.1 pad.3.clone
  2.0 0.1 pad.2.clone
  2.1 0.7 stack.15
  2.7 0.7 stack.16
  3.4 0.7 maximum_convert_fusion.vectors
  4.1 157.5 %forward.1 = (bf16[4,256,2048]{2,1,0:T(8,128)(2,1)}, f32[8,2048]{1,0:T(8,128)}, bf16[8,256,2816]{2,1,0:T(8,128)(2,1)}, bf16[8,256,1536]{2,1,0:T(8,128)(2,1)}, bf...) custom-call(s32[4]{0:T(128)} %bitcast.20, ...), custom_call_target="tpu_custom_call" | custom-call | tf_op jit(solution)/shard_map/forward/pallas_call | solution.py:678
  161.5 287.1 %backward.1 = (bf16[4,25,256,256]{3,2,1,0:T(8,128)(2,1)}, f32[2,256,2048]{2,1,0:T(8,128)}) custom-call(s32[4]{0:T(128)} %bitcast.21, s32[4]{0:T(128)} %select_reduce_fusion.slots, bf16[1408,1024]{1,0:T(8,128)(2,1)} %get-tuple-element.37.hid_t, bf16[512,1024]{1,0:T(8,128)(2,1)} %get-tuple-element.38.att_t, f32[1024,128]{1,0:T(8,128)} %constant.4.clone.cos, ...), custom_call_target="tpu_custom_call" | custom-call | tf_op jit(solution)/shard_map/backward/pallas_call | solution.py:1214
  448.6 18.0 %assemble.1 = (bf16[256,2048]{1,0:T(8,128)(2,1)}, f32[256,2048]{1,0:T(8,128)}, f32[256,6144]{1,0:T(8,128)}, f32[256,5632]{1,0:T(8,128)}, f32[256,5632]{1,0:T(8,1...) custom-call(bf16[4,25,256,256]{3,2,1,0:T(8,128)(2,1)} %get-tuple-element.53.rows_in.cols_i, ...), custom_call_target="tpu_custom_call" | custom-call | tf_op jit(solution)/shard_map/assemble/pallas_call | solution.py:1357
  (2 shorter events, 0.0 us)
